TPU v7x, 32 devices: a whole 2x2x4 slice. The times are simulated.
32 devices in a mesh: dp: 16 (over z, x, core), tensor: 2 (over y).
Axes of the slice: x: 2, y: 2, z: 4, core: 2. Of those that a mesh axis runs over, the one named last changes fastest.
Arguments:
- layer_input: bfloat16 [32768, 512], P(('dp', 'tensor')), may hold values from -6 to 6
- gene_known: int32 [32768], P('dp'), may hold values 0 or 1
- cell_genes: int32 [16, 4], P('dp'), may hold values from 0 to 2048, as said below
- w_qkv: bfloat16 [512, 3, 512], P(None, None, 'tensor'), may hold values from -0.25 to 0.25
- bias_qv: bfloat16 [2, 512], P(None, 'tensor'), may hold values from -3 to 3
- w_out: bfloat16 [512, 512], P('tensor'), may hold values from -4 to 4
- b_out: float32 [512], replicated, may hold values from -3 to 3
- ln1_gain: float32 [512], replicated, may hold values from 0.1 to 1.9
- ln1_bias: float32 [512], replicated, may hold values from -2 to 2
- w_up: bfloat16 [512, 512], P(None, 'tensor'), may hold values from -0.25 to 0.25
- b_up: bfloat16 [512], P('tensor'), may hold values from -3 to 3
- w_down: bfloat16 [512, 512], P('tensor'), may hold values from -0.25 to 0.25
- b_down: float32 [512], replicated, may hold values from -3 to 3
- ln2_gain: float32 [512], replicated, may hold values from 0.1 to 1.9
- ln2_bias: float32 [512], replicated, may hold values from -2 to 2
- cotangent: bfloat16 [32768, 512], P(('dp', 'tensor')), may hold values from -6 to 6
Outputs:
- activations: bfloat16 [32768, 512], P(('dp', 'tensor'))
- input_grad: float32 [32768, 512], P(('dp', 'tensor'))
- w_qkv_grad: float32 [512, 3, 512], P(None, None, 'tensor')
- bias_qv_grad: float32 [2, 512], P(None, 'tensor')
- w_out_grad: float32 [512, 512], P('tensor')
- b_out_grad: float32 [512], replicated
- ln1_gain_grad: float32 [512], replicated
- ln1_bias_grad: float32 [512], replicated
- w_up_grad: float32 [512, 512], P(None, 'tensor')
- b_up_grad: float32 [512], P('tensor')
- w_down_grad: float32 [512, 512], P('tensor')
- b_down_grad: float32 [512], replicated
- ln2_gain_grad: float32 [512], replicated
- ln2_bias_grad: float32 [512], replicated
Inputs may be any that keep to these rules, and one draw needn't show every extreme that they name: `cell_genes`: each row sums to 2048; a row is either 2048 followed by 4 - 1 zeros, or 4 positive lengths; at least one group holds a single cell.
All inputs are finite; a program needn't handle non-finite values. No bound on the sum of `gene_known` on one device may be relied on, other than what follows from the above.
Results may differ from a plain program's by a relative error of at most 0.019.
Values may be sent and summed in bfloat16 or wider, within the bound.
No kernel may reach another device: no remote copies, remote signals or barrier semaphores. Data moves between devices by JAX's collectives and lax.ppermute only.
A program may use at most 128 MiB of HBM per device.

v0:
```python
import jax
import jax.numpy as jnp
from jax import lax
from jax.sharding import PartitionSpec as P

HD = 64


NORM_EPS = 1e-05
MASKED = -1e30


def cell_layout(known_row, lengths):
    positions = jnp.arange(known_row.shape[0], dtype=jnp.int32)
    ends = jnp.cumsum(lengths)
    starts = ends - lengths
    cell_of = jnp.sum((positions[:, None] >= ends[None, :]).astype(jnp.int32), axis=1)
    opening = jnp.any((positions[:, None] == starts[None, :]) & (lengths[None, :] > 0), axis=1)
    key_live = (known_row > 0) | opening
    return (key_live, cell_of)


def layer_norm(values, gain_vec, shift_vec):
    average = jnp.mean(values, axis=-1, keepdims=True)
    centered = values - average
    variance = jnp.mean(centered * centered, axis=-1, keepdims=True)
    return centered * lax.rsqrt(variance + NORM_EPS) * gain_vec + shift_vec


def gelu_exact(values):
    return jax.nn.gelu(values, approximate=False)


def contract_dims(left, right, left_dim, right_dim):
    return lax.dot_general(
        left, right, (((left_dim,), (right_dim,)), ((), ())), preferred_element_type=jnp.float32
    )


def scores_of(query_block, cell_block, keys_all, cell_of, key_live):
    logits = jnp.einsum("qhd,khd->hqk", query_block, keys_all, preferred_element_type=jnp.float32)
    allowed = (cell_block[:, None] == cell_of[None, :]) & key_live[None, :]
    return jnp.where(allowed[None], logits * HD ** (-0.5), MASKED)


def attend_forward(queries, query_cells, keys_all, values_all, cell_of, key_live):

    def attend_block(inputs_pair):
        query_block, cell_block = inputs_pair
        scores = scores_of(query_block, cell_block, keys_all, cell_of, key_live)
        peak = jnp.max(scores, axis=-1, keepdims=True)
        expo = jnp.exp(scores - peak)
        summed = jnp.sum(expo, axis=-1, keepdims=True)
        probs = expo / summed
        mixed = jnp.einsum(
            "hqk,khd->qhd",
            probs.astype(jnp.bfloat16),
            values_all,
            preferred_element_type=jnp.float32,
        )
        return (mixed.astype(jnp.bfloat16), (peak + jnp.log(summed))[..., 0])

    return lax.map(attend_block, (queries, query_cells))


def attend_backward(
    queries, query_cells, grad_blocks, log_norm, keys_all, values_all, cell_of, key_live
):

    def back_block(running, inputs_four):
        query_block, cell_block, grad_block, norm_block = inputs_four
        scores = scores_of(query_block, cell_block, keys_all, cell_of, key_live)
        probs = jnp.exp(scores - norm_block[..., None])
        prob_grad = jnp.einsum(
            "qhd,khd->hqk", grad_block, values_all, preferred_element_type=jnp.float32
        )
        inner = jnp.sum(probs * prob_grad, axis=-1, keepdims=True)
        logit_grad = (probs * (prob_grad - inner) * HD ** (-0.5)).astype(jnp.bfloat16)
        query_grad = jnp.einsum(
            "hqk,khd->qhd", logit_grad, keys_all, preferred_element_type=jnp.float32
        )
        key_grad = running[0] + jnp.einsum(
            "hqk,qhd->khd", logit_grad, query_block, preferred_element_type=jnp.float32
        )
        value_grad = running[1] + jnp.einsum(
            "hqk,qhd->khd",
            probs.astype(jnp.bfloat16),
            grad_block,
            preferred_element_type=jnp.float32,
        )
        return ((key_grad, value_grad), query_grad)

    zeros_kv = jnp.zeros(keys_all.shape, jnp.float32)
    return lax.scan(back_block, (zeros_kv, zeros_kv), (queries, query_cells, grad_blocks, log_norm))


def local(
    layer_input,
    gene_known,
    cell_genes,
    w_qkv,
    bias_qv,
    w_out,
    b_out,
    ln1_gain,
    ln1_bias,
    w_up,
    b_up,
    w_down,
    b_down,
    ln2_gain,
    ln2_bias,
    cotangent,
):
    group_rows = gene_known.shape[0]
    width = layer_input.shape[1]
    local_width = w_qkv.shape[2]
    key_live, cell_of = cell_layout(gene_known, cell_genes[0])
    gathered = lax.all_gather(layer_input, "tensor", axis=0, tiled=True)
    local_heads = local_width // HD
    block_rows = min(512, group_rows)
    blocks = group_rows // block_rows
    flat_qkv = w_qkv.reshape(width, 3 * local_width)
    bias_flat = jnp.concatenate(
        [bias_qv[0], jnp.zeros((local_width,), jnp.bfloat16), bias_qv[1]]
    ).astype(jnp.float32)
    projected = (
        jnp.dot(gathered, flat_qkv, preferred_element_type=jnp.float32) + bias_flat
    ).astype(jnp.bfloat16)
    queries = projected[:, :local_width].reshape(blocks, block_rows, local_heads, HD)
    keys_all = projected[:, local_width : 2 * local_width].reshape(group_rows, local_heads, HD)
    values_all = projected[:, 2 * local_width :].reshape(group_rows, local_heads, HD)
    query_cells = cell_of.reshape(blocks, block_rows)
    attended_blocks, log_norm = attend_forward(
        queries, query_cells, keys_all, values_all, cell_of, key_live
    )
    attended = attended_blocks.reshape(group_rows, local_width)
    attn_branch = lax.psum_scatter(
        jnp.dot(attended, w_out, preferred_element_type=jnp.float32).astype(jnp.bfloat16),
        "tensor",
        scatter_dimension=0,
        tiled=True,
    ).astype(jnp.float32)
    residual_one = layer_input.astype(jnp.float32) + attn_branch + b_out
    first_norm, first_back = jax.vjp(layer_norm, residual_one, ln1_gain, ln1_bias)
    first_low = first_norm.astype(jnp.bfloat16)
    norm_all = lax.all_gather(first_low, "tensor", axis=0, tiled=True)
    hidden_pre = jnp.dot(norm_all, w_up, preferred_element_type=jnp.float32) + b_up.astype(
        jnp.float32
    )
    hidden_act, gelu_back = jax.vjp(gelu_exact, hidden_pre)
    hidden_low = hidden_act.astype(jnp.bfloat16)
    ffn_branch = lax.psum_scatter(
        jnp.dot(hidden_low, w_down, preferred_element_type=jnp.float32).astype(jnp.bfloat16),
        "tensor",
        scatter_dimension=0,
        tiled=True,
    ).astype(jnp.float32)
    residual_two = first_norm + ffn_branch + b_down
    final_norm, second_back = jax.vjp(layer_norm, residual_two, ln2_gain, ln2_bias)
    activations = final_norm.astype(jnp.bfloat16)
    grad_two, gain_two_grad, shift_two_grad = second_back(cotangent.astype(jnp.float32))
    down_bias_grad = jnp.sum(grad_two, axis=0)
    grad_two_low = grad_two.astype(jnp.bfloat16)
    grad_all = lax.all_gather(grad_two_low, "tensor", axis=0, tiled=True)
    down_grad = contract_dims(hidden_low, grad_all, 0, 0)
    hidden_grad = contract_dims(grad_all, w_down, 1, 1)
    pre_grad = gelu_back(hidden_grad)[0].astype(jnp.bfloat16)
    up_grad = contract_dims(norm_all, pre_grad, 0, 0)
    up_bias_grad = jnp.sum(pre_grad, axis=0, dtype=jnp.float32)
    grad_one = grad_two + lax.psum_scatter(
        contract_dims(pre_grad, w_up, 1, 1).astype(jnp.bfloat16),
        "tensor",
        scatter_dimension=0,
        tiled=True,
    ).astype(jnp.float32)
    residual_grad, gain_one_grad, shift_one_grad = first_back(grad_one)
    out_bias_grad = jnp.sum(residual_grad, axis=0)
    residual_low = residual_grad.astype(jnp.bfloat16)
    attn_grad_all = lax.all_gather(residual_low, "tensor", axis=0, tiled=True)
    out_grad = contract_dims(attended, attn_grad_all, 0, 0)
    attended_grad = contract_dims(attn_grad_all, w_out, 1, 1).astype(jnp.bfloat16)
    grad_blocks = attended_grad.reshape(blocks, block_rows, local_heads, HD)
    (key_grad, value_grad), query_grad = attend_backward(
        queries, query_cells, grad_blocks, log_norm, keys_all, values_all, cell_of, key_live
    )
    qkv_grad = jnp.concatenate(
        [
            query_grad.reshape(group_rows, local_width),
            key_grad.reshape(group_rows, local_width),
            value_grad.reshape(group_rows, local_width),
        ],
        axis=1,
    ).astype(jnp.bfloat16)
    bias_grad = jnp.stack(
        [
            jnp.sum(qkv_grad[:, :local_width], axis=0, dtype=jnp.float32),
            jnp.sum(qkv_grad[:, 2 * local_width :], axis=0, dtype=jnp.float32),
        ]
    )
    qkv_weight_grad = contract_dims(gathered, qkv_grad, 0, 0).reshape(width, 3, local_width)
    input_grad = residual_grad + lax.psum_scatter(
        contract_dims(qkv_grad, flat_qkv, 1, 1).astype(jnp.bfloat16),
        "tensor",
        scatter_dimension=0,
        tiled=True,
    ).astype(jnp.float32)
    qkv_weight_grad, bias_grad, out_grad, up_grad, up_bias_grad, down_grad = lax.psum(
        (qkv_weight_grad, bias_grad, out_grad, up_grad, up_bias_grad, down_grad), "dp"
    )
    small_grads = lax.psum(
        (
            out_bias_grad,
            gain_one_grad,
            shift_one_grad,
            down_bias_grad,
            gain_two_grad,
            shift_two_grad,
        ),
        ("dp", "tensor"),
    )
    return (
        activations,
        input_grad,
        qkv_weight_grad,
        bias_grad,
        out_grad,
        small_grads[0],
        small_grads[1],
        small_grads[2],
        up_grad,
        up_bias_grad,
        down_grad,
        small_grads[3],
        small_grads[4],
        small_grads[5],
    )


def solution(mesh):
    placed = (
        P(("dp", "tensor"), None),
        P("dp"),
        P("dp", None),
        P(None, None, "tensor"),
        P(None, "tensor"),
        P("tensor", None),
        P(),
        P(),
        P(),
        P(None, "tensor"),
        P("tensor"),
        P("tensor", None),
        P(),
        P(),
        P(),
        P(("dp", "tensor"), None),
    )
    return jax.shard_map(
        local,
        mesh=mesh,
        in_specs=placed,
        out_specs=(
            P(("dp", "tensor"), None),
            P(("dp", "tensor"), None),
            P(None, None, "tensor"),
            P(None, "tensor"),
            P("tensor", None),
            P(),
            P(),
            P(),
            P(None, "tensor"),
            P("tensor"),
            P("tensor", None),
            P(),
            P(),
            P(),
        ),
        check_vma=False,
    )
```

profile of v0, /device:TPU:0, one launch (start us, length us, event | category | flops | bytes accessed | tf_op | source)
XLA Modules:
  0.0 816.5 jit_solution(5096313961852948735)
XLA Ops:
  10.6 34.8 %all-gather.5.cloned.1.call-done = bf16[2048,512]{1,0:T(8,128)(2,1)} async-done(((bf16[1024,512]{1,0:T(8,128)(2,1)}), bf16[2048,512]{1,0:T(8,128)(2,1)}) %all-gather.5.cloned.1.call-update) | async-done | bytes 2097168 | tf_op jit(solution)/shard_map/all_gather | solution.py:119
  45.5 3.4 add_convert_fusion
  52.1 57.2 %while.27 = (s32[]{:T(128)}, bf16[4,512,4,64]{1,3,2,0:T(8,128)(2,1)}, f32[4,4,512]{2,1,0:T(4,128)S(1)}, s32[4,512]{1,0:T(4,128)S(1)}, s32[2048]{0:T(1024)S(1)}, ...) while((s32[]{:T(128)}, ...), condition=%wide.region_6.7_spmd, body=%wide.region_3.6_spmd.sunk | while | flops 1126299648 | bytes 57229436 | solution.py:63
  52.9 3.2 fusion.165
  56.1 4.3 fusion.166
  60.5 5.9 fusion.167
  67.2 3.2 fusion.165
  70.4 4.3 fusion.166
  74.8 5.9 fusion.167
  84.7 4.3 fusion.166
  89.0 5.9 fusion.167
  99.0 4.3 fusion.166
  103.3 5.9 fusion.167
  115.9 31.6 %reduce-scatter.5.cloned.1.call-done = bf16[1024,512]{1,0:T(8,128)(2,1)} async-done(((bf16[2048,512]{1,0:T(8,128)(2,1)}), bf16[1024,512]{1,0:T(8,128)(2,1)}) %reduce-scatter.5.cloned.1.call-update) | async-done | bytes 1048592 | tf_op jit(solution)/shard_map/reduce_scatter | solution.py:138
  151.6 33.2 %all-gather.7.cloned.1.call-done = bf16[2048,512]{1,0:T(8,128)(2,1)} async-done(((bf16[1024,512]{1,0:T(8,128)(2,1)}), bf16[2048,512]{1,0:T(8,128)(2,1)}) %all-gather.7.cloned.1.call-update) | async-done | bytes 2097168 | tf_op jit(solution)/shard_map/all_gather | solution.py:147
  184.8 7.9 multiply_convert_fusion.1
  195.8 31.9 %reduce-scatter.7.cloned.1.call-done = bf16[1024,512]{1,0:T(8,128)(2,1)} async-done(((bf16[2048,512]{1,0:T(8,128)(2,1)}), bf16[1024,512]{1,0:T(8,128)(2,1)}) %reduce-scatter.7.cloned.1.call-update) | async-done | bytes 1048592 | tf_op jit(solution)/shard_map/reduce_scatter | solution.py:153
  237.3 33.2 %all-gather.9.cloned.1.call-done = bf16[2048,512]{1,0:T(8,128)(2,1)} async-done(((bf16[1024,512]{1,0:T(8,128)(2,1)}), bf16[2048,512]{1,0:T(8,128)(2,1)}) %all-gather.9.cloned.1.call-update) | async-done | bytes 2097168 | tf_op jit(solution)/shard_map/all_gather | solution.py:165
  270.5 4.7 convert_reduce_fusion.1
  278.3 31.9 %reduce-scatter.9.cloned.1.call-done = bf16[1024,512]{1,0:T(8,128)(2,1)} async-done(((bf16[2048,512]{1,0:T(8,128)(2,1)}), bf16[1024,512]{1,0:T(8,128)(2,1)}) %reduce-scatter.9.cloned.1.call-update) | async-done | bytes 1048592 | tf_op jit(solution)/shard_map/reduce_scatter | solution.py:171
  310.3 3.7 multiply_reduce_fusion.1
  318.7 33.2 %all-gather.11.cloned.1.call-done = bf16[2048,512]{1,0:T(8,128)(2,1)} async-done(((bf16[1024,512]{1,0:T(8,128)(2,1)}), bf16[2048,512]{1,0:T(8,128)(2,1)}) %all-gather.11.cloned.1.call-update) | async-done | bytes 2097168 | tf_op jit(solution)/shard_map/all_gather | solution.py:180
  356.1 4.1 copy.47
  360.3 294.4 %while.28 = (s32[]{:T(128)}, f32[2048,4,64]{0,2,1:T(8,128)}, f32[2048,4,64]{0,2,1:T(8,128)}, bf16[4,512,4,64]{1,3,2,0:T(8,128)(2,1)}, bf16[4,512,4,64]{1,3,2,0:T...) while((s32[]{:T(128)}, f32[2048,4,64]{0,2,1:T(8,128)}, ...), condition=%wide.region_20.21_spmd.clone, body=%wide.region_18.20_spmd.clone.sunk | while | flops 2797608960 | bytes 271130816 | solution.py:94
  370.4 3.3 fusion.179
  373.7 7.3 fusion.181
  381.0 9.0 %fusion.178 = f32[4,512,2048]{2,1,0:T(8,128)} fusion(bf16[2048,4,64]{0,2,1:T(8,128)(2,1)S(1)} %get-tuple-element.518, bf16[4,512,4,64]{1,3,2,0:T(8,128)(2,1)} %get-tuple-element.517, s32[]{:T(128)S(6)} %copy.70), kind=kOutput, calls=%fused_computation.44.clone.1 | convolution fusion | flops 536870912 | bytes 18087940 | tf_op jit(solution)/shard_map/while/body/eval_jaxpr/qhd,khd->hqk/dot_general | solution.py:74
  390.1 24.0 %fusion.182 = bf16[4,512,4,64]{1,3,2,0:T(8,128)(2,1)} fusion(bf16[4,512,4,64]{1,3,2,0:T(8,128)(2,1)} %get-tuple-element.496, s32[]{:T(128)S(6)} %copy.70, bf16[2048,4,64]{0,2,1:T(8,128)(2,1)S(1)} %get-tuple-element.515, f32[4,512,2048]{2,1,0:T(8,128)} %fusion.178, f32[4,512,2048]{2,1,0:T(8,128)} %copy-done.2, ...), kind=kOutput, calls=%fused_computation.42.clone.1 | convolution fusion | flops 583012352 | bytes 70795264 | tf_op jit(solution)/shard_map/while/body/eval_jaxpr/hqk,khd->qhd/dot_general | solution.py:79
  414.0 25.5 %fusion.180 = f32[2048,4,64]{0,2,1:T(8,128)} fusion(f32[4,512,2048]{2,1,0:T(8,128)} %fusion.178, f32[4,512,2048]{2,1,0:T(8,128)} %copy-done.2, f32[4,512]{1,0:T(4,128)S(1)} %dynamic-slice_bitcast_fusion.2, pred[512,2048]{1,0:T(8,128)(4,1)S(1)} %compare_and_fusion.5, f32[2048,4,64]{0,2,1:T(8,128)} %get-tuple-element.494, pred[]{:T(512)S(6)} %compare.3, ...), kind=kOutput, calls=%fused_computation.40.clone.1 | convolution fusion | flops 584060928 | bytes 73678856 | tf_op jit(solution)/shard_map/while/body/eval_jaxpr/hqk,qhd->khd/dot_general | solution.py:82
  440.3 3.3 fusion.179
  443.6 8.5 %fusion.181 = f32[2048,4,64]{0,2,1:T(8,128)} fusion(f32[4,512,2048]{2,1,0:T(8,128)S(1)} %fusion.179, f32[4,512]{1,0:T(4,128)S(1)} %dynamic-slice_bitcast_fusion.2, pred[512,2048]{1,0:T(8,128)(4,1)S(1)} %compare_and_fusion.5, f32[2048,4,64]{0,2,1:T(8,128)} %get-tuple-element.495, pred[]{:T(512)S(6)} %compare.3, ...), kind=kOutput, calls=%fused_computation.39.clone.1 | convolution fusion | flops 554696704 | bytes 22290436 | tf_op jit(solution)/shard_map/while/body/eval_jaxpr/hqk,qhd->khd/dot_general | solution.py:85
  452.1 9.0 %fusion.178 = f32[4,512,2048]{2,1,0:T(8,128)} fusion(bf16[2048,4,64]{0,2,1:T(8,128)(2,1)S(1)} %get-tuple-element.518, bf16[4,512,4,64]{1,3,2,0:T(8,128)(2,1)} %get-tuple-element.517, s32[]{:T(128)S(6)} %copy.70), kind=kOutput, calls=%fused_computation.44.clone.1 | convolution fusion | flops 536870912 | bytes 18087940 | tf_op jit(solution)/shard_map/while/body/eval_jaxpr/qhd,khd->hqk/dot_general | solution.py:74
  461.1 24.0 %fusion.182 = bf16[4,512,4,64]{1,3,2,0:T(8,128)(2,1)} fusion(bf16[4,512,4,64]{1,3,2,0:T(8,128)(2,1)} %get-tuple-element.496, s32[]{:T(128)S(6)} %copy.70, bf16[2048,4,64]{0,2,1:T(8,128)(2,1)S(1)} %get-tuple-element.515, f32[4,512,2048]{2,1,0:T(8,128)} %fusion.178, f32[4,512,2048]{2,1,0:T(8,128)} %copy-done.2, ...), kind=kOutput, calls=%fused_computation.42.clone.1 | convolution fusion | flops 583012352 | bytes 70795264 | tf_op jit(solution)/shard_map/while/body/eval_jaxpr/hqk,khd->qhd/dot_general | solution.py:79
  485.1 26.1 %fusion.180 = f32[2048,4,64]{0,2,1:T(8,128)} fusion(f32[4,512,2048]{2,1,0:T(8,128)} %fusion.178, f32[4,512,2048]{2,1,0:T(8,128)} %copy-done.2, f32[4,512]{1,0:T(4,128)S(1)} %dynamic-slice_bitcast_fusion.2, pred[512,2048]{1,0:T(8,128)(4,1)S(1)} %compare_and_fusion.5, f32[2048,4,64]{0,2,1:T(8,128)} %get-tuple-element.494, pred[]{:T(512)S(6)} %compare.3, ...), kind=kOutput, calls=%fused_computation.40.clone.1 | convolution fusion | flops 584060928 | bytes 73678856 | tf_op jit(solution)/shard_map/while/body/eval_jaxpr/hqk,qhd->khd/dot_general | solution.py:82
  511.9 3.3 fusion.179
  515.3 8.5 %fusion.181 = f32[2048,4,64]{0,2,1:T(8,128)} fusion(f32[4,512,2048]{2,1,0:T(8,128)S(1)} %fusion.179, f32[4,512]{1,0:T(4,128)S(1)} %dynamic-slice_bitcast_fusion.2, pred[512,2048]{1,0:T(8,128)(4,1)S(1)} %compare_and_fusion.5, f32[2048,4,64]{0,2,1:T(8,128)} %get-tuple-element.495, pred[]{:T(512)S(6)} %compare.3, ...), kind=kOutput, calls=%fused_computation.39.clone.1 | convolution fusion | flops 554696704 | bytes 22290436 | tf_op jit(solution)/shard_map/while/body/eval_jaxpr/hqk,qhd->khd/dot_general | solution.py:85
  523.7 9.0 %fusion.178 = f32[4,512,2048]{2,1,0:T(8,128)} fusion(bf16[2048,4,64]{0,2,1:T(8,128)(2,1)S(1)} %get-tuple-element.518, bf16[4,512,4,64]{1,3,2,0:T(8,128)(2,1)} %get-tuple-element.517, s32[]{:T(128)S(6)} %copy.70), kind=kOutput, calls=%fused_computation.44.clone.1 | convolution fusion | flops 536870912 | bytes 18087940 | tf_op jit(solution)/shard_map/while/body/eval_jaxpr/qhd,khd->hqk/dot_general | solution.py:74
  532.8 24.0 %fusion.182 = bf16[4,512,4,64]{1,3,2,0:T(8,128)(2,1)} fusion(bf16[4,512,4,64]{1,3,2,0:T(8,128)(2,1)} %get-tuple-element.496, s32[]{:T(128)S(6)} %copy.70, bf16[2048,4,64]{0,2,1:T(8,128)(2,1)S(1)} %get-tuple-element.515, f32[4,512,2048]{2,1,0:T(8,128)} %fusion.178, f32[4,512,2048]{2,1,0:T(8,128)} %copy-done.2, ...), kind=kOutput, calls=%fused_computation.42.clone.1 | convolution fusion | flops 583012352 | bytes 70795264 | tf_op jit(solution)/shard_map/while/body/eval_jaxpr/hqk,khd->qhd/dot_general | solution.py:79
  556.7 26.1 %fusion.180 = f32[2048,4,64]{0,2,1:T(8,128)} fusion(f32[4,512,2048]{2,1,0:T(8,128)} %fusion.178, f32[4,512,2048]{2,1,0:T(8,128)} %copy-done.2, f32[4,512]{1,0:T(4,128)S(1)} %dynamic-slice_bitcast_fusion.2, pred[512,2048]{1,0:T(8,128)(4,1)S(1)} %compare_and_fusion.5, f32[2048,4,64]{0,2,1:T(8,128)} %get-tuple-element.494, pred[]{:T(512)S(6)} %compare.3, ...), kind=kOutput, calls=%fused_computation.40.clone.1 | convolution fusion | flops 584060928 | bytes 73678856 | tf_op jit(solution)/shard_map/while/body/eval_jaxpr/hqk,qhd->khd/dot_general | solution.py:82
  583.6 3.3 fusion.179
  586.9 8.5 %fusion.181 = f32[2048,4,64]{0,2,1:T(8,128)} fusion(f32[4,512,2048]{2,1,0:T(8,128)S(1)} %fusion.179, f32[4,512]{1,0:T(4,128)S(1)} %dynamic-slice_bitcast_fusion.2, pred[512,2048]{1,0:T(8,128)(4,1)S(1)} %compare_and_fusion.5, f32[2048,4,64]{0,2,1:T(8,128)} %get-tuple-element.495, pred[]{:T(512)S(6)} %compare.3, ...), kind=kOutput, calls=%fused_computation.39.clone.1 | convolution fusion | flops 554696704 | bytes 22290436 | tf_op jit(solution)/shard_map/while/body/eval_jaxpr/hqk,qhd->khd/dot_general | solution.py:85
  595.4 9.0 %fusion.178 = f32[4,512,2048]{2,1,0:T(8,128)} fusion(bf16[2048,4,64]{0,2,1:T(8,128)(2,1)S(1)} %get-tuple-element.518, bf16[4,512,4,64]{1,3,2,0:T(8,128)(2,1)} %get-tuple-element.517, s32[]{:T(128)S(6)} %copy.70), kind=kOutput, calls=%fused_computation.44.clone.1 | convolution fusion | flops 536870912 | bytes 18087940 | tf_op jit(solution)/shard_map/while/body/eval_jaxpr/qhd,khd->hqk/dot_general | solution.py:74
  604.4 24.0 %fusion.182 = bf16[4,512,4,64]{1,3,2,0:T(8,128)(2,1)} fusion(bf16[4,512,4,64]{1,3,2,0:T(8,128)(2,1)} %get-tuple-element.496, s32[]{:T(128)S(6)} %copy.70, bf16[2048,4,64]{0,2,1:T(8,128)(2,1)S(1)} %get-tuple-element.515, f32[4,512,2048]{2,1,0:T(8,128)} %fusion.178, f32[4,512,2048]{2,1,0:T(8,128)} %copy-done.2, ...), kind=kOutput, calls=%fused_computation.42.clone.1 | convolution fusion | flops 583012352 | bytes 70795264 | tf_op jit(solution)/shard_map/while/body/eval_jaxpr/hqk,khd->qhd/dot_general | solution.py:79
  628.4 26.1 %fusion.180 = f32[2048,4,64]{0,2,1:T(8,128)} fusion(f32[4,512,2048]{2,1,0:T(8,128)} %fusion.178, f32[4,512,2048]{2,1,0:T(8,128)} %copy-done.2, f32[4,512]{1,0:T(4,128)S(1)} %dynamic-slice_bitcast_fusion.2, pred[512,2048]{1,0:T(8,128)(4,1)S(1)} %compare_and_fusion.5, f32[2048,4,64]{0,2,1:T(8,128)} %get-tuple-element.494, pred[]{:T(512)S(6)} %compare.3, ...), kind=kOutput, calls=%fused_computation.40.clone.1 | convolution fusion | flops 584060928 | bytes 73678856 | tf_op jit(solution)/shard_map/while/body/eval_jaxpr/hqk,qhd->khd/dot_general | solution.py:82
  663.2 3.6 fusion.115
  678.8 39.8 %all-reduce = (f32[512]{0:T(512)}, f32[512]{0:T(512)}, f32[512]{0:T(512)}, f32[512]{0:T(512)}, f32[512]{0:T(512)}, /*index=5*/f32[512]{0:T(512)}) all-reduce(f32[512]{0:T(512)S(1)} %copy-done.44, f32[512]{0:T(512)S(1)} %copy-done.36, f32[512]{0:T(512)S(1)} %copy-done.37, ...), channel_id=1, replica_groups=mesh['dp'=16,'tensor'=2] {'dp','tensor'}, use_global_device_ids=true, to_apply=%region_28.29 | all-reduce | flops 3072 | bytes 24576 | tf_op jit(solution)/shard_map/psum | solution.py:211
  718.8 33.4 %all-reduce.1 = (f32[2,256]{1,0:T(2,128)}, f32[256]{0:T(256)}) all-reduce(f32[2,256]{1,0:T(2,128)S(1)} %pad_maximum_fusion.3, f32[256]{0:T(256)S(1)} %copy-done.48), channel_id=1, replica_groups=mesh['dp'=16,'tensor'=2] {'dp'}, use_global_device_ids=true, to_apply=%region_25.26 | all-reduce | flops 768 | bytes 6144 | tf_op jit(solution)/shard_map/psum | solution.py:208
  755.0 49.6 %all-reduce.5.cloned.1.call-done = (f32[512,3,256]{2,0,1:T(8,128)}, f32[256,512]{1,0:T(8,128)}, f32[512,256]{1,0:T(8,128)}, f32[256,512]{1,0:T(8,128)}) async-done(((f32[512,3,256]{2,0,1:T(8,128)}, f32[256,512]{1,0:T(8,128)}, f32[512,256]{1,0:T(8,128)}, f32[256,512]{1,0:T(8,128)}), (f32[512,3,256]{2,0,1:T(8,128)}, f32[256,512]{1,0:T(8,128)}, f32[512,256]{1,0:T(8,128)}, ...) | async-done | bytes 3145744 | tf_op jit(solution)/shard_map/psum | solution.py:208
  (216 shorter events, 82.7 us)
Async XLA Ops:
  7.2 177.6 %copy-start = (bf16[512,256]{1,0:T(8,128)(2,1)S(1)}, bf16[512,256]{1,0:T(8,128)(2,1)}, u32[]{:S(2)}) copy-start(bf16[512,256]{1,0:T(8,128)(2,1)} %param.29) | copy-start | bytes 786436
  7.2 3.3 copy-start.50
  7.2 3.2 copy-start.45
  7.2 3.4 copy-start.39
  7.2 38.2 %all-gather.5.cloned.1.call-start = ((), (), s32[]{:S(2)}) async-start(), calls=%async_computation.4 | async-start | bytes 3145728 | tf_op jit(solution)/shard_map/all_gather | solution.py:119
  8.0 139.5 %reduce-scatter.5.cloned.1.call-start = ((), (), s32[]{:S(2)}) async-start(), calls=%async_computation.5 | async-start | bytes 3145728 | tf_op jit(solution)/shard_map/reduce_scatter | solution.py:138
  10.4 35.1 %copy-start.26 = (bf16[512,3,256]{0,2,1:T(8,128)(2,1)}, bf16[512,3,256]{0,2,1:T(8,128)(2,1)S(1)}, u32[]{:S(2)}) copy-start(bf16[512,3,256]{0,2,1:T(8,128)(2,1)S(1)} %copy.42) | copy-start | bytes 2359300
  109.3 3.1 copy-start.5
  109.3 3.1 copy-start.11
  109.3 4.1 copy-start.24
  115.5 32.0 %copy-start.3 = (bf16[1024,512]{1,0:T(8,128)(2,1)S(1)}, bf16[1024,512]{1,0:T(8,128)(2,1)}, u32[]{:S(2)}) copy-start(bf16[1024,512]{1,0:T(8,128)(2,1)} %param.20) | copy-start | bytes 3145732
  115.5 32.0 %copy-start.32 = (f32[512]{0:T(512)S(1)}, f32[512]{0:T(512)}, u32[]{:S(2)}) copy-start(f32[512]{0:T(512)} %param.26) | copy-start | bytes 6148
  115.5 34.4 %copy-start.35 = (f32[512]{0:T(512)S(1)}, f32[512]{0:T(512)}, u32[]{:S(2)}) copy-start(f32[512]{0:T(512)} %param.27) | copy-start | bytes 6148
  115.5 34.4 %copy-start.40 = (f32[512]{0:T(512)S(1)}, f32[512]{0:T(512)}, u32[]{:S(2)}) copy-start(f32[512]{0:T(512)} %param.28) | copy-start | bytes 6148
  115.5 69.3 %all-gather.7.cloned.1.call-start = ((), (), s32[]{:S(2)}) async-start(), calls=%async_computation.6 | async-start | bytes 3145728 | tf_op jit(solution)/shard_map/all_gather | solution.py:147
  147.5 1.7 copy-start.4
  149.9 1.7 copy-start.51
  151.5 76.3 %reduce-scatter.7.cloned.1.call-start = ((), (), s32[]{:S(2)}) async-start(), calls=%async_computation.7 | async-start | bytes 3145728 | tf_op jit(solution)/shard_map/reduce_scatter | solution.py:153
  184.8 8.9 %copy-start.31 = (bf16[256,512]{1,0:T(8,128)(2,1)S(1)}, bf16[256,512]{1,0:T(8,128)(2,1)}, u32[]{:S(2)}) copy-start(bf16[256,512]{1,0:T(8,128)(2,1)} %param.31) | copy-start | bytes 786436
  193.7 34.1 %copy-start.46 = (f32[512]{0:T(512)S(1)}, f32[512]{0:T(512)}, u32[]{:S(2)}) copy-start(f32[512]{0:T(512)} %param.32) | copy-start | bytes 6148
  195.8 74.7 %all-gather.9.cloned.1.call-start = ((), (), s32[]{:S(2)}) async-start(), calls=%async_computation.8 | async-start | bytes 3145728 | tf_op jit(solution)/shard_map/all_gather | solution.py:165
  230.5 2.2 copy-start.47
  237.2 73.0 %reduce-scatter.9.cloned.1.call-start = ((), (), s32[]{:S(2)}) async-start(), calls=%async_computation.9 | async-start | bytes 3145728 | tf_op jit(solution)/shard_map/reduce_scatter | solution.py:171
  278.3 73.6 %all-gather.11.cloned.1.call-start = ((), (), s32[]{:S(2)}) async-start(), calls=%async_computation.10 | async-start | bytes 3145728 | tf_op jit(solution)/shard_map/all_gather | solution.py:180
  310.3 3.7 copy-start.8
  310.3 3.7 copy-start.16
  315.5 3.1 copy-start.33
  316.8 35.1 %copy-start.25 = (bf16[256,512]{1,0:T(8,128)(2,1)S(1)}, bf16[256,512]{1,0:T(8,128)(2,1)}, u32[]{:S(2)}) copy-start(bf16[256,512]{1,0:T(8,128)(2,1)} %param.25) | copy-start | bytes 786436
  318.7 433.5 %reduce-scatter.11.cloned.1.call-start = ((), (), s32[]{:S(2)}) async-start(), calls=%async_computation.11 | async-start | bytes 3145728 | tf_op jit(solution)/shard_map/reduce_scatter | solution.py:202
  356.1 4.1 copy-start.6
  373.7 7.3 copy-start.2
  443.6 8.5 %copy-start.2 = (f32[4,512,2048]{2,1,0:T(8,128)}, f32[4,512,2048]{2,1,0:T(8,128)S(1)}, u32[]{:S(2)}) copy-start(f32[4,512,2048]{2,1,0:T(8,128)S(1)} %fusion.179) | copy-start | bytes 50331652 | tf_op jit(solution)/shard_map/while
  515.3 8.5 %copy-start.2 = (f32[4,512,2048]{2,1,0:T(8,128)}, f32[4,512,2048]{2,1,0:T(8,128)S(1)}, u32[]{:S(2)}) copy-start(f32[4,512,2048]{2,1,0:T(8,128)S(1)} %fusion.179) | copy-start | bytes 50331652 | tf_op jit(solution)/shard_map/while
  586.9 8.5 %copy-start.2 = (f32[4,512,2048]{2,1,0:T(8,128)}, f32[4,512,2048]{2,1,0:T(8,128)S(1)}, u32[]{:S(2)}) copy-start(f32[4,512,2048]{2,1,0:T(8,128)S(1)} %fusion.179) | copy-start | bytes 50331652 | tf_op jit(solution)/shard_map/while
  654.7 2.5 copy-start.19
  657.3 2.6 copy-start.27
  663.1 3.7 copy-start.15
  663.1 141.5 %all-reduce.5.cloned.1.call-start = ((), (), s32[]{:S(2)}) async-start(), calls=%async_computation.12 | async-start | bytes 6291456 | tf_op jit(solution)/shard_map/psum | solution.py:208
  663.1 3.6 copy-start.18
  666.7 2.1 copy-start.49
  671.8 3.1 copy-start.13
  678.0 40.8 %copy-start.48 = (f32[256]{0:T(256)S(1)}, f32[256]{0:T(256)}, u32[]{:S(2)}) copy-start(f32[256]{0:T(256)} %get-tuple-element.296) | copy-start | bytes 3076
  678.1 74.1 %copy-start.10 = (f32[1024,512]{1,0:T(8,128)S(1)}, f32[1024,512]{1,0:T(8,128)}, u32[]{:S(2)}) copy-start(f32[1024,512]{1,0:T(8,128)} %copy-done.9) | copy-start | bytes 6291460
  678.1 74.1 %copy-start.34 = (f32[1024]{0:T(1024)S(1)}, f32[1024]{0:T(1024)}, u32[]{:S(2)}) copy-start(f32[1024]{0:T(1024)} %copy-done.33) | copy-start | bytes 12292
  804.6 2.8 copy-start.30
  804.6 3.6 copy-start.29
  804.6 4.4 copy-start.28
  804.6 5.2 copy-start.1
  (16 other events, 16.5 us)
Sparse Core Ops, SparseCore 0:
  9.6 35.8 all-gather.4
  115.6 31.8 reduce-scatter.4
  151.7 33.1 all-gather.6
  195.9 31.8 reduce-scatter.6
  237.3 33.1 all-gather.8
  278.4 31.8 reduce-scatter.8
  318.8 33.1 all-gather.10
  663.2 32.4 reduce-scatter.10
  700.7 103.8 all-reduce.4
where the time goes:
time: 821 us; the launch traced here: 817 us
  matrix products  357 us (43%)
  waiting for transfers between devices  280 us (34%)
  blocking collectives  73.2 us (9%)
  other arithmetic  46 us (6%)
  local copies, waits for them, and re-layouts  34.7 us (4%)
  between operations  14.7 us (2%)
  loops' own time  9.78 us (1%)
    dot_general x4, matrix products, back_block(): jnp.einsum('hqk,qhd->khd', logit_grad, query_block, preferred_element_typ...  104 us
    dot_general x4, matrix products, back_block(): jnp.einsum('hqk,khd->qhd', logit_grad, keys_all, preferred_element_type=j...  95.9 us
    psum x1, waiting for transfers between devices, local(): lax.psum((qkv_weight_grad, bias_grad, out_grad, up_grad, up_bias_grad, do...  49.6 us
    psum x1, blocking collectives, local(): lax.psum((out_bias_grad, gain_one_grad, shift_one_grad, down_bias_grad, g...  39.8 us
    dot_general x4, matrix products, back_block(): jnp.einsum('qhd,khd->hqk', grad_block, values_all, preferred_element_type...  36.1 us
    all_gather x1, waiting for transfers between devices, local(): gathered = lax.all_gather(layer_input, 'tensor', axis=0, tiled=True)  34.8 us
    psum x1, blocking collectives, local(): lax.psum((qkv_weight_grad, bias_grad, out_grad, up_grad, up_bias_grad, do...  33.4 us
    all_gather x1, waiting for transfers between devices, local(): grad_all = lax.all_gather(grad_two_low, 'tensor', axis=0, tiled=True)  33.2 us
  transfers between devices with their start and end apart: 9, of which 8 were waited for; matrix products, arithmetic and copies ran while one was open for 2% of the time, Pallas kernels for 0%

commit v1 on v0

v1 whole, which is shorter than its diff:
```python
import functools

import jax
import jax.numpy as jnp
from jax import lax
from jax.experimental import pallas as pl
from jax.experimental.pallas import tpu as pltpu
from jax.sharding import PartitionSpec as P

HD = 64
LANES = 128
NORM_EPS = 1e-05
MASK_BIG = 2.0**100
LOG2E = 1.4426950408889634
VMEM_BYTES = 58 * 2**20
BF = jnp.bfloat16
F32 = jnp.float32
VMEM = pl.BlockSpec(memory_space=pltpu.VMEM)
HBM = pl.BlockSpec(memory_space=pl.ANY)


def dot(left, right, left_dim, right_dim):
    return lax.dot_general(
        left, right, (((left_dim,), (right_dim,)), ((), ())), preferred_element_type=F32
    )


def params():
    return pltpu.CompilerParams(vmem_limit_bytes=VMEM_BYTES)


def cost(macs, moved):
    return pl.CostEstimate(flops=2 * macs, bytes_accessed=moved, transcendentals=0)


def key_value_blocks(x_block, w_k, w_v, bias_v, extra_k, extra_v, k_ref, v_ref, rows):
    heads = k_ref.shape[0]
    low = lax.broadcasted_iota(jnp.int32, extra_k.shape, 1) < HD
    keys = dot(x_block, w_k, 1, 0)
    values = dot(x_block, w_v, 1, 0) + bias_v
    for h in range(heads):
        pair = slice((h // 2) * LANES, (h // 2 + 1) * LANES)
        k_pair, v_pair = keys[:, pair], values[:, pair]
        if h % 2:
            k_pair, v_pair = pltpu.roll(k_pair, HD, 1), pltpu.roll(v_pair, HD, 1)
        k_ref[h, rows, :] = jnp.where(low, k_pair, extra_k).astype(BF)
        v_ref[h, rows, :] = jnp.where(low, v_pair, extra_v).astype(BF)


def project_kernel(block, x_ref, w_ref, bias_v_ref, extra_k_ref, k_ref, v_ref):
    width = x_ref.shape[1]
    w_k, w_v = w_ref[:, width : 2 * width], w_ref[:, 2 * width :]
    lane = lax.broadcasted_iota(jnp.int32, (block, LANES), 1)
    extra_v = jnp.where((lane == HD) | (lane == HD + 1), 1.0, 0.0)

    @pl.loop(0, x_ref.shape[0] // block)
    def _(i):
        rows = pl.ds(pl.multiple_of(i * block, block), block)
        key_value_blocks(
            x_ref[rows, :], w_k, w_v, bias_v_ref[...], extra_k_ref[rows, :], extra_v, k_ref, v_ref, rows
        )


def project(x, w_qkv, bias_v, extra_k):
    tokens, width = x.shape
    heads = width // HD
    out = jax.ShapeDtypeStruct((heads, tokens, LANES), BF)
    return pl.pallas_call(
        functools.partial(project_kernel, 256),
        out_shape=(out, out),
        in_specs=[VMEM] * 4,
        out_specs=(VMEM, VMEM),
        compiler_params=params(),
        cost_estimate=cost(2 * tokens * width * width, 8 * tokens * width),
        name="project_kv",
    )(x, w_qkv, bias_v, extra_k)


def query_kernel(x_ref, w_ref, bias_ref, bias_col_ref, extra_ref, qt_ref, q_ref):
    width = x_ref.shape[1]
    w_q = w_ref[:, :width]
    q_ref[...] = (dot(x_ref[...], w_q, 1, 0) + bias_ref[...]).astype(BF)
    for h in range(width // HD):
        head = slice(h * HD, (h + 1) * HD)
        turned = dot(w_ref[:, head], x_ref[...], 0, 1) + bias_col_ref[head, :]
        qt_ref[h, :HD, :] = turned.astype(BF)
        qt_ref[h, HD:, :] = extra_ref[...]


def project_queries(x, w_qkv, bias, bias_col, extra):
    tokens, width = x.shape
    return pl.pallas_call(
        query_kernel,
        out_shape=(
            jax.ShapeDtypeStruct((width // HD, LANES, tokens), BF),
            jax.ShapeDtypeStruct((tokens, width), BF),
        ),
        in_specs=[VMEM] * 5,
        out_specs=(VMEM, VMEM),
        compiler_params=params(),
        cost_estimate=cost(2 * tokens * width * width, 8 * tokens * width),
        name="project_q",
    )(x, w_qkv, bias, bias_col, extra)


def attend_kernel(
    block, qt_ref, k0_ref, k1_ref, v0_ref, v1_ref, p_hbm, ot_ref, linv_ref,
    s_scr, peak_scr, row_scr, acc_scr, p_scr, sem,
):
    heads, _, queries = qt_ref.shape
    half = k0_ref.shape[1] // block
    blocks = 2 * half

    def copy_out(h, j, slot):
        return pltpu.make_async_copy(
            p_scr.at[slot], p_hbm.at[h, pl.ds(pl.multiple_of(j * block, block), block), :], sem.at[slot]
        )

    def scores(h, keys, j):
        slot = lax.rem(h, 2)
        s = dot(keys, qt_ref[h], 1, 0)
        s_scr[slot, pl.ds(pl.multiple_of(j * block, block), block), :] = s
        top = jnp.max(s.reshape(block // 8, 8, queries), axis=0)
        peak_scr[slot] = jnp.maximum(peak_scr[slot], top)

    def mix(h, values, j):
        slot = lax.rem(j, 2)

        @pl.when((h > 0) | (j > 1))
        def _():
            copy_out(h, j, slot).wait()

        s = s_scr[lax.rem(h, 2), pl.ds(pl.multiple_of(j * block, block), block), :]
        p = jnp.exp2((s - row_scr[...]) * (LOG2E * HD**-0.5)).astype(BF)
        p_scr[slot] = p
        copy_out(h, j, slot).start()
        acc_scr[...] += dot(values, p, 0, 0)

    def at(j):
        return pl.ds(pl.multiple_of(j * block, block), block)

    def over_blocks(h, score, mixing):
        for part, (k_ref, v_ref) in enumerate(((k0_ref, v0_ref), (k1_ref, v1_ref))):

            @pl.loop(0, half)
            def _(i):
                j = part * half + i
                if score:
                    scores(h + 1, k_ref[h + 1, at(i), :], j)
                if mixing:
                    mix(h, v_ref[h, at(i), :], j)

    def open_scores(h):
        peak_scr[lax.rem(h, 2)] = jnp.full((8, queries), -jnp.inf, F32)

    def open_mix(h):
        row_scr[...] = jnp.max(peak_scr[lax.rem(h, 2)], axis=0, keepdims=True)
        acc_scr[...] = jnp.zeros_like(acc_scr)

    def close_mix(h):
        inverse = 1.0 / acc_scr[HD : HD + 1, :]
        linv_ref[h] = inverse
        ot_ref[h] = acc_scr[:HD, :] * inverse

    open_scores(0)
    over_blocks(-1, True, False)

    @pl.loop(0, heads - 1)
    def _(h):
        open_scores(h + 1)
        open_mix(h)
        over_blocks(h, True, True)
        close_mix(h)

    open_mix(heads - 1)
    over_blocks(heads - 1, False, True)
    close_mix(heads - 1)
    for slot in range(2):
        copy_out(heads - 1, blocks - 2 + slot, slot).wait()


def attend(qt, k_own, k_oth, v_own, v_oth):
    heads, _, queries = qt.shape
    keys = 2 * k_own.shape[1]
    block = 256
    return pl.pallas_call(
        functools.partial(attend_kernel, block),
        out_shape=(
            jax.ShapeDtypeStruct((heads, keys, queries), BF),
            jax.ShapeDtypeStruct((heads, HD, queries), F32),
            jax.ShapeDtypeStruct((heads, 1, queries), F32),
        ),
        in_specs=[VMEM] * 5,
        out_specs=(HBM, VMEM, VMEM),
        scratch_shapes=[
            pltpu.VMEM((2, keys, queries), F32),
            pltpu.VMEM((2, 8, queries), F32),
            pltpu.VMEM((1, queries), F32),
            pltpu.VMEM((LANES, queries), F32),
            pltpu.VMEM((2, block, queries), BF),
            pltpu.SemaphoreType.DMA((2,)),
        ],
        compiler_params=params(),
        cost_estimate=cost(heads * keys * queries * 512, 2 * heads * keys * queries),
        name="attend",
    )(qt, k_own, k_oth, v_own, v_oth)


def normalize(values):
    mean = jnp.mean(values, axis=-1, keepdims=True)
    centered = values - mean
    inverse = lax.rsqrt(jnp.mean(centered * centered, axis=-1, keepdims=True) + NORM_EPS)
    return centered * inverse, inverse


def norm_back(e, normed, inverse):
    return inverse * (
        e - jnp.mean(e, axis=-1, keepdims=True) - normed * jnp.mean(e * normed, axis=-1, keepdims=True)
    )


def middle_kernel(
    block, x_ref, cot_ref, ot_ref, linv_ref, w_out_ref, w_up_ref, w_down_ref, b_up_ref,
    vec_ref, act_ref, res_ref, dot_ref, dnat_ref, gw_ref, small_ref, att_scr,
):
    tokens, width = x_ref.shape
    heads = width // HD
    b_out, gain1, bias1, b_down, gain2, bias2 = (vec_ref[i : i + 1, :] for i in range(6))
    gw_ref[...] = jnp.zeros_like(gw_ref)
    small_ref[...] = jnp.zeros_like(small_ref)

    def col_sum(row, values):
        small_ref[row : row + 1, :] += jnp.sum(values, axis=0, keepdims=True)

    @pl.loop(0, tokens // block)
    def _(i):
        rows = pl.ds(pl.multiple_of(i * block, block), block)
        for h in range(heads):
            att_scr[h * HD : (h + 1) * HD, :] = ot_ref[h, :, rows].astype(BF)
        att = att_scr[...]
        first_sum = x_ref[rows, :].astype(F32) + dot(att, w_out_ref[...], 0, 0) + b_out
        n1, inv1 = normalize(first_sum)
        first = n1 * gain1 + bias1
        first_low = first.astype(BF)
        pre = dot(first_low, w_up_ref[...], 1, 0) + b_up_ref[...]
        cdf = 0.5 * (1.0 + lax.erf(pre * 0.5**0.5))
        hidden = (pre * cdf).astype(BF)
        slope = cdf + pre * (0.3989422804014327 * jnp.exp(-0.5 * pre * pre))
        n2, inv2 = normalize(first + dot(hidden, w_down_ref[...], 1, 0) + b_down)
        act_ref[rows, :] = (n2 * gain2 + bias2).astype(BF)
        cot = cot_ref[rows, :].astype(F32)
        two = norm_back(cot * gain2, n2, inv2)
        col_sum(3, two)
        col_sum(4, cot * n2)
        col_sum(5, cot)
        two_low = two.astype(BF)
        gw_ref[2] += dot(hidden, two_low, 0, 0)
        pre_grad = (dot(two_low, w_down_ref[...], 1, 1) * slope).astype(BF)
        gw_ref[1] += dot(first_low, pre_grad, 0, 0)
        col_sum(6, pre_grad.astype(F32))
        one = two + dot(pre_grad, w_up_ref[...], 1, 1)
        col_sum(1, one * n1)
        col_sum(2, one)
        res = norm_back(one * gain1, n1, inv1)
        col_sum(0, res)
        res_ref[rows, :] = res
        res_low = res.astype(BF)
        gw_ref[0] += dot(att, res_low, 1, 0)
        for h in range(heads):
            head = slice(h * HD, (h + 1) * HD)
            grad = dot(w_out_ref[head, :], res_low, 1, 1).astype(BF).astype(F32)
            grad = (grad * linv_ref[h, :, rows]).astype(BF)
            dot_ref[h, :HD, rows] = grad
            inner = -jnp.sum(grad.astype(F32) * ot_ref[h, :, rows], axis=0, keepdims=True)
            high = inner.astype(BF).astype(F32)
            pick = lax.broadcasted_iota(jnp.int32, (HD, block), 0)
            dot_ref[h, HD:, rows] = jnp.where(
                pick == 0, high, jnp.where(pick == 1, inner - high, 0.0)
            ).astype(BF)
            att_scr[head, :] = grad
        dnat_ref[rows, :] = att_scr[...].T


def middle(x, cot, ot, linv, w_out, w_up, w_down, b_up, vectors):
    tokens, width = x.shape
    heads = width // HD
    block = 256
    return pl.pallas_call(
        functools.partial(middle_kernel, block),
        out_shape=(
            jax.ShapeDtypeStruct((tokens, width), BF),
            jax.ShapeDtypeStruct((tokens, width), F32),
            jax.ShapeDtypeStruct((heads, LANES, tokens), BF),
            jax.ShapeDtypeStruct((tokens, width), BF),
            jax.ShapeDtypeStruct((3, width, width), F32),
            jax.ShapeDtypeStruct((8, width), F32),
        ),
        in_specs=[VMEM] * 9,
        out_specs=(VMEM,) * 6,
        scratch_shapes=[pltpu.VMEM((width, block), BF)],
        compiler_params=params(),
        cost_estimate=cost(9 * tokens * width * width, 20 * tokens * width),
        name="middle",
    )(x, cot, ot, linv, w_out, w_up, w_down, b_up, vectors)


def backward_kernel(
    block, p_hbm, dot_ref, dnat_ref, q_ref, k0_ref, k1_ref, v0_ref, v1_ref,
    dqt_ref, dk_ref, dv_ref, acc_scr, p_scr, sem,
):
    heads, _, queries = dot_ref.shape
    half = k0_ref.shape[1] // block
    blocks = 2 * half
    pairs = heads // 2
    low = lax.broadcasted_iota(jnp.int32, (block, LANES), 1) < HD

    def at(j):
        return pl.ds(pl.multiple_of(j * block, block), block)

    def copy_in(p, j, slot):
        return pltpu.make_async_copy(p_hbm.at[pl.ds(2 * p, 2), at(j), :], p_scr.at[slot], sem.at[slot])

    copy_in(0, 0, 0).start()

    @pl.loop(0, pairs)
    def _(p):
        lanes = pl.ds(pl.multiple_of(p * LANES, LANES), LANES)
        acc_scr[...] = jnp.zeros_like(acc_scr)
        for part, (k_ref, v_ref) in enumerate(((k0_ref, v0_ref), (k1_ref, v1_ref))):

            @pl.loop(0, half)
            def _(i):
                j = part * half + i
                slot = lax.rem(j, 2)
                copy_in(p, j, slot).wait()
                wrap = (j + 1) // blocks

                @pl.when(p * blocks + j + 1 < pairs * blocks)
                def _():
                    copy_in(p + wrap, lax.rem(j + 1, blocks), 1 - slot).start()

                dks, dvs = [], []
                for side in range(2):
                    h = 2 * p + side
                    prob = p_scr[slot, side]
                    slope = dot(v_ref[h, at(i), :], dot_ref[h], 1, 0)
                    dvs.append(dot(prob, dnat_ref[:, lanes], 1, 0))
                    ds = (prob.astype(F32) * slope).astype(BF)
                    dks.append(dot(ds, q_ref[:, lanes], 1, 0))
                    acc_scr[side] += dot(k_ref[h, at(i), :], ds, 0, 0)
                dk_ref[at(j), lanes] = (jnp.where(low, dks[0], dks[1]) * HD**-0.5).astype(BF)
                dv_ref[at(j), lanes] = jnp.where(low, dvs[0], dvs[1]).astype(BF)

        for side in range(2):
            dqt_ref[2 * p + side] = (acc_scr[side, :HD, :] * HD**-0.5).astype(BF)


def attend_backward(probs, dot_turned, dnat, q, k_own, k_oth, v_own, v_oth):
    heads, keys, queries = probs.shape
    width = heads * HD
    block = 256
    return pl.pallas_call(
        functools.partial(backward_kernel, block),
        out_shape=(
            jax.ShapeDtypeStruct((heads, HD, queries), BF),
            jax.ShapeDtypeStruct((keys, width), BF),
            jax.ShapeDtypeStruct((keys, width), BF),
        ),
        in_specs=[HBM] + [VMEM] * 7,
        out_specs=(VMEM,) * 3,
        scratch_shapes=[
            pltpu.VMEM((2, LANES, queries), F32),
            pltpu.VMEM((2, 2, block, queries), BF),
            pltpu.SemaphoreType.DMA((2,)),
        ],
        compiler_params=params(),
        cost_estimate=cost(heads * keys * queries * 1024, 2 * heads * keys * queries),
        name="attend_back",
    )(probs, dot_turned, dnat, q, k_own, k_oth, v_own, v_oth)


def finish_kernel(block, x0_ref, x1_ref, res_ref, dqt_ref, dk_ref, dv_ref, w_ref, own_ref, oth_ref, gw_ref, bias_ref):
    tokens, width = x0_ref.shape
    half = tokens // block
    gw_ref[...] = jnp.zeros_like(gw_ref)
    bias_ref[...] = jnp.zeros_like(bias_ref)
    w_q, w_k, w_v = (w_ref[:, i * width : (i + 1) * width] for i in range(3))

    @pl.loop(0, half)
    def _(i):
        rows = pl.ds(pl.multiple_of(i * block, block), block)
        after = pl.ds(pl.multiple_of((half + i) * block, block), block)
        dq = dqt_ref[:, rows].T
        dk, dv = dk_ref[rows, :], dv_ref[rows, :]
        own_ref[rows, :] = res_ref[rows, :] + dot(dq, w_q, 1, 1) + dot(dk, w_k, 1, 1) + dot(dv, w_v, 1, 1)
        dk1, dv1 = dk_ref[after, :], dv_ref[after, :]
        oth_ref[rows, :] = (dot(dk1, w_k, 1, 1) + dot(dv1, w_v, 1, 1)).astype(BF)
        x0, x1 = x0_ref[rows, :], x1_ref[rows, :]
        gw_ref[:, :width] += dot(x0, dq, 0, 0)
        gw_ref[:, width : 2 * width] += dot(x0, dk, 0, 0) + dot(x1, dk1, 0, 0)
        gw_ref[:, 2 * width :] += dot(x0, dv, 0, 0) + dot(x1, dv1, 0, 0)
        bias_ref[0:1, :] += jnp.sum(dq.astype(F32), axis=0, keepdims=True)
        bias_ref[1:2, :] += jnp.sum(dv.astype(F32) + dv1.astype(F32), axis=0, keepdims=True)


def finish(x_own, x_oth, res, dqt, dk, dv, w_qkv):
    tokens, width = x_own.shape
    return pl.pallas_call(
        functools.partial(finish_kernel, 256),
        out_shape=(
            jax.ShapeDtypeStruct((tokens, width), F32),
            jax.ShapeDtypeStruct((tokens, width), BF),
            jax.ShapeDtypeStruct((width, 3 * width), F32),
            jax.ShapeDtypeStruct((8, width), F32),
        ),
        in_specs=[VMEM] * 7,
        out_specs=(VMEM,) * 4,
        compiler_params=params(),
        cost_estimate=cost(10 * tokens * width * width, 20 * tokens * width),
        name="finish",
    )(x_own, x_oth, res, dqt, dk, dv, w_qkv)


def mask_columns(known, lengths):
    positions = jnp.arange(known.shape[0], dtype=jnp.int32)
    ends = jnp.cumsum(lengths)
    starts = ends - lengths
    inside = (positions[:, None] >= starts[None, :]) & (positions[:, None] < ends[None, :])
    opening = jnp.any((positions[:, None] == starts[None, :]) & (lengths[None, :] > 0), axis=1)
    dead = ~((known > 0) | opening)
    slots = lengths.shape[0]
    keys = jnp.concatenate([inside, dead[:, None]], axis=1).astype(F32)
    keys = jnp.pad(keys, ((0, 0), (HD, LANES - HD - slots - 1)))
    queries = jnp.where(jnp.pad(inside, ((0, 0), (0, 1))), 0.0, -MASK_BIG)
    queries = jnp.pad(queries, ((0, 0), (0, HD - slots - 1))).T.astype(BF)
    return keys, queries


def local(
    layer_input, gene_known, cell_genes, w_qkv, bias_qv, w_out, b_out, ln1_gain, ln1_bias,
    w_up, b_up, w_down, b_down, ln2_gain, ln2_bias, cotangent,
):
    tokens, width = layer_input.shape
    shard = w_qkv.shape[2]
    swap = [(0, 1), (1, 0)]
    side = lax.axis_index("tensor")

    def swapped(values):
        return lax.ppermute(values, "tensor", swap)

    x_oth = swapped(layer_input)
    qkv_oth, bias_oth = swapped(w_qkv), swapped(bias_qv)
    out_oth, up_oth, down_oth, b_up_oth = swapped(w_out), swapped(w_up), swapped(w_down), swapped(b_up)

    w_all = jnp.concatenate([w_qkv, qkv_oth], axis=2).reshape(width, 3 * width)
    bias_all = jnp.concatenate([bias_qv, bias_oth], axis=1).astype(F32)
    w_out_all = jnp.concatenate([w_out, out_oth], axis=0)
    w_up_all = jnp.concatenate([w_up, up_oth], axis=1)
    w_down_all = jnp.concatenate([w_down, down_oth], axis=0)
    b_up_all = jnp.concatenate([b_up, b_up_oth])[None].astype(F32)

    key_cols, query_rows = mask_columns(gene_known, cell_genes[0])
    key_own = lax.dynamic_slice_in_dim(key_cols, side * tokens, tokens, 0)
    key_oth = lax.dynamic_slice_in_dim(key_cols, (1 - side) * tokens, tokens, 0)
    query_own = lax.dynamic_slice_in_dim(query_rows, side * tokens, tokens, 1)

    qt, q = project_queries(layer_input, w_all, bias_all[:1], bias_all[0][:, None], query_own)
    k_own, v_own = project(layer_input, w_all, bias_all[1:], key_own)
    k_oth, v_oth = project(x_oth, w_all, bias_all[1:], key_oth)
    probs, ot, linv = attend(qt, k_own, k_oth, v_own, v_oth)
    vectors = jnp.stack([b_out, ln1_gain, ln1_bias, b_down, ln2_gain, ln2_bias, b_out, b_out])
    activations, res, dot_turned, dnat, gw_mid, small = middle(
        layer_input, cotangent, ot, linv, w_out_all, w_up_all, w_down_all, b_up_all, vectors
    )
    dqt, dk, dv = attend_backward(probs, dot_turned, dnat, q, k_own, k_oth, v_own, v_oth)
    grad_own, grad_oth, gw_qkv, bias_grad = finish(
        layer_input, x_oth, res, dqt.reshape(width, tokens), dk, dv, w_all
    )
    input_grad = grad_own + swapped(grad_oth).astype(F32)

    def shards(values, axis):
        return lax.slice_in_dim(values, 0, shard, axis=axis), lax.slice_in_dim(values, shard, 2 * shard, axis=axis)

    parts = [
        shards(gw_qkv.reshape(width, 3, width), 2),
        shards(bias_grad[:2], 1),
        shards(gw_mid[0], 0),
        shards(gw_mid[1], 1),
        shards(small[6], 0),
        shards(gw_mid[2], 0),
    ]
    got = [swapped(oth.astype(BF)).astype(F32) + own for own, oth in parts]
    qkv_g, bias_g, out_g, up_g, b_up_g, down_g = lax.psum(got, "dp")
    small_g = lax.psum(small[:6], ("dp", "tensor"))
    return (
        activations, input_grad, qkv_g, bias_g, out_g, small_g[0], small_g[1], small_g[2],
        up_g, b_up_g, down_g, small_g[3], small_g[4], small_g[5],
    )


def solution(mesh):
    placed = (
        P(("dp", "tensor"), None),
        P("dp"),
        P("dp", None),
        P(None, None, "tensor"),
        P(None, "tensor"),
        P("tensor", None),
        P(),
        P(),
        P(),
        P(None, "tensor"),
        P("tensor"),
        P("tensor", None),
        P(),
        P(),
        P(),
        P(("dp", "tensor"), None),
    )
    return jax.shard_map(
        local,
        mesh=mesh,
        in_specs=placed,
        out_specs=(
            P(("dp", "tensor"), None),
            P(("dp", "tensor"), None),
            P(None, None, "tensor"),
            P(None, "tensor"),
            P("tensor", None),
            P(),
            P(),
            P(),
            P(None, "tensor"),
            P("tensor"),
            P("tensor", None),
            P(),
            P(),
            P(),
        ),
        check_vma=False,
    )
```

time: 821 us -> 360 us (0.44)
  matrix products: 357 us -> 0 us
  waiting for transfers between devices: 280 us -> 59.2 us
  Pallas kernels: 0 us -> 144 us
  other arithmetic: 46 us -> 18.4 us
  starting transfers between devices: 0.63 us -> 16.2 us
  local copies, waits for them, and re-layouts: 34.7 us -> 20.5 us
  blocking collectives: 73.2 us -> 85.2 us
  loops' own time: 9.78 us -> 0 us
    dot_general x40 -> x0, matrix products: 357 us -> none  [the longest x4 104 us: back_block(): jnp.einsum('hqk,qhd->khd', logit_grad, query_block, preferred_element_typ...]
    pallas_call x0 -> x7, Pallas kernels: none -> 144 us  [the longest x1 47.7 us: attend_backward(): pl.pallas_call(functools.partial(backward_kernel, block), out_shape=(jax....]
    all_gather x4 -> x0, waiting for transfers between devices: 134 us -> none  [the longest x1 34.8 us: local(): gathered = lax.all_gather(layer_input, 'tensor', axis=0, tiled=True)]
    reduce_scatter x4 -> x0, waiting for transfers between devices: 95.5 us -> none  [the longest x1 31.9 us: local(): lax.psum_scatter(jnp.dot(hidden_low, w_down, preferred_element_type=jnp.f...]
    ppermute x0 -> x14, waiting for transfers between devices: none -> 46.2 us  [swapped(): return lax.ppermute(values, 'tensor', swap)]
    psum x1, waiting for transfers between devices: 49.6 us -> 13 us  [local(): qkv_g, bias_g, out_g, up_g, b_up_g, down_g = lax.psum(got, 'dp')]
    reduce_sum x16 -> x0, other arithmetic: 33.3 us -> none  [the longest x4 17.3 us: attend_block(): summed = jnp.sum(expo, axis=-1, keepdims=True)]
    ppermute x0 -> x14, starting transfers between devices: none -> 16.1 us  [swapped(): return lax.ppermute(values, 'tensor', swap)]
  transfers between devices with their start and end apart: 9 -> 15, of which waited for: 8 -> 6; matrix products, arithmetic and copies ran while one was open for 2% -> 8% of each run, Pallas kernels for 0% -> 20%
where the time goes in v1:
time: 360 us; the launch traced here: 358 us
  Pallas kernels  144 us (40%)
  blocking collectives  85.2 us (24%)
  waiting for transfers between devices  59.2 us (16%)
  local copies, waits for them, and re-layouts  20.5 us (6%)
  other arithmetic  18.4 us (5%)
  starting transfers between devices  16.2 us (4%)
  between operations  14.3 us (4%)
    psum x1, blocking collectives, local(): small_g = lax.psum(small[:6], ('dp', 'tensor'))  53.7 us
    pallas_call x1, Pallas kernels, attend_backward(): pl.pallas_call(functools.partial(backward_kernel, block), out_shape=(jax....  47.7 us
    pallas_call x1, Pallas kernels, attend(): pl.pallas_call(functools.partial(attend_kernel, block), out_shape=(jax.Sh...  46.9 us
    ppermute x14, waiting for transfers between devices, swapped(): return lax.ppermute(values, 'tensor', swap)  46.2 us
    psum x1, blocking collectives, local(): qkv_g, bias_g, out_g, up_g, b_up_g, down_g = lax.psum(got, 'dp')  31.5 us
    pallas_call x1, Pallas kernels, middle(): pl.pallas_call(functools.partial(middle_kernel, block), out_shape=(jax.Sh...  18.7 us
    ppermute x14, starting transfers between devices, swapped(): return lax.ppermute(values, 'tensor', swap)  16.1 us
    psum x1, waiting for transfers between devices, local(): qkv_g, bias_g, out_g, up_g, b_up_g, down_g = lax.psum(got, 'dp')  13 us
  transfers between devices with their start and end apart: 15, of which 6 were waited for; matrix products, arithmetic and copies ran while one was open for 8% of the time, Pallas kernels for 20%

profile of v1, /device:TPU:0, one launch (start us, length us, event | category | flops | bytes accessed | tf_op | source)
XLA Modules:
  0.0 357.7 jit_solution(6784263149575721316)
XLA Ops:
  7.2 3.0 collective-permute-start.6
  10.3 1.9 collective-permute-start.3
  12.4 1.9 collective-permute-start.5
  15.6 0.8 reduce-window.4
  17.2 0.7 or_not_fusion
  18.5 1.4 copy.46
  21.0 1.0 constant_dynamic-slice_fusion
  23.4 1.9 collective-permute-start.2
  26.0 0.9 copy.48.bias_col_ref
  26.8 1.8 pad_maximum_fusion.1.w_out_ref
  28.6 1.8 pad_maximum_fusion.2.w_up_ref
  30.4 0.7 collective-permute-done.5
  31.1 1.8 pad_maximum_fusion.3.w_down_ref
  32.9 15.0 %collective-permute-done = bf16[512,3,256]{0,2,1:T(8,128)(2,1)S(1)} collective-permute-done((bf16[512,3,256]{0,2,1:T(8,128)(2,1)S(1)}, bf16[512,3,256]{0,2,1:T(8,128)(2,1)S(1)}, u32[]{:S(2)}, u32[]{:S(2)}) %collective-permute-start) | collective-permute-done | bytes 786464 | tf_op jit(solution)/shard_map/ppermute | solution.py:449
  48.0 1.8 copy.47.w_ref
  49.7 5.8 %project_kv.2 = (bf16[8,1024,128]{2,1,0:T(8,128)(2,1)}, bf16[8,1024,128]{2,1,0:T(8,128)(2,1)}) custom-call(bf16[1024,512]{1,0:T(8,128)(2,1)} %x0_ref.1, bf16[512,1536]{1,0:T(8,128)(2,1)} %copy.47.w_ref, f32[1,512]{1,0:T(1,128)} %get-tuple-element.104.bias_v_ref, f32[1024,128]{1,0:T(8,128)} %get-tuple-element.97.extra_k_ref), custom_call_target="tpu_custom_call" | custom-call | flops 1073741824 | bytes 4194304 | tf_op jit(solution)/shard_map/project_kv/pallas_call | solution.py:68
  55.6 6.3 %project_q.1 = (bf16[8,128,1024]{2,1,0:T(8,128)(2,1)}, bf16[1024,512]{1,0:T(8,128)(2,1)}) custom-call(bf16[1024,512]{1,0:T(8,128)(2,1)} %x0_ref.1, bf16[512,1536]{1,0:T(8,128)(2,1)} %copy.47.w_ref, f32[1,512]{1,0:T(1,128)} %get-tuple-element.106.bias_ref, f32[512,1]{1,0:T(8,128)} %copy.48.bias_col_ref, bf16[64,1024]{1,0:T(8,128)(2,1)} %fusion.extra_ref), custom_call_target="tpu_custom_call" | custom-call | flops 1073741824 | bytes 4194304 | tf_op jit(solution)/shard_map/project_q/pallas_call | solution.py:92
  61.8 7.2 %collective-permute-done.2.x_ref.x1_ref = bf16[1024,512]{1,0:T(8,128)(2,1)} collective-permute-done((bf16[1024,512]{1,0:T(8,128)(2,1)}, bf16[1024,512]{1,0:T(8,128)(2,1)}, u32[]{:S(2)}, u32[]{:S(2)}) %collective-permute-start.2) | collective-permute-done | bytes 1048608 | tf_op jit(solution)/shard_map/ppermute | solution.py:449
  69.0 5.8 %project_kv.3 = (bf16[8,1024,128]{2,1,0:T(8,128)(2,1)}, bf16[8,1024,128]{2,1,0:T(8,128)(2,1)}) custom-call(bf16[1024,512]{1,0:T(8,128)(2,1)} %collective-permute-done.2.x_ref.x1_ref, bf16[512,1536]{1,0:T(8,128)(2,1)} %copy.47.w_ref, f32[1,512]{1,0:T(1,128)} %get-tuple-element.104.bias_v_ref, f32[1024,128]{1,0:T(8,128)} %get-tuple-element.96.extra_k_ref), custom_call_target="tpu_custom_call" | custom-call | flops 1073741824 | bytes 4194304 | tf_op jit(solution)/shard_map/project_kv/pallas_call | solution.py:68
  74.8 46.9 %attend.1 = (bf16[8,2048,1024]{2,1,0:T(8,128)(2,1)}, f32[8,64,1024]{2,1,0:T(8,128)}, f32[8,1,1024]{2,1,0:T(1,128)}) custom-call(bf16[8,128,1024]{2,1,0:T(8,128)(2,1)} %get-tuple-element.36.qt_ref, bf16[8,1024,128]{2,1,0:T(8,128)(2,1)} %get-tuple-element.37.k0_ref, bf16[8,1024,128]{2,1,0:T(8,128)(2,1)} %get-tuple-element.38.k1_ref, ...), custom_call_target="tpu_custom_call" | custom-call | flops 17179869184 | bytes 33554432 | tf_op jit(solution)/shard_map/attend/pallas_call | solution.py:186
  121.7 18.7 %middle.1 = (bf16[1024,512]{1,0:T(8,128)(2,1)}, f32[1024,512]{1,0:T(8,128)}, bf16[8,128,1024]{2,1,0:T(8,128)(2,1)}, bf16[1024,512]{1,0:T(8,128)(2,1)}, f32[3,512,512]{2,1,0:T(8,128)}, /*index=5*/f32[8,512]{1,0:T(8,128)}) custom-call(bf16[1024,512]{1,0:T(8,128)(2,1)} %x0_ref.1, bf16[1024,512]{1,0:T(8,128)(2,1)} %cot_ref.1, ...), custom_call_target="tpu_custom_call" | custom-call | flops 4831838208 | bytes 10485760 | tf_op jit(solution)/shard_map/middle/pallas_call | solution.py:288
  140.4 1.3 slice_bitcast_fusion
  141.7 1.0 copy-done
  142.7 0.7 slice.155
  143.4 1.7 collective-permute-start.11
  145.1 47.7 %attend_back.1 = (bf16[8,64,1024]{2,1,0:T(8,128)(2,1)}, bf16[2048,512]{1,0:T(8,128)(2,1)}, bf16[2048,512]{1,0:T(8,128)(2,1)}) custom-call(bf16[8,2048,1024]{2,1,0:T(8,128)(2,1)} %get-tuple-element.45.p_hbm, bf16[8,128,1024]{2,1,0:T(8,128)(2,1)} %get-tuple-element.46.dot_ref, bf16[1024,512]{1,0:T(8,128)(2,1)} %get-tuple-element.47.dnat_ref, ...), custom_call_target="tpu_custom_call" | custom-call | flops 34359738368 | bytes 33554432 | tf_op jit(solution)/shard_map/attend_back/pallas_call | solution.py:362
  192.8 12.7 %finish.1 = (f32[1024,512]{1,0:T(8,128)}, bf16[1024,512]{1,0:T(8,128)(2,1)}, f32[512,1536]{1,0:T(8,128)}, f32[8,512]{1,0:T(8,128)}) custom-call(bf16[1024,512]{1,0:T(8,128)(2,1)} %x0_ref.1, bf16[1024,512]{1,0:T(8,128)(2,1)} %collective-permute-done.2.x_ref.x1_ref, f32[1024,512]{1,0:T(8,128)} %get-tuple-element.44.res_ref, bf16[512,1024]{1,0:T(8,128)(2,1)} %bitcast.62, ...), custom_call_target="tpu_custom_call" | custom-call | flops 5368709120 | bytes 10485760 | tf_op jit(solution)/shard_map/finish/pallas_call | solution.py:408
  205.4 2.4 copy.53
  208.4 2.1 convert.25
  210.5 1.7 collective-permute-start.13
  212.6 0.9 slice_add_fusion.1
  213.5 20.5 %collective-permute-done.13 = bf16[256,512]{1,0:T(8,128)(2,1)S(1)} collective-permute-done((bf16[256,512]{1,0:T(8,128)(2,1)S(1)}, bf16[256,512]{1,0:T(8,128)(2,1)S(1)}, u32[]{:S(2)}, u32[]{:S(2)}) %collective-permute-start.13) | collective-permute-done | bytes 262176 | tf_op jit(solution)/shard_map/ppermute | solution.py:449
  234.0 2.8 collective-permute-done.10
  236.8 2.3 bitcast_add_fusion
  239.1 1.4 slice_add_fusion
  240.6 0.7 collective-permute-start.7
  241.3 0.7 slice.156
  242.0 1.4 collective-permute-start.12
  243.4 0.7 collective-permute-start.9
  244.1 53.7 %psum.52 = f32[6,512]{1,0:T(8,128)S(1)} all-reduce(f32[6,512]{1,0:T(8,128)S(1)} %bitcast.44), channel_id=1, replica_groups=mesh['dp'=16,'tensor'=2] {'dp','tensor'}, use_global_device_ids=true, to_apply=%region_5.6 | all-reduce | flops 3072 | bytes 24576 | tf_op jit(solution)/shard_map/psum | solution.py:494
  298.5 0.7 slice_add_fusion.2
  299.2 31.5 %all-reduce.3 = (f32[2,256]{1,0:T(2,128)}, f32[256]{0:T(256)}) all-reduce(f32[2,256]{1,0:T(2,128)S(1)} %slice_add_fusion.2, f32[256]{0:T(256)S(1)} %convert_add_fusion.1), channel_id=1, replica_groups=mesh['dp'=16,'tensor'=2] {'dp'}, use_global_device_ids=true, to_apply=%region_3.4 | all-reduce | flops 768 | bytes 6144 | tf_op jit(solution)/shard_map/psum | solution.py:493
  330.7 1.6 convert_add_fusion
  332.3 13.0 %all-reduce.7.cloned.1.call-done = (f32[512,3,256]{0,2,1:T(8,128)}, f32[256,512]{1,0:T(8,128)}, f32[512,256]{1,0:T(8,128)}, f32[256,512]{1,0:T(8,128)}) async-done(((f32[512,3,256]{0,2,1:T(8,128)}, f32[256,512]{1,0:T(8,128)}, f32[512,256]{1,0:T(8,128)}, f32[256,512]{1,0:T(8,128)}), (f32[512,3,256]{0,2,1:T(8,128)}, f32[256,512]{1,0:T(8,128)}, f32[512,256]{1,0:T(8,128)}, ...) | async-done | bytes 3145744 | tf_op jit(solution)/shard_map/psum | solution.py:493
  345.3 3.1 copy.54
  348.5 0.8 copy.59
  349.3 0.8 copy.60
  350.1 0.8 copy.61
  (71 shorter events, 7.5 us)
Async XLA Ops:
  7.2 338.2 %all-reduce.7.cloned.1.call-start = ((), (), s32[]{:S(2)}) async-start(), calls=%async_computation | async-start | bytes 6291456 | tf_op jit(solution)/shard_map/psum | solution.py:493
  7.2 15.5 %collective-permute-start.6 = (bf16[256]{0:T(256)(128)(2,1)}, bf16[256]{0:T(256)(128)(2,1)S(1)}, u32[]{:S(2)}, u32[]{:S(2)}) collective-permute-start(bf16[256]{0:T(256)(128)(2,1)} %param.26), channel_id=1, source_target_pairs={{0,1},{1,0},{2,3},{3,2},{4,5},{5,4},{6,7},{7,6},{8,9},{9,8},{10,11... | collective-permute-start | bytes 1544 | tf_op jit(solution)/shard_map/ppermute | solution.py:449
  10.3 13.2 %collective-permute-start.1 = (bf16[2,256]{1,0:T(2,128)(2,1)}, bf16[2,256]{1,0:T(2,128)(2,1)S(1)}, u32[]{:S(2)}, u32[]{:S(2)}) collective-permute-start(bf16[2,256]{1,0:T(2,128)(2,1)} %param.20), channel_id=1, source_target_pairs={{0,1},{1,0},{2,3},{3,2},{4,5},{5,4},{6,7},{7,6},{8,9},{9,8},{10,11... | collective-permute-start | bytes 3080 | tf_op jit(solution)/shard_map/ppermute | solution.py:449
  10.3 16.5 %collective-permute-start.3 = (bf16[256,512]{1,0:T(8,128)(2,1)}, bf16[256,512]{1,0:T(8,128)(2,1)}, u32[]{:S(2)}, u32[]{:S(2)}) collective-permute-start(bf16[256,512]{1,0:T(8,128)(2,1)} %param.21), channel_id=1, source_target_pairs={{0,1},{1,0},{2,3},{3,2},{4,5},{5,4},{6,7},{7,6},{8,9},{9,8},{10,11... | collective-permute-start | bytes 786440 | tf_op jit(solution)/shard_map/ppermute | solution.py:449
  12.3 16.3 %collective-permute-start.4 = (bf16[512,256]{1,0:T(8,128)(2,1)}, bf16[512,256]{1,0:T(8,128)(2,1)}, u32[]{:S(2)}, u32[]{:S(2)}) collective-permute-start(bf16[512,256]{1,0:T(8,128)(2,1)} %param.25), channel_id=1, source_target_pairs={{0,1},{1,0},{2,3},{3,2},{4,5},{5,4},{6,7},{7,6},{8,9},{9,8},{10,11... | collective-permute-start | bytes 786440 | tf_op jit(solution)/shard_map/ppermute | solution.py:449
  12.4 18.8 %collective-permute-start.5 = (bf16[256,512]{1,0:T(8,128)(2,1)}, bf16[256,512]{1,0:T(8,128)(2,1)}, u32[]{:S(2)}, u32[]{:S(2)}) collective-permute-start(bf16[256,512]{1,0:T(8,128)(2,1)} %param.27), channel_id=1, source_target_pairs={{0,1},{1,0},{2,3},{3,2},{4,5},{5,4},{6,7},{7,6},{8,9},{9,8},{10,11... | collective-permute-start | bytes 786440 | tf_op jit(solution)/shard_map/ppermute | solution.py:449
  19.9 2.2 copy-start.10
  19.9 2.2 copy-start.11
  19.9 2.1 copy-start.12
  19.9 2.1 copy-start.13
  20.0 2.1 copy-start.14
  20.0 2.1 copy-start.15
  20.0 5.4 %copy-start.16 = (bf16[2,256]{1,0:T(2,128)(2,1)S(1)}, bf16[2,256]{1,0:T(2,128)(2,1)}, u32[]{:S(2)}) copy-start(bf16[2,256]{1,0:T(2,128)(2,1)} %param.20) | copy-start | bytes 3076
  20.0 6.8 %copy-start.6 = (bf16[256,512]{1,0:T(8,128)(2,1)S(1)}, bf16[256,512]{1,0:T(8,128)(2,1)}, u32[]{:S(2)}) copy-start(bf16[256,512]{1,0:T(8,128)(2,1)} %param.21) | copy-start | bytes 786436
  20.3 8.3 %copy-start.7 = (bf16[512,256]{1,0:T(8,128)(2,1)S(1)}, bf16[512,256]{1,0:T(8,128)(2,1)}, u32[]{:S(2)}) copy-start(bf16[512,256]{1,0:T(8,128)(2,1)} %param.25) | copy-start | bytes 786436
  21.0 10.1 %copy-start.8 = (bf16[256,512]{1,0:T(8,128)(2,1)S(1)}, bf16[256,512]{1,0:T(8,128)(2,1)}, u32[]{:S(2)}) copy-start(bf16[256,512]{1,0:T(8,128)(2,1)} %param.27) | copy-start | bytes 786436
  22.7 25.1 %collective-permute-start = (bf16[512,3,256]{0,2,1:T(8,128)(2,1)S(1)}, bf16[512,3,256]{0,2,1:T(8,128)(2,1)S(1)}, u32[]{:S(2)}, u32[]{:S(2)}) collective-permute-start(bf16[512,3,256]{0,2,1:T(8,128)(2,1)S(1)} %copy.46), channel_id=1, source_target_pairs={{0,1},{1,0},{2,3},{3,2},{4,5},{5,4},{6,7},{7,6},{8,9},{9,8},{10,11... | collective-permute-start | bytes 2359304 | tf_op jit(solution)/shard_map/ppermute | solution.py:449
  23.4 45.6 %collective-permute-start.2 = (bf16[1024,512]{1,0:T(8,128)(2,1)}, bf16[1024,512]{1,0:T(8,128)(2,1)}, u32[]{:S(2)}, u32[]{:S(2)}) collective-permute-start(bf16[1024,512]{1,0:T(8,128)(2,1)} %x0_ref.1), channel_id=1, source_target_pairs={{0,1},{1,0},{2,3},{3,2},{4,5},{5,4},{6,7},{7,6},{8,9},{9,8},{10,11... | collective-permute-start | bytes 3145736 | tf_op jit(solution)/shard_map/ppermute | solution.py:449
  141.7 1.0 copy-start
  143.4 69.2 %collective-permute-start.11 = (bf16[512,256]{1,0:T(8,128)(2,1)}, bf16[512,256]{1,0:T(8,128)(2,1)S(1)}, u32[]{:S(2)}, u32[]{:S(2)}) collective-permute-start(bf16[512,256]{1,0:T(8,128)(2,1)} %slice.155), channel_id=1, source_target_pairs={{0,1},{1,0},{2,3},{3,2},{4,5},{5,4},{6,7},{7,6},{8,9},{9,8},{10,11... | collective-permute-start | bytes 786440 | tf_op jit(solution)/shard_map/ppermute | solution.py:449
  207.9 4.7 %copy-start.1 = (f32[512,512]{1,0:T(8,128)S(1)}, f32[512,512]{1,0:T(8,128)}, u32[]{:S(2)}) copy-start(f32[512,512]{1,0:T(8,128)} %copy-done) | copy-start | bytes 3145732
  207.9 31.2 %collective-permute-start.8 = (bf16[512,3,256]{0,2,1:T(8,128)(2,1)S(1)}, bf16[512,3,256]{0,2,1:T(8,128)(2,1)S(1)}, u32[]{:S(2)}, u32[]{:S(2)}) collective-permute-start(bf16[512,3,256]{0,2,1:T(8,128)(2,1)S(1)} %slice.154), channel_id=1, source_target_pairs={{0,1},{1,0},{2,3},{3,2},{4,5},{5,4},{6,7},{7,6},{8,9},{9,8},{10,11... | collective-permute-start | bytes 2359304 | tf_op jit(solution)/shard_map/ppermute | solution.py:449
  210.5 23.4 %collective-permute-start.13 = (bf16[256,512]{1,0:T(8,128)(2,1)S(1)}, bf16[256,512]{1,0:T(8,128)(2,1)S(1)}, u32[]{:S(2)}, u32[]{:S(2)}) collective-permute-start(bf16[256,512]{1,0:T(8,128)(2,1)S(1)} %get-tuple-element.94), channel_id=1, source_target_pairs={{0,1},{1,0},{2,3},{3,2},{4,5},{5,4},{6,7},{7,6},{8,9},{9,8},{10,11... | collective-permute-start | bytes 786440 | tf_op jit(solution)/shard_map/ppermute | solution.py:449
  212.2 24.5 %collective-permute-start.10 = (bf16[256,512]{1,0:T(8,128)(2,1)S(1)}, bf16[256,512]{1,0:T(8,128)(2,1)S(1)}, u32[]{:S(2)}, u32[]{:S(2)}) collective-permute-start(bf16[256,512]{1,0:T(8,128)(2,1)S(1)} %get-tuple-element.95), channel_id=1, source_target_pairs={{0,1},{1,0},{2,3},{3,2},{4,5},{5,4},{6,7},{7,6},{8,9},{9,8},{10,11... | collective-permute-start | bytes 786440 | tf_op jit(solution)/shard_map/ppermute | solution.py:449
  240.5 1.5 copy-start.9
  240.5 90.1 %copy-start.2 = (f32[1024,512]{1,0:T(8,128)S(1)}, f32[1024,512]{1,0:T(8,128)}, u32[]{:S(2)}) copy-start(f32[1024,512]{1,0:T(8,128)} %get-tuple-element.52) | copy-start | bytes 6291460
  240.6 90.1 %collective-permute-start.7 = (bf16[1024,512]{1,0:T(8,128)(2,1)}, bf16[1024,512]{1,0:T(8,128)(2,1)S(1)}, u32[]{:S(2)}, u32[]{:S(2)}) collective-permute-start(bf16[1024,512]{1,0:T(8,128)(2,1)} %get-tuple-element.53), channel_id=1, source_target_pairs={{0,1},{1,0},{2,3},{3,2},{4,5},{5,4},{6,7},{7,6},{8,9},{9,8},{10,11... | collective-permute-start | bytes 3145736 | tf_op jit(solution)/shard_map/ppermute | solution.py:449
  242.0 56.4 %collective-permute-start.12 = (bf16[256]{0:T(256)(128)(2,1)S(1)}, bf16[256]{0:T(256)(128)(2,1)S(1)}, u32[]{:S(2)}, u32[]{:S(2)}) collective-permute-start(bf16[256]{0:T(256)(128)(2,1)S(1)} %fusion.5), channel_id=1, source_target_pairs={{0,1},{1,0},{2,3},{3,2},{4,5},{5,4},{6,7},{7,6},{8,9},{9,8},{10,11... | collective-permute-start | bytes 1544 | tf_op jit(solution)/shard_map/ppermute | solution.py:449
  243.4 55.0 %collective-permute-start.9 = (bf16[2,256]{1,0:T(2,128)(2,1)S(1)}, bf16[2,256]{1,0:T(2,128)(2,1)S(1)}, u32[]{:S(2)}, u32[]{:S(2)}) collective-permute-start(bf16[2,256]{1,0:T(2,128)(2,1)S(1)} %slice.156), channel_id=1, source_target_pairs={{0,1},{1,0},{2,3},{3,2},{4,5},{5,4},{6,7},{7,6},{8,9},{9,8},{10,11... | collective-permute-start | bytes 3080 | tf_op jit(solution)/shard_map/ppermute | solution.py:449
  345.3 3.1 copy-start.5
  345.3 3.9 %copy-start.4 = (f32[512,256]{1,0:T(8,128)S(1)}, f32[512,256]{1,0:T(8,128)}, u32[]{:S(2)}) copy-start(f32[512,256]{1,0:T(8,128)} %get-tuple-element.117) | copy-start | bytes 1572868
  345.3 4.7 %copy-start.3 = (f32[256,512]{1,0:T(8,128)S(1)}, f32[256,512]{1,0:T(8,128)}, u32[]{:S(2)}) copy-start(f32[256,512]{1,0:T(8,128)} %get-tuple-element.119) | copy-start | bytes 1572868
Sparse Core Ops, SparseCore 0:
  240.7 104.6 all-reduce.6

commit v2 on v1

v2 whole, which is shorter than its diff:
```python
import functools

import jax
import jax.numpy as jnp
from jax import lax
from jax.experimental import pallas as pl
from jax.experimental.pallas import tpu as pltpu
from jax.sharding import PartitionSpec as P

HD = 64
LANES = 128
NORM_EPS = 1e-05
MASK_BIG = 2.0**100
LOG2E = 1.4426950408889634
VMEM_BYTES = 58 * 2**20
BF = jnp.bfloat16
F32 = jnp.float32
VMEM = pl.BlockSpec(memory_space=pltpu.VMEM)
HBM = pl.BlockSpec(memory_space=pl.ANY)


def dot(left, right, left_dim, right_dim):
    return lax.dot_general(
        left, right, (((left_dim,), (right_dim,)), ((), ())), preferred_element_type=F32
    )


def params():
    return pltpu.CompilerParams(vmem_limit_bytes=VMEM_BYTES)


def cost(macs, moved):
    return pl.CostEstimate(flops=2 * macs, bytes_accessed=moved, transcendentals=0)


def values_columns(rows):
    lane = lax.broadcasted_iota(jnp.int32, (rows, LANES), 1)
    return jnp.where((lane == HD) | (lane == HD + 1), 1.0, 0.0)


def key_value_block(x, w_refs, bias_ref, extra_k, k_ref, v_ref, rows):
    shard = w_refs[0].shape[1] // 3
    extra_k = extra_k.astype(F32)
    extra_v = values_columns(x.shape[0])
    low = lax.broadcasted_iota(jnp.int32, extra_k.shape, 1) < HD
    for side, w_ref in enumerate(w_refs):
        mine = slice(side * shard, (side + 1) * shard)
        keys = dot(x, w_ref[:, shard : 2 * shard], 1, 0)
        values = dot(x, w_ref[:, 2 * shard :], 1, 0) + bias_ref[1:2, mine]
        for i in range(shard // HD):
            pair = slice((i // 2) * LANES, (i // 2 + 1) * LANES)
            k_pair, v_pair = keys[:, pair], values[:, pair]
            if i % 2:
                k_pair, v_pair = pltpu.roll(k_pair, HD, 1), pltpu.roll(v_pair, HD, 1)
            h = side * (shard // HD) + i
            k_ref[h, rows, :] = jnp.where(low, k_pair, extra_k).astype(BF)
            v_ref[h, rows, :] = jnp.where(low, v_pair, extra_v).astype(BF)


def project_kernel(x_ref, own_ref, oth_ref, bias_ref, extra_k_ref, extra_q_ref, k_ref, v_ref, qt_ref, q_ref):
    x = x_ref[...]
    shard = own_ref.shape[1] // 3
    key_value_block(x, (own_ref, oth_ref), bias_ref, extra_k_ref[...], k_ref, v_ref, slice(None))
    for side, w_ref in enumerate((own_ref, oth_ref)):
        mine = slice(side * shard, (side + 1) * shard)
        q = (dot(x, w_ref[:, :shard], 1, 0) + bias_ref[0:1, mine]).astype(BF)
        q_ref[:, mine] = q
        turned = q.T
        for i in range(shard // HD):
            h = side * (shard // HD) + i
            qt_ref[h, :HD, :] = turned[i * HD : (i + 1) * HD, :]
            qt_ref[h, HD:, :] = extra_q_ref[...]


def project(x, w_own, w_oth, bias, extra_k, extra_q):
    tokens, width = x.shape
    heads = width // HD
    block = 256
    whole = lambda *shape: pl.BlockSpec(shape, lambda i: (0,) * len(shape))
    per_head = pl.BlockSpec((heads, block, LANES), lambda i: (0, i, 0))
    return pl.pallas_call(
        project_kernel,
        grid=(tokens // block,),
        out_shape=(
            jax.ShapeDtypeStruct((heads, tokens, LANES), BF),
            jax.ShapeDtypeStruct((heads, tokens, LANES), BF),
            jax.ShapeDtypeStruct((heads, LANES, tokens), BF),
            jax.ShapeDtypeStruct((tokens, width), BF),
        ),
        in_specs=[
            pl.BlockSpec((block, width), lambda i: (i, 0)),
            whole(*w_own.shape),
            whole(*w_oth.shape),
            whole(*bias.shape),
            pl.BlockSpec((block, LANES), lambda i: (i, 0)),
            pl.BlockSpec((HD, block), lambda i: (0, i)),
        ],
        out_specs=(
            per_head,
            per_head,
            pl.BlockSpec((heads, LANES, block), lambda i: (0, 0, i)),
            pl.BlockSpec((block, width), lambda i: (i, 0)),
        ),
        compiler_params=params(),
        cost_estimate=cost(3 * tokens * width * width, 12 * tokens * width),
        name="project",
    )(x, w_own, w_oth, bias, extra_k, extra_q)


def attend_kernel(
    sub, chunk, qt_hbm, k_hbm, v_hbm, x_ref, own_ref, oth_ref, bias_ref, extra_ref,
    p_hbm, ot_ref, linv_ref, k_oth_hbm, v_oth_hbm,
    qt_ref, k0_ref, k1_ref, v0_ref, v1_ref,
    s0_scr, s1_scr, peak0_scr, peak1_scr, row_scr, acc_scr, p_scr, sem, in_sem, out_sem,
):
    heads, _, queries = qt_ref.shape
    half = k0_ref.shape[1]
    parts = queries // chunk
    steps = heads * parts
    slots = p_scr.shape[0]

    def copies_in(h):
        return [
            pltpu.make_async_copy(src.at[h], dst.at[h], in_sem.at[h, n])
            for n, (src, dst) in enumerate(((qt_hbm, qt_ref), (k_hbm, k0_ref), (v_hbm, v0_ref)))
        ]

    for h in range(heads):
        for copy in copies_in(h):
            copy.start()

    @pl.loop(0, half // sub)
    def _(i):
        rows = pl.ds(pl.multiple_of(i * sub, sub), sub)
        key_value_block(x_ref[rows, :], (own_ref, oth_ref), bias_ref, extra_ref[rows, :], k1_ref, v1_ref, rows)

    copies_kv = [
        pltpu.make_async_copy(k1_ref, k_oth_hbm, out_sem.at[0]),
        pltpu.make_async_copy(v1_ref, v_oth_hbm, out_sem.at[1]),
    ]
    for copy in copies_kv:
        copy.start()

    def columns(step):
        return pl.ds(pl.multiple_of(lax.rem(step, parts) * chunk, chunk), chunk)

    def copy_out(step):
        slot = lax.rem(step, slots)
        return pltpu.make_async_copy(p_scr.at[slot], p_hbm.at[step // parts, :, columns(step)], sem.at[slot])

    def blocks(first, second):
        for part, ref in enumerate((first, second)):
            for u in range(half // sub):
                yield ref, slice(u * sub, (u + 1) * sub), slice(part * half + u * sub, part * half + (u + 1) * sub)

    def scores(step, s_ref, peak, keys, rows, to):
        s = dot(keys[step // parts, rows, :], qt_ref[step // parts, :, columns(step)], 1, 0)
        s_ref[to, :] = s
        return jnp.maximum(peak, jnp.max(s.reshape(sub // 8, 8, chunk), axis=0))

    def mix(step, s_ref, values, rows, to):
        p = jnp.exp2((s_ref[to, :] - row_scr[...]) * (LOG2E * HD**-0.5)).astype(BF)
        p_scr[lax.rem(step, slots), to, :] = p
        return dot(values[step // parts, rows, :], p, 0, 0)

    def run(step, s_ref, peak_ref, after, s_after, peak_after):
        row_scr[...] = jnp.max(peak_ref[...], axis=0, keepdims=True)

        @pl.when(step >= slots)
        def _():
            copy_out(step - slots).wait()

        peak = jnp.full((8, chunk), -jnp.inf, F32)
        acc = jnp.zeros((LANES, chunk), F32)
        for (k_ref, rows, to), (v_ref, _, _) in zip(blocks(k0_ref, k1_ref), blocks(v0_ref, v1_ref)):
            peak = scores(after, s_after, peak, k_ref, rows, to)
            acc = acc + mix(step, s_ref, v_ref, rows, to)
        peak_after[...] = peak
        acc_scr[...] = acc
        copy_out(step).start()
        inverse = 1.0 / acc_scr[HD : HD + 1, :]
        linv_ref[step // parts, :, columns(step)] = inverse
        ot_ref[step // parts, :, columns(step)] = acc_scr[:HD, :] * inverse

    for copy in copies_in(0):
        copy.wait()
    peak = jnp.full((8, chunk), -jnp.inf, F32)
    for k_ref, rows, to in blocks(k0_ref, k1_ref):
        peak = scores(0, s0_scr, peak, k_ref, rows, to)
    peak0_scr[...] = peak

    @pl.loop(0, steps // 2)
    def _(i):
        run(2 * i, s0_scr, peak0_scr, 2 * i + 1, s1_scr, peak1_scr)
        after = 2 * i + 2

        @pl.when((after < steps) & (lax.rem(after, parts) == 0))
        def _():
            for copy in copies_in(after // parts):
                copy.wait()

        run(2 * i + 1, s1_scr, peak1_scr, jnp.minimum(after, steps - 1), s0_scr, peak0_scr)

    for slot in range(slots):
        copy_out(steps - slots + slot).wait()
    for copy in copies_kv:
        copy.wait()


def attend(qt, k_own, v_own, x_oth, w_own, w_oth, bias, extra):
    heads, _, queries = qt.shape
    keys = 2 * queries
    sub, chunk, slots = 256, 512, 4
    per_head = jax.ShapeDtypeStruct(k_own.shape, BF)
    return pl.pallas_call(
        functools.partial(attend_kernel, sub, chunk),
        out_shape=(
            jax.ShapeDtypeStruct((heads, keys, queries), BF),
            jax.ShapeDtypeStruct((heads, HD, queries), F32),
            jax.ShapeDtypeStruct((heads, 1, queries), F32),
            per_head,
            per_head,
        ),
        in_specs=[HBM] * 3 + [VMEM] * 5,
        out_specs=(HBM, VMEM, VMEM, HBM, HBM),
        scratch_shapes=[
            pltpu.VMEM(qt.shape, BF),
            pltpu.VMEM(k_own.shape, BF),
            pltpu.VMEM(k_own.shape, BF),
            pltpu.VMEM(k_own.shape, BF),
            pltpu.VMEM(k_own.shape, BF),
            pltpu.VMEM((keys, chunk), F32),
            pltpu.VMEM((keys, chunk), F32),
            pltpu.VMEM((8, chunk), F32),
            pltpu.VMEM((8, chunk), F32),
            pltpu.VMEM((1, chunk), F32),
            pltpu.VMEM((LANES, chunk), F32),
            pltpu.VMEM((slots, keys, chunk), BF),
            pltpu.SemaphoreType.DMA((slots,)),
            pltpu.SemaphoreType.DMA((heads, 3)),
            pltpu.SemaphoreType.DMA((2,)),
        ],
        compiler_params=params(),
        cost_estimate=cost(heads * keys * queries * 512, 2 * heads * keys * queries),
        name="attend",
    )(qt, k_own, v_own, x_oth, w_own, w_oth, bias, extra)


def normalize(values):
    mean = jnp.mean(values, axis=-1, keepdims=True)
    centered = values - mean
    inverse = lax.rsqrt(jnp.mean(centered * centered, axis=-1, keepdims=True) + NORM_EPS)
    return centered * inverse, inverse


def norm_back(e, normed, inverse):
    return inverse * (
        e - jnp.mean(e, axis=-1, keepdims=True) - normed * jnp.mean(e * normed, axis=-1, keepdims=True)
    )


def middle_kernel(
    sub, x_ref, cot_ref, ot_ref, linv_ref, w_own_ref, w_oth_ref, vec_ref,
    act_ref, res_ref, dot_ref, dnat_ref, own_ref, oth_ref, small_ref,
    att_scr, w_out_ref, w_up_ref, w_down_ref, b_up_ref, gw_ref,
):
    block, width = x_ref.shape
    heads = width // HD
    shard = width // 2
    b_out, gain1, bias1, b_down, gain2, bias2 = (vec_ref[i : i + 1, :] for i in range(6))

    @pl.when(pl.program_id(0) == 0)
    def _():
        gw_ref[...] = jnp.zeros_like(gw_ref)
        small_ref[...] = jnp.zeros_like(small_ref)
        for side, ref in enumerate((w_own_ref, w_oth_ref)):
            mine = slice(side * shard, (side + 1) * shard)
            w_out_ref[mine, :] = ref[:shard, :]
            w_down_ref[mine, :] = ref[shard : 2 * shard, :]
            w_up_ref[:shard, mine] = ref[2 * shard : 3 * shard, :shard]
            w_up_ref[shard:, mine] = ref[2 * shard : 3 * shard, shard:]
            b_up_ref[:, mine] = ref[3 * shard : 3 * shard + 1, :shard].astype(F32)

    def col_sum(row, values):
        small_ref[row : row + 1, :] += jnp.sum(values, axis=0, keepdims=True)

    def chain(u):
        rows = slice(u * sub, (u + 1) * sub)
        for h in range(heads):
            att_scr[u, h * HD : (h + 1) * HD, :] = ot_ref[h, :, rows].astype(BF)
        branch = dot(att_scr[u], w_out_ref[...], 0, 0)
        yield
        n1, inv1 = normalize(x_ref[rows, :].astype(F32) + branch + b_out)
        first = n1 * gain1 + bias1
        first_low = first.astype(BF)
        yield
        pre = dot(first_low, w_up_ref[...], 1, 0) + b_up_ref[...]
        yield
        cdf = 0.5 * (1.0 + lax.erf(pre * 0.5**0.5))
        hidden = (pre * cdf).astype(BF)
        slope = cdf + pre * (0.3989422804014327 * jnp.exp(-0.5 * pre * pre))
        yield
        branch = dot(hidden, w_down_ref[...], 1, 0)
        yield
        n2, inv2 = normalize(first + branch + b_down)
        act_ref[rows, :] = (n2 * gain2 + bias2).astype(BF)
        cot = cot_ref[rows, :].astype(F32)
        two = norm_back(cot * gain2, n2, inv2)
        two_low = two.astype(BF)
        yield
        back = dot(two_low, w_down_ref[...], 1, 1)
        gw_ref[2] += dot(hidden, two_low, 0, 0)
        col_sum(3, two)
        col_sum(4, cot * n2)
        col_sum(5, cot)
        yield
        pre_grad = (back * slope).astype(BF)
        yield
        back = dot(pre_grad, w_up_ref[...], 1, 1)
        gw_ref[1] += dot(first_low, pre_grad, 0, 0)
        col_sum(6, pre_grad.astype(F32))
        yield
        one = two + back
        res = norm_back(one * gain1, n1, inv1)
        res_ref[rows, :] = res
        res_low = res.astype(BF)
        yield
        turned = dot(w_out_ref[...], res_low, 1, 1)
        gw_ref[0] += dot(att_scr[u], res_low, 1, 0)
        col_sum(1, one * n1)
        col_sum(2, one)
        col_sum(0, res)
        yield
        pick = lax.broadcasted_iota(jnp.int32, (HD, sub), 0)
        for h in range(heads):
            head = slice(h * HD, (h + 1) * HD)
            grad = (turned[head].astype(BF).astype(F32) * linv_ref[h, :, rows]).astype(BF)
            inner = -jnp.sum(grad.astype(F32) * ot_ref[h, :, rows], axis=0, keepdims=True)
            high = inner.astype(BF).astype(F32)
            dot_ref[h, :HD, rows] = grad
            dot_ref[h, HD:, rows] = jnp.where(pick == 0, high, jnp.where(pick == 1, inner - high, 0.0)).astype(BF)
            att_scr[u, head, :] = grad
        dnat_ref[rows, :] = att_scr[u].T
        yield

    for _ in zip(*(chain(u) for u in range(block // sub))):
        pass

    @pl.when(pl.program_id(0) == pl.num_programs(0) - 1)
    def _():
        for ref, mine in ((own_ref, slice(0, shard)), (oth_ref, slice(shard, width))):
            ref[:shard, :] = gw_ref[0, mine, :].astype(ref.dtype)
            ref[shard:width, :] = gw_ref[2, mine, :].astype(ref.dtype)
            ref[width:, :shard] = gw_ref[1, :shard, mine].astype(ref.dtype)
            ref[width:, shard:] = gw_ref[1, shard:, mine].astype(ref.dtype)


def middle(x, cot, ot, linv, w_own, w_oth, vectors):
    tokens, width = x.shape
    heads = width // HD
    block, sub = 512, 256
    whole = lambda *shape: pl.BlockSpec(shape, lambda i: (0,) * len(shape))
    rows = pl.BlockSpec((block, width), lambda i: (i, 0))
    columns = lambda n: pl.BlockSpec((heads, n, block), lambda i: (0, 0, i))
    square = pltpu.VMEM((width, width), BF)
    return pl.pallas_call(
        functools.partial(middle_kernel, sub),
        grid=(tokens // block,),
        out_shape=(
            jax.ShapeDtypeStruct((tokens, width), BF),
            jax.ShapeDtypeStruct((tokens, width), F32),
            jax.ShapeDtypeStruct((heads, LANES, tokens), BF),
            jax.ShapeDtypeStruct((tokens, width), BF),
            jax.ShapeDtypeStruct((3 * width // 2, width), F32),
            jax.ShapeDtypeStruct((3 * width // 2, width), BF),
            jax.ShapeDtypeStruct((8, width), F32),
        ),
        in_specs=[rows, rows, columns(HD), columns(1), whole(*w_own.shape), whole(*w_oth.shape), whole(*vectors.shape)],
        out_specs=(
            rows, rows, columns(LANES), rows,
            whole(3 * width // 2, width), whole(3 * width // 2, width), whole(8, width),
        ),
        scratch_shapes=[
            pltpu.VMEM((block // sub, width, sub), BF), square, square, square,
            pltpu.VMEM((1, width), F32), pltpu.VMEM((3, width, width), F32),
        ],
        compiler_params=params(),
        cost_estimate=cost(9 * tokens * width * width, 20 * tokens * width),
        name="middle",
    )(x, cot, ot, linv, w_own, w_oth, vectors)


def times_weights(grad, own_ref, oth_ref, third):
    shard = own_ref.shape[1] // 3
    mine = slice(third * shard, (third + 1) * shard)
    return dot(grad[:, :shard], own_ref[:, mine], 1, 1) + dot(grad[:, shard:], oth_ref[:, mine], 1, 1)


def backward_kernel(sub, count, part, *refs):
    if part:
        (p_hbm, dot_hbm, dnat_hbm, q_hbm, k_hbm, v_hbm, x_hbm, own_hbm, oth_hbm,
         dq_ref, dx_ref, gw_ref,
         dot_ref, dnat_ref, q_ref, k_ref, v_ref, x_ref, own_ref, oth_ref,
         dk_ref, dv_ref, acc_scr, p_scr, sem, pair_sem, last_sem) = refs
        more = ((own_hbm, own_ref), (oth_hbm, oth_ref))
    else:
        (p_hbm, dot_hbm, dnat_hbm, q_hbm, k_hbm, v_hbm, x_hbm, dq_hbm, gw_hbm,
         pack_ref, bias_ref, dq_out, dk_ref, dv_ref,
         dot_ref, dnat_ref, q_ref, k_ref, v_ref, x_ref, before_ref, gw_ref, dq_ref,
         acc_scr, p_scr, sem, pair_sem, last_sem) = refs
        more = ((dq_hbm, before_ref), (gw_hbm, gw_ref))
    heads, _, queries = dot_ref.shape
    keys = k_ref.shape[1]
    width = heads * HD
    shard = width // 2
    block = sub * count
    blocks = keys // block
    slots = p_scr.shape[0]
    total = heads // 2 * blocks
    low = lax.broadcasted_iota(jnp.int32, (sub, LANES), 1) < HD

    def copy_in(step):
        rows = pl.ds(pl.multiple_of(part * keys + lax.rem(step, blocks) * block, block), block)
        pair = pl.ds(step // blocks * 2, 2)
        slot = lax.rem(step, slots)
        return pltpu.make_async_copy(p_hbm.at[pair, rows, :], p_scr.at[slot], sem.at[slot])

    def pair_copies(p):
        pair = pl.ds(2 * p, 2)
        lanes = pl.ds(pl.multiple_of(p * LANES, LANES), LANES)
        by_head = ((dot_hbm, dot_ref), (k_hbm, k_ref), (v_hbm, v_ref))
        by_lane = ((dnat_hbm, dnat_ref), (q_hbm, q_ref))
        return [
            pltpu.make_async_copy(src.at[pair], dst.at[pair], pair_sem.at[p, n]) for n, (src, dst) in enumerate(by_head)
        ] + [
            pltpu.make_async_copy(src.at[:, lanes], dst.at[:, lanes], pair_sem.at[p, 3 + n])
            for n, (src, dst) in enumerate(by_lane)
        ]

    last = ((x_hbm, x_ref),) + more
    last_copies = [pltpu.make_async_copy(src, dst, last_sem.at[n]) for n, (src, dst) in enumerate(last)]

    for copy in pair_copies(0):
        copy.start()
    for step in range(slots - 1):
        copy_in(step).start()
    for p in range(1, heads // 2):
        for copy in pair_copies(p):
            copy.start()
    for copy in last_copies:
        copy.start()

    @pl.loop(0, heads // 2)
    def _(p):
        lanes = pl.ds(pl.multiple_of(p * LANES, LANES), LANES)
        for copy in pair_copies(p):
            copy.wait()
        acc_scr[...] = jnp.zeros_like(acc_scr)

        @pl.loop(0, blocks)
        def _(j):
            step = p * blocks + j
            slot = lax.rem(step, slots)
            copy_in(step).wait()

            @pl.when(step + slots - 1 < total)
            def _():
                copy_in(step + slots - 1).start()

            acc = [0.0, 0.0]
            for u in range(count):
                here = pl.ds(pl.multiple_of(j * block + u * sub, sub), sub)
                dks, dvs = [], []
                for side in range(2):
                    h = 2 * p + side
                    prob = p_scr[slot, side, u * sub : (u + 1) * sub, :]
                    slope = dot(v_ref[h, here, :], dot_ref[h], 1, 0)
                    dvs.append(dot(prob, dnat_ref[:, lanes], 1, 0))
                    ds = (prob.astype(F32) * slope).astype(BF)
                    dks.append(dot(ds, q_ref[:, lanes], 1, 0))
                    acc[side] = acc[side] + dot(k_ref[h, here, :], ds, 0, 0)
                dk_ref[here, lanes] = (jnp.where(low, dks[0], dks[1]) * HD**-0.5).astype(BF)
                dv_ref[here, lanes] = jnp.where(low, dvs[0], dvs[1]).astype(BF)
            for side in range(2):
                acc_scr[side] += acc[side]

        for side in range(2):
            dq_ref[pl.ds(pl.multiple_of((2 * p + side) * HD, HD), HD), :] = acc_scr[side, :HD, :]

    for copy in last_copies:
        copy.wait()
    if part:
        gw_ref[...] = jnp.zeros_like(gw_ref)
    else:
        bias_ref[...] = jnp.zeros_like(bias_ref)

    @pl.loop(0, keys // sub)
    def _(i):
        rows = pl.ds(pl.multiple_of(i * sub, sub), sub)
        x, dk, dv = x_ref[rows, :], dk_ref[rows, :], dv_ref[rows, :]
        gw_ref[0] += dot(x, dk, 0, 0)
        gw_ref[1] += dot(x, dv, 0, 0)
        if part:
            dx_ref[rows, :] = (times_weights(dk, own_ref, oth_ref, 1) + times_weights(dv, own_ref, oth_ref, 2)).astype(BF)
            gw_ref[2, 0:1, :] += jnp.sum(dv.astype(F32), axis=0, keepdims=True)
        else:
            dq = ((before_ref[:, rows] + dq_ref[:, rows]) * HD**-0.5).astype(BF).T
            dq_out[rows, :] = dq
            gw_ref[2] = jnp.where(i == 0, 0.0, gw_ref[2]) + dot(x, dq, 0, 0)
            bias_ref[0:1, :] += jnp.sum(dq.astype(F32), axis=0, keepdims=True)
            bias_ref[1:2, :] += jnp.sum(dv.astype(F32), axis=0, keepdims=True)

    if not part:
        for cut in range(2):
            for third in range(3):
                row = third * shard + cut * (shard // 2)
                core, at = row // (3 * shard // 2), row % (3 * shard // 2)
                to = slice(at, at + shard // 2)
                grad = gw_ref.at[(2, 0, 1)[third]]
                for side in range(2):
                    mine = slice(side * shard, (side + 1) * shard)
                    for place, start in ((slice(0, shard), 0), (slice(shard, width), shard)):
                        top = slice(start + cut * (shard // 2), start + (cut + 1) * (shard // 2))
                        pack_ref[core, side, to, place] = grad[top, mine].astype(BF)


def attend_backward(part, probs, dot_turned, dnat, q, k, v, x, *more):
    heads, keys, queries = probs.shape
    width = heads * HD
    sub, count, slots = 256, 2, 4
    sums = jax.ShapeDtypeStruct((3, width, width), F32)
    turned = jax.ShapeDtypeStruct((width, queries), F32)
    grad = jax.ShapeDtypeStruct((queries, width), BF)
    inputs = (dot_turned, dnat, q, k, v, x) + more
    held = [pltpu.VMEM(a.shape, a.dtype) for a in inputs]
    if part:
        out_shape = (turned, grad, sums)
        held += [pltpu.VMEM(grad.shape, BF)] * 2
    else:
        out_shape = (
            jax.ShapeDtypeStruct((2, 2, 3 * width // 4, width), BF),
            jax.ShapeDtypeStruct((2, width), F32),
            grad,
            grad,
            grad,
        )
        held = held[:6] + [pltpu.VMEM(turned.shape, F32), pltpu.VMEM(sums.shape, F32), pltpu.VMEM(turned.shape, F32)]
    return pl.pallas_call(
        functools.partial(backward_kernel, sub, count, part),
        out_shape=out_shape,
        in_specs=[HBM] * (1 + len(inputs)),
        out_specs=(VMEM,) * len(out_shape),
        scratch_shapes=held
        + [
            pltpu.VMEM((2, LANES, queries), F32),
            pltpu.VMEM((slots, 2, sub * count, queries), BF),
            pltpu.SemaphoreType.DMA((slots,)),
            pltpu.SemaphoreType.DMA((heads // 2, 5)),
            pltpu.SemaphoreType.DMA((1 + len(more),)),
        ],
        compiler_params=params(),
        cost_estimate=cost(heads * keys * queries * 512, heads * keys * queries),
        name="attend_back_own" if not part else "attend_back_other",
    )(probs, *inputs)


def input_kernel(res_ref, got_ref, dq_ref, dk_ref, dv_ref, own_ref, oth_ref, dx_ref):
    dx = res_ref[...] + got_ref[...].astype(F32)
    for third, ref in enumerate((dq_ref, dk_ref, dv_ref)):
        dx = dx + times_weights(ref[...], own_ref, oth_ref, third)
    dx_ref[...] = dx


def input_gradient(res, got, dq, dk, dv, w_own, w_oth):
    tokens, width = res.shape
    rows = pl.BlockSpec((256, width), lambda i: (i, 0))
    whole = pl.BlockSpec(w_own.shape, lambda i: (0, 0))
    return pl.pallas_call(
        input_kernel,
        grid=(tokens // 256,),
        out_shape=jax.ShapeDtypeStruct((tokens, width), F32),
        in_specs=[rows] * 5 + [whole] * 2,
        out_specs=rows,
        compiler_params=params(),
        cost_estimate=cost(3 * tokens * width * width, 16 * tokens * width),
        name="input_gradient",
    )(res, got, dq, dk, dv, w_own, w_oth)


def two_halves(values):
    high = values.astype(BF)
    return jnp.concatenate([high, (values - high.astype(F32)).astype(BF)], axis=0)


def one_value(halves):
    return halves[:8].astype(F32) + halves[8:].astype(F32)


def take(values, which):
    return lax.dynamic_index_in_dim(values, which, 0, False)


def in_order(mine, theirs, which):
    return jnp.concatenate([jnp.where(which == 0, mine, theirs), jnp.where(which == 0, theirs, mine)])


def sum_gradients(packed, small_own, small_oth, mid, devices):
    index = lax.axis_index("dp")
    core, near = lax.rem(index, 2), lax.rem(index // 2, 2)
    rows = packed.shape[2]

    def across(values, bit):
        return lax.ppermute(values, "dp", [(i, i ^ bit) for i in range(devices)])

    own_two, oth_two = two_halves(small_own), two_halves(small_oth)
    sent = jnp.concatenate([take(packed, 1 - core).reshape(2 * rows, -1), own_two, oth_two])
    got = across(sent, 1)
    kept = take(packed, core).reshape(2 * rows, -1).astype(F32) + got[: 2 * rows].astype(F32)
    small_own = one_value(own_two) + one_value(got[2 * rows : 2 * rows + 16])
    small_oth = one_value(oth_two) + one_value(got[2 * rows + 16 :])
    halves = mid.reshape(2, rows // 2, -1)
    mid = take(halves, core) + across(take(halves, 1 - core).astype(BF), 1).astype(F32)

    own_two, oth_two = two_halves(small_own), two_halves(small_oth)
    got = lax.ppermute(jnp.concatenate([kept[rows:].astype(BF), oth_two]), "tensor", [(0, 1), (1, 0)])
    kept = kept[:rows] + got[:rows].astype(F32)
    small = one_value(own_two) + one_value(got[rows:])

    halves = kept.reshape(2, rows // 2, -1)
    two = two_halves(small)
    got = across(jnp.concatenate([take(halves, 1 - near).astype(BF), two]), 2)
    kept = take(halves, near) + got[: rows // 2].astype(F32)
    small = one_value(two) + one_value(got[rows // 2 :])

    bit = 4
    while bit < devices:
        low = mid.astype(BF)
        mid = low.astype(F32) + across(low, bit).astype(F32)
        sent = jnp.concatenate([kept.astype(BF), two_halves(small)])
        got = across(sent, bit)
        kept = sent[: rows // 2].astype(F32) + got[: rows // 2].astype(F32)
        small = one_value(sent[rows // 2 :]) + one_value(got[rows // 2 :])
        bit *= 2

    mid = mid.astype(BF)
    mid = in_order(mid, across(mid, 1), core)
    mid = in_order(mid, across(mid, 2), near)
    kept = kept.astype(BF)
    kept = in_order(kept, across(kept, 2), near)
    kept = in_order(kept, across(kept, 1), core)
    return kept.astype(F32), small, mid.astype(F32)


def mask_columns(known, lengths):
    positions = jnp.arange(known.shape[0], dtype=jnp.int32)
    ends = jnp.cumsum(lengths)
    starts = ends - lengths
    inside = (positions[:, None] >= starts[None, :]) & (positions[:, None] < ends[None, :])
    opening = jnp.any((positions[:, None] == starts[None, :]) & (lengths[None, :] > 0), axis=1)
    dead = ~((known > 0) | opening)
    slots = lengths.shape[0]
    keys = jnp.concatenate([inside, dead[:, None]], axis=1).astype(F32)
    keys = jnp.pad(keys, ((0, 0), (HD, LANES - HD - slots - 1))).astype(BF)
    queries = jnp.where(jnp.pad(inside, ((0, 0), (0, 1))), 0.0, -MASK_BIG)
    queries = jnp.pad(queries, ((0, 0), (0, HD - slots - 1))).T.astype(BF)
    return keys, queries


def local(
    devices, layer_input, gene_known, cell_genes, w_qkv, bias_qv, w_out, b_out, ln1_gain, ln1_bias,
    w_up, b_up, w_down, b_down, ln2_gain, ln2_bias, cotangent,
):
    tokens, width = layer_input.shape
    shard = w_qkv.shape[2]
    side, index = lax.axis_index("tensor"), lax.axis_index("dp")
    core, near = lax.rem(index, 2), lax.rem(index // 2, 2)

    def swapped(values):
        return lax.ppermute(values, "tensor", [(0, 1), (1, 0)])

    def across(values, bit):
        return lax.ppermute(values, "dp", [(i, i ^ bit) for i in range(devices)])

    w_own = w_qkv.reshape(width, 3 * shard)
    quarter = width // 4
    bias_row = jnp.pad(bias_qv.reshape(1, 2 * shard), ((0, 15), (0, shard)))
    sent = jnp.concatenate([lax.dynamic_slice_in_dim(w_own, (2 * core + near) * quarter, quarter, 0), bias_row])
    got = swapped(sent)
    x_oth = swapped(layer_input)
    piece = got[:quarter]
    piece = in_order(piece, across(piece, 2), near)
    w_oth = in_order(piece, across(piece, 1), core)
    bias_oth = got[quarter, : 2 * shard].reshape(2, shard)
    bias = jnp.concatenate([bias_qv, bias_oth], axis=1).astype(F32)

    key_cols, query_rows = mask_columns(gene_known, cell_genes[0])
    key_own = lax.dynamic_slice_in_dim(key_cols, side * tokens, tokens, 0)
    key_oth = lax.dynamic_slice_in_dim(key_cols, (1 - side) * tokens, tokens, 0)
    query_own = lax.dynamic_slice_in_dim(query_rows, side * tokens, tokens, 1)
    b_up_row = jnp.pad(b_up[None], ((0, 15), (0, shard)))
    mid_w = jnp.concatenate([w_out, w_down, jnp.concatenate([w_up[:shard], w_up[shard:]], axis=1), b_up_row])
    vectors = jnp.stack([b_out, ln1_gain, ln1_bias, b_down, ln2_gain, ln2_bias, b_out, b_out])

    k_own, v_own, qt, q = project(layer_input, w_own, w_oth, bias, key_own, query_own)
    x_oth, k_own, mid_w = lax.optimization_barrier((x_oth, k_own, mid_w))
    mid_w_oth = swapped(mid_w)
    probs, ot, linv, k_oth, v_oth = attend(qt, k_own, v_own, x_oth, w_own, w_oth, bias, key_oth)
    activations, res, dot_turned, dnat, mid_own, mid_oth, small = middle(
        layer_input, cotangent, ot, linv, mid_w, mid_w_oth, vectors
    )
    mid_got = swapped(mid_oth)
    dq, dx_oth, sums = attend_backward(1, probs, dot_turned, dnat, q, k_oth, v_oth, x_oth, w_own, w_oth)
    mid_got, dq = lax.optimization_barrier((mid_got, dq))
    mid = (mid_own + mid_got.astype(F32)).reshape(2, 3 * shard // 2, width)
    mid_got = across(take(mid, 1 - near).astype(BF), 2)
    dx_got = swapped(dx_oth)
    packed, bias_grad, dq, dk, dv = attend_backward(
        0, probs, dot_turned, dnat, q, k_own, v_own, layer_input, dq, sums
    )
    mid_got, dx_got, packed = lax.optimization_barrier((mid_got, dx_got, packed))
    mid = take(mid, near) + mid_got.astype(F32)
    input_grad = input_gradient(res, dx_got, dq, dk, dv, w_own, w_oth)
    values_grad = bias_grad[1:2] + sums[2, 0:1]

    def small_rows(mine):
        b_up_row = jnp.pad(small[6:7, mine], ((0, 0), (0, shard)))
        bias_row = jnp.concatenate([bias_grad[0:1, mine], values_grad[:, mine]], axis=1)
        return jnp.concatenate([small[:6], b_up_row, bias_row])

    qkv, small, mid = sum_gradients(
        packed, small_rows(slice(0, shard)), small_rows(slice(shard, width)), mid, devices
    )
    qkv_g = qkv.reshape(3, shard, 2, shard).transpose(2, 1, 0, 3).reshape(width, 3, shard)
    up_g = jnp.concatenate([mid[width:, :shard], mid[width:, shard:]])
    return (
        activations, input_grad, qkv_g, small[7].reshape(2, shard), mid[:shard], small[0], small[1], small[2],
        up_g, small[6, :shard], mid[shard:width], small[3], small[4], small[5],
    )


def solution(mesh):
    placed = (
        P(("dp", "tensor"), None),
        P("dp"),
        P("dp", None),
        P(None, None, "tensor"),
        P(None, "tensor"),
        P("tensor", None),
        P(),
        P(),
        P(),
        P(None, "tensor"),
        P("tensor"),
        P("tensor", None),
        P(),
        P(),
        P(),
        P(("dp", "tensor"), None),
    )
    return jax.shard_map(
        functools.partial(local, mesh.shape["dp"]),
        mesh=mesh,
        in_specs=placed,
        out_specs=(
            P(("dp", "tensor"), None),
            P(("dp", "tensor"), None),
            P(None, None, "tensor"),
            P(None, "tensor"),
            P("tensor", None),
            P(),
            P(),
            P(),
            P(None, "tensor"),
            P("tensor"),
            P("tensor", None),
            P(),
            P(),
            P(),
        ),
        check_vma=False,
    )
```

time: 360 us -> 191 us (0.53)
  blocking collectives: 85.2 us -> 0 us
  Pallas kernels: 144 us -> 103 us
  waiting for transfers between devices: 59.2 us -> 45.7 us
  between operations: 14.3 us -> 1.34 us
  other arithmetic: 18.4 us -> 7.21 us
  local copies, waits for them, and re-layouts: 20.5 us -> 12 us
  starting transfers between devices: 16.2 us -> 21 us
    psum x2 -> x0, blocking collectives: 85.2 us -> none  [the longest x1 53.7 us: local(): small_g = lax.psum(small[:6], ('dp', 'tensor'))]
    pallas_call x7 -> x6, Pallas kernels: 144 us -> 103 us  [the longest x2 52.1 us: attend_backward(): pl.pallas_call(functools.partial(backward_kernel, sub, count, part), out_...]
    psum x1 -> x0, waiting for transfers between devices: 13 us -> none  [local(): qkv_g, bias_g, out_g, up_g, b_up_g, down_g = lax.psum(got, 'dp')]
    add x6, other arithmetic: 6.99 us -> 1.59 us  [the longest x1 0.84 us: local(): values_grad = bias_grad[1:2] + sums[2, 0:1]]
    unnamed x39 -> x43, local copies, waits for them, and re-layouts: 7.99 us -> 3.06 us
    ppermute x14 -> x20, starting transfers between devices: 16.1 us -> 21 us  [the longest x14 13.4 us: across(): return lax.ppermute(values, 'dp', [(i, i ^ bit) for i in range(devices)])]
    ppermute x14 -> x20, waiting for transfers between devices: 46.2 us -> 45.7 us  [the longest x14 33.5 us: across(): return lax.ppermute(values, 'dp', [(i, i ^ bit) for i in range(devices)])]
  transfers between devices with their start and end apart: 15 -> 20, of which waited for: 6 -> 12; matrix products, arithmetic and copies ran while one was open for 8% -> 7% of each run, Pallas kernels for 20% -> 47%
where the time goes in v2:
time: 191 us
  Pallas kernels  103 us (54%)
  waiting for transfers between devices  45.7 us (24%)
  starting transfers between devices  21 us (11%)
  local copies, waits for them, and re-layouts  12 us (6%)
  other arithmetic  7.21 us (4%)
    pallas_call x2, Pallas kernels, attend_backward(): pl.pallas_call(functools.partial(backward_kernel, sub, count, part), out_...  52.1 us
    ppermute x14, waiting for transfers between devices, across(): return lax.ppermute(values, 'dp', [(i, i ^ bit) for i in range(devices)])  33.5 us
    pallas_call x1, Pallas kernels, attend(): pl.pallas_call(functools.partial(attend_kernel, sub, chunk), out_shape=(j...  25 us
    pallas_call x1, Pallas kernels, middle(): pl.pallas_call(functools.partial(middle_kernel, sub), grid=(tokens // blo...  13.6 us
    ppermute x14, starting transfers between devices, across(): return lax.ppermute(values, 'dp', [(i, i ^ bit) for i in range(devices)])  13.4 us
    ppermute x5, waiting for transfers between devices, swapped(): return lax.ppermute(values, 'tensor', [(0, 1), (1, 0)])  10.1 us
    ppermute x5, starting transfers between devices, swapped(): return lax.ppermute(values, 'tensor', [(0, 1), (1, 0)])  7 us
    pallas_call x1, Pallas kernels, project(): pl.pallas_call(project_kernel, grid=(tokens // block,), out_shape=(jax.Sh...  6.46 us
  transfers between devices with their start and end apart: 20, of which 12 were waited for; matrix products, arithmetic and copies ran while one was open for 7% of the time, Pallas kernels for 47%

profile of v2, /device:TPU:0, one launch (start us, length us, event | category | flops | bytes accessed | tf_op | source)
XLA Modules:
  0.0 190.7 jit_solution(12371684892739160182)
XLA Ops:
  0.7 1.4 copy.42
  2.5 3.0 %collective-permute-start = (bf16[144,768]{1,0:T(8,128)(2,1)S(1)}, bf16[144,768]{1,0:T(8,128)(2,1)S(1)}, u32[]{:S(2)}, u32[]{:S(2)}) collective-permute-start(bf16[144,768]{1,0:T(8,128)(2,1)S(1)} %fusion.6), channel_id=1, source_target_pairs={{0,1},{1,0},{2,3},{3,2},{4,5},{5,4},{6,7},{7,6},{8,9},{9,8},{10,11... | collective-permute-start | bytes 663560 | tf_op jit(solution)/shard_map/ppermute | solution.py:679
  6.0 0.5 copy.44
  6.8 0.8 constant_dynamic-slice_fusion.2
  7.8 4.0 %collective-permute-done = bf16[144,768]{1,0:T(8,128)(2,1)S(1)} collective-permute-done((bf16[144,768]{1,0:T(8,128)(2,1)S(1)}, bf16[144,768]{1,0:T(8,128)(2,1)S(1)}, u32[]{:S(2)}, u32[]{:S(2)}) %collective-permute-start) | collective-permute-done | bytes 221216 | tf_op jit(solution)/shard_map/ppermute | solution.py:679
  11.8 2.1 %collective-permute-start.1 = (bf16[128,768]{1,0:T(8,128)(2,1)S(1)}, bf16[128,768]{1,0:T(8,128)(2,1)S(1)}, u32[]{:S(2)}, u32[]{:S(2)}) collective-permute-start(bf16[128,768]{1,0:T(8,128)(2,1)S(1)} %slice.196), channel_id=1, source_target_pairs={{0,4},{2,6},{4,0},{6,2},{8,12},{10,14},{12,8},{14,10},{16,20},{18,... | collective-permute-start | bytes 589832 | tf_op jit(solution)/shard_map/ppermute | solution.py:682
  13.9 3.6 %collective-permute-done.1 = bf16[128,768]{1,0:T(8,128)(2,1)S(1)} collective-permute-done((bf16[128,768]{1,0:T(8,128)(2,1)S(1)}, bf16[128,768]{1,0:T(8,128)(2,1)S(1)}, u32[]{:S(2)}, u32[]{:S(2)}) %collective-permute-start.1) | collective-permute-done | bytes 196640 | tf_op jit(solution)/shard_map/ppermute | solution.py:682
  17.7 0.7 fusion.9.extra_q_ref
  18.4 0.6 stack.29.vec_ref
  19.2 0.7 maximum_convert_fusion.5.bias_ref
  20.0 1.0 pad_maximum_fusion.oth_ref.refs_8_
  21.0 6.5 %project.1 = (bf16[8,1024,128]{2,1,0:T(8,128)(2,1)}, bf16[8,1024,128]{2,1,0:T(8,128)(2,1)}, bf16[8,128,1024]{2,1,0:T(8,128)(2,1)}, bf16[1024,512]{1,0:T(8,128)(2,1)}) custom-call(bf16[1024,512]{1,0:T(8,128)(2,1)} %refs_6_.1, bf16[512,768]{1,0:T(8,128)(2,1)} %copy-done, bf16[512,768]{1,0:T(8,128)(2,1)} %pad_maximum_fusion.oth_ref.refs_8_, ...), custom_call_target="tpu_custom_call" | custom-call | flops 1610612736 | bytes 6291456 | tf_op jit(solution)/shard_map/project/pallas_call | solution.py:81
  27.4 6.1 %collective-permute-done.3.x_ref.refs_6_ = bf16[1024,512]{1,0:T(8,128)(2,1)} collective-permute-done((bf16[1024,512]{1,0:T(8,128)(2,1)}, bf16[1024,512]{1,0:T(8,128)(2,1)}, u32[]{:S(2)}, u32[]{:S(2)}) %collective-permute-start.3) | collective-permute-done | bytes 1048608 | tf_op jit(solution)/shard_map/ppermute | solution.py:679
  33.5 1.7 collective-permute-start.4
  35.3 25.0 %attend.1 = (bf16[8,2048,1024]{2,1,0:T(8,128)(2,1)}, f32[8,64,1024]{2,1,0:T(8,128)}, f32[8,1,1024]{2,1,0:T(1,128)}, bf16[8,1024,128]{2,1,0:T(8,128)(2,1)}, bf16[8,1024,128]{2,1,0:T(8,128)(2,1)}) custom-call(bf16[8,128,1024]{2,1,0:T(8,128)(2,1)} %get-tuple-element.46.qt_hbm, bf16[8,1024,128]{2,1,0:T(8,128)(2,1)} %get-tuple-element.48.k_hbm.refs_4_, ...), custom_call_target="tpu_custom_call" | custom-call | flops 17179869184 | bytes 33554432 | tf_op jit(solution)/shard_map/attend/pallas_call | solution.py:215
  60.3 0.9 copy-done.17
  61.2 13.6 %middle.1 = (bf16[1024,512]{1,0:T(8,128)(2,1)}, f32[1024,512]{1,0:T(8,128)}, bf16[8,128,1024]{2,1,0:T(8,128)(2,1)}, bf16[1024,512]{1,0:T(8,128)(2,1)}, f32[768,5...) custom-call(bf16[1024,512]{1,0:T(8,128)(2,1)} %refs_6_.1, bf16[1024,512]{1,0:T(8,128)(2,1)} %cot_ref.1, ...), custom_call_target="tpu_custom_call" | custom-call | flops 4831838208 | bytes 10485760 | tf_op jit(solution)/shard_map/middle/pallas_call | solution.py:366
  75.2 26.6 %attend_back_other.1 = (f32[512,1024]{1,0:T(8,128)}, bf16[1024,512]{1,0:T(8,128)(2,1)}, f32[3,512,512]{2,1,0:T(8,128)}) custom-call(bf16[8,2048,1024]{2,1,0:T(8,128)(2,1)} %get-tuple-element.58.refs_0_, bf16[8,128,1024]{2,1,0:T(8,128)(2,1)} %get-tuple-element.59.refs_1_, bf16[1024,512]{1,0:T(8,128)(2,1)} %get-tuple-element.60.refs_2_, ...), custom_call_target="tpu_custom_call" | custom-call | flops 17179869184 | bytes 16777216 | tf_op jit(solution)/shard_map/attend_back_other/pallas_call | solution.py:548
  101.9 1.8 collective-permute-start.7
  104.0 1.6 collective-permute-start.6
  105.6 25.4 %attend_back_own.1 = (bf16[2,2,384,512]{3,2,1,0:T(8,128)(2,1)}, f32[2,512]{1,0:T(2,128)}, bf16[1024,512]{1,0:T(8,128)(2,1)}, bf16[1024,512]{1,0:T(8,128)(2,1)}, bf16[1024,512]{1,0:T(8,128)(2,1)}) custom-call(bf16[8,2048,1024]{2,1,0:T(8,128)(2,1)} %get-tuple-element.58.refs_0_, bf16[8,128,1024]{2,1,0:T(8,128)(2,1)} %get-tuple-element.59.refs_1_, ...), custom_call_target="tpu_custom_call" | custom-call | flops 17179869184 | bytes 16777216 | tf_op jit(solution)/shard_map/attend_back_own/pallas_call | solution.py:548
  131.0 0.8 bitcast_add_fusion.3
  131.8 0.7 fusion.39
  132.9 0.6 copy-done.3
  134.3 1.6 collective-permute-start.16
  135.9 5.4 %collective-permute-done.16 = bf16[192,512]{1,0:T(8,128)(2,1)S(1)} collective-permute-done((bf16[192,512]{1,0:T(8,128)(2,1)S(1)}, bf16[192,512]{1,0:T(8,128)(2,1)S(1)}, u32[]{:S(2)}, u32[]{:S(2)}) %collective-permute-start.16) | collective-permute-done | bytes 196640 | tf_op jit(solution)/shard_map/ppermute | solution.py:613
  141.3 2.6 %collective-permute-start.17 = (bf16[192,512]{1,0:T(8,128)(2,1)S(1)}, bf16[192,512]{1,0:T(8,128)(2,1)S(1)}, u32[]{:S(2)}, u32[]{:S(2)}) collective-permute-start(bf16[192,512]{1,0:T(8,128)(2,1)S(1)} %add_convert_fusion.1), channel_id=1, source_target_pairs={{0,16},{2,18},{4,20},{6,22},{8,24},{10,26},{12,28},{14,30},{16,0},... | collective-permute-start | bytes 589832 | tf_op jit(solution)/shard_map/ppermute | solution.py:613
  144.4 0.6 collective-permute-start.9
  145.0 6.3 %input_gradient.1 = f32[1024,512]{1,0:T(8,128)} custom-call(f32[1024,512]{1,0:T(8,128)} %get-tuple-element.55.res_ref, bf16[1024,512]{1,0:T(8,128)(2,1)} %copy-done.3, bf16[1024,512]{1,0:T(8,128)(2,1)} %get-tuple-element.71.dq_ref, bf16[1024,512]{1,0:T(8,128)(2,1)} %get-tuple-element.72.dk_ref, bf16[1024,512]{1,0:T(8,128)(2,1)} %get-tuple-element.73.dv_ref, ...), custom_call_target="tpu_custom_call" | custom-call | flops 1610612736 | bytes 8388608 | tf_op jit(solution)/shard_map/input_gradient/pallas_call | solution.py:578
  151.3 1.3 collective-permute-done.17
  152.8 2.1 %collective-permute-done.9 = bf16[400,512]{1,0:T(8,128)(2,1)S(1)} collective-permute-done((bf16[400,512]{1,0:T(8,128)(2,1)S(1)}, bf16[400,512]{1,0:T(8,128)(2,1)S(1)}, u32[]{:S(2)}, u32[]{:S(2)}) %collective-permute-start.9) | collective-permute-done | bytes 409632 | tf_op jit(solution)/shard_map/ppermute | solution.py:625
  155.1 0.6 collective-permute-start.10
  155.7 1.6 collective-permute-start.19
  157.3 6.0 %collective-permute-done.10 = bf16[208,512]{1,0:T(8,128)(2,1)S(1)} collective-permute-done((bf16[208,512]{1,0:T(8,128)(2,1)S(1)}, bf16[208,512]{1,0:T(8,128)(2,1)S(1)}, u32[]{:S(2)}, u32[]{:S(2)}) %collective-permute-start.10) | collective-permute-done | bytes 213024 | tf_op jit(solution)/shard_map/ppermute | solution.py:613
  163.4 1.6 collective-permute-start.11
  165.1 4.1 %collective-permute-done.19 = bf16[384,512]{1,0:T(8,128)(2,1)S(1)} collective-permute-done((bf16[384,512]{1,0:T(8,128)(2,1)S(1)}, bf16[384,512]{1,0:T(8,128)(2,1)S(1)}, u32[]{:S(2)}, u32[]{:S(2)}) %collective-permute-start.19) | collective-permute-done | bytes 393248 | tf_op jit(solution)/shard_map/ppermute | solution.py:613
  169.4 0.8 collective-permute-start.12
  170.4 0.8 slice.220
  171.2 0.9 maximum_convert_fusion.2
  172.1 8.2 %collective-permute-done.12 = bf16[208,512]{1,0:T(8,128)(2,1)S(1)} collective-permute-done((bf16[208,512]{1,0:T(8,128)(2,1)S(1)}, bf16[208,512]{1,0:T(8,128)(2,1)S(1)}, u32[]{:S(2)}, u32[]{:S(2)}) %collective-permute-start.12) | collective-permute-done | bytes 213024 | tf_op jit(solution)/shard_map/ppermute | solution.py:613
  180.4 0.6 collective-permute-start.13
  181.0 0.8 pad_maximum_fusion.1
  181.8 4.3 %collective-permute-done.13 = bf16[192,512]{1,0:T(8,128)(2,1)S(1)} collective-permute-done((bf16[192,512]{1,0:T(8,128)(2,1)S(1)}, bf16[192,512]{1,0:T(8,128)(2,1)S(1)}, u32[]{:S(2)}, u32[]{:S(2)}) %collective-permute-start.13) | collective-permute-done | bytes 196640 | tf_op jit(solution)/shard_map/ppermute | solution.py:613
  186.3 0.6 slice.224
  186.9 0.6 fusion.37
  187.5 0.6 reshape_squeeze.7
  188.4 1.0 reshape.89
  189.4 1.3 copy.49
  (116 shorter events, 5.2 us)
Async XLA Ops:
  0.7 1.8 copy-start.11
  2.1 3.5 %copy-start.18 = (s32[1,4]{1,0:T(1,128)S(1)}, s32[1,4]{1,0:T(1,128)}, u32[]{:S(2)}) copy-start(s32[1,4]{1,0:T(1,128)} %param.18) | copy-start | bytes 52
  2.1 3.8 %copy-start.10 = (s32[2048]{0:T(1024)S(1)}, s32[2048]{0:T(1024)}, u32[]{:S(2)}) copy-start(s32[2048]{0:T(1024)} %param.17) | copy-start | bytes 24580
  2.4 5.4 %copy-start = (bf16[512,768]{1,0:T(8,128)(2,1)}, bf16[512,768]{1,0:T(8,128)(2,1)S(1)}, u32[]{:S(2)}) copy-start(bf16[512,768]{1,0:T(8,128)(2,1)S(1)} %copy.45.own_ref.refs_7_) | copy-start | bytes 2359300
  2.4 5.3 %copy-start.6 = (bf16[512,256]{1,0:T(8,128)(2,1)S(1)}, bf16[512,256]{1,0:T(8,128)(2,1)}, u32[]{:S(2)}) copy-start(bf16[512,256]{1,0:T(8,128)(2,1)} %param.25) | copy-start | bytes 786436
  2.5 9.3 %collective-permute-start = (bf16[144,768]{1,0:T(8,128)(2,1)S(1)}, bf16[144,768]{1,0:T(8,128)(2,1)S(1)}, u32[]{:S(2)}, u32[]{:S(2)}) collective-permute-start(bf16[144,768]{1,0:T(8,128)(2,1)S(1)} %fusion.6), channel_id=1, source_target_pairs={{0,1},{1,0},{2,3},{3,2},{4,5},{5,4},{6,7},{7,6},{8,9},{9,8},{10,11... | collective-permute-start | bytes 663560 | tf_op jit(solution)/shard_map/ppermute | solution.py:679
  5.5 28.0 %collective-permute-start.3 = (bf16[1024,512]{1,0:T(8,128)(2,1)}, bf16[1024,512]{1,0:T(8,128)(2,1)}, u32[]{:S(2)}, u32[]{:S(2)}) collective-permute-start(bf16[1024,512]{1,0:T(8,128)(2,1)} %refs_6_.1), channel_id=1, source_target_pairs={{0,1},{1,0},{2,3},{3,2},{4,5},{5,4},{6,7},{7,6},{8,9},{9,8},{10,11... | collective-permute-start | bytes 3145736 | tf_op jit(solution)/shard_map/ppermute | solution.py:679
  7.7 10.7 %copy-start.19 = (bf16[256]{0:T(256)(128)(2,1)S(1)}, bf16[256]{0:T(256)(128)(2,1)}, u32[]{:S(2)}) copy-start(bf16[256]{0:T(256)(128)(2,1)} %param.26) | copy-start | bytes 1540
  7.7 10.7 %copy-start.9 = (f32[512]{0:T(512)S(1)}, f32[512]{0:T(512)}, u32[]{:S(2)}) copy-start(f32[512]{0:T(512)} %param.22) | copy-start | bytes 6148
  7.7 10.7 %copy-start.12 = (f32[512]{0:T(512)S(1)}, f32[512]{0:T(512)}, u32[]{:S(2)}) copy-start(f32[512]{0:T(512)} %param.23) | copy-start | bytes 6148
  7.7 10.7 %copy-start.13 = (f32[512]{0:T(512)S(1)}, f32[512]{0:T(512)}, u32[]{:S(2)}) copy-start(f32[512]{0:T(512)} %param.24) | copy-start | bytes 6148
  7.7 10.7 %copy-start.14 = (f32[512]{0:T(512)S(1)}, f32[512]{0:T(512)}, u32[]{:S(2)}) copy-start(f32[512]{0:T(512)} %param.28) | copy-start | bytes 6148
  7.7 10.7 %copy-start.15 = (f32[512]{0:T(512)S(1)}, f32[512]{0:T(512)}, u32[]{:S(2)}) copy-start(f32[512]{0:T(512)} %param.29) | copy-start | bytes 6148
  7.7 10.7 %copy-start.16 = (f32[512]{0:T(512)S(1)}, f32[512]{0:T(512)}, u32[]{:S(2)}) copy-start(f32[512]{0:T(512)} %param.30) | copy-start | bytes 6148
  7.7 11.3 %copy-start.7 = (bf16[256,512]{1,0:T(8,128)(2,1)S(1)}, bf16[256,512]{1,0:T(8,128)(2,1)}, u32[]{:S(2)}) copy-start(bf16[256,512]{1,0:T(8,128)(2,1)} %param.27) | copy-start | bytes 786436
  7.7 11.3 %copy-start.8 = (bf16[256,512]{1,0:T(8,128)(2,1)S(1)}, bf16[256,512]{1,0:T(8,128)(2,1)}, u32[]{:S(2)}) copy-start(bf16[256,512]{1,0:T(8,128)(2,1)} %param.21) | copy-start | bytes 786436
  11.8 5.7 %collective-permute-start.1 = (bf16[128,768]{1,0:T(8,128)(2,1)S(1)}, bf16[128,768]{1,0:T(8,128)(2,1)S(1)}, u32[]{:S(2)}, u32[]{:S(2)}) collective-permute-start(bf16[128,768]{1,0:T(8,128)(2,1)S(1)} %slice.196), channel_id=1, source_target_pairs={{0,4},{2,6},{4,0},{6,2},{8,12},{10,14},{12,8},{14,10},{16,20},{18,... | collective-permute-start | bytes 589832 | tf_op jit(solution)/shard_map/ppermute | solution.py:682
  17.6 2.2 %collective-permute-start.2 = (bf16[256,768]{1,0:T(8,128)(2,1)S(1)}, bf16[256,768]{1,0:T(8,128)(2,1)S(1)}, u32[]{:S(2)}, u32[]{:S(2)}) collective-permute-start(bf16[256,768]{1,0:T(8,128)(2,1)S(1)} %pad_maximum_fusion.3), channel_id=1, source_target_pairs={{0,2},{2,0},{4,6},{6,4},{8,10},{10,8},{12,14},{14,12},{16,18},{18,... | collective-permute-start | bytes 1179656 | tf_op jit(solution)/shard_map/ppermute | solution.py:682
  19.1 14.4 %copy-start.4 = (bf16[784,512]{1,0:T(8,128)(2,1)}, bf16[784,512]{1,0:T(8,128)(2,1)S(1)}, u32[]{:S(2)}) copy-start(bf16[784,512]{1,0:T(8,128)(2,1)S(1)} %fusion.1.w_own_ref) | copy-start | bytes 2408452
  33.5 26.8 %collective-permute-start.4 = (bf16[784,512]{1,0:T(8,128)(2,1)S(1)}, bf16[784,512]{1,0:T(8,128)(2,1)S(1)}, u32[]{:S(2)}, u32[]{:S(2)}) collective-permute-start(bf16[784,512]{1,0:T(8,128)(2,1)S(1)} %fusion.1.w_own_ref), channel_id=1, source_target_pairs={{0,1},{1,0},{2,3},{3,2},{4,5},{5,4},{6,7},{7,6},{8,9},{9,8},{10,11... | collective-permute-start | bytes 2408456 | tf_op jit(solution)/shard_map/ppermute | solution.py:679
  60.3 0.9 copy-start.17
  74.9 28.8 %collective-permute-start.5 = (bf16[768,512]{1,0:T(8,128)(2,1)}, bf16[768,512]{1,0:T(8,128)(2,1)S(1)}, u32[]{:S(2)}, u32[]{:S(2)}) collective-permute-start(bf16[768,512]{1,0:T(8,128)(2,1)} %get-tuple-element.57), channel_id=1, source_target_pairs={{0,1},{1,0},{2,3},{3,2},{4,5},{5,4},{6,7},{7,6},{8,9},{9,8},{10,11... | collective-permute-start | bytes 2359304 | tf_op jit(solution)/shard_map/ppermute | solution.py:679
  75.2 28.5 %copy-start.5 = (f32[8,512]{1,0:T(8,128)S(1)}, f32[8,512]{1,0:T(8,128)}, u32[]{:S(2)}) copy-start(f32[8,512]{1,0:T(8,128)} %get-tuple-element.75) | copy-start | bytes 49156
  75.2 28.5 %copy-start.2 = (f32[768,512]{1,0:T(8,128)S(1)}, f32[768,512]{1,0:T(8,128)}, u32[]{:S(2)}) copy-start(f32[768,512]{1,0:T(8,128)} %get-tuple-element.56) | copy-start | bytes 4718596
  101.9 30.7 %collective-permute-start.7 = (bf16[1024,512]{1,0:T(8,128)(2,1)}, bf16[1024,512]{1,0:T(8,128)(2,1)S(1)}, u32[]{:S(2)}, u32[]{:S(2)}) collective-permute-start(bf16[1024,512]{1,0:T(8,128)(2,1)} %get-tuple-element.66), channel_id=1, source_target_pairs={{0,1},{1,0},{2,3},{3,2},{4,5},{5,4},{6,7},{7,6},{8,9},{9,8},{10,11... | collective-permute-start | bytes 3145736 | tf_op jit(solution)/shard_map/ppermute | solution.py:679
  104.0 28.5 %collective-permute-start.6 = (bf16[384,512]{1,0:T(8,128)(2,1)S(1)}, bf16[384,512]{1,0:T(8,128)(2,1)S(1)}, u32[]{:S(2)}, u32[]{:S(2)}) collective-permute-start(bf16[384,512]{1,0:T(8,128)(2,1)S(1)} %fusion.3), channel_id=1, source_target_pairs={{0,4},{2,6},{4,0},{6,2},{8,12},{10,14},{12,8},{14,10},{16,20},{18,... | collective-permute-start | bytes 1179656 | tf_op jit(solution)/shard_map/ppermute | solution.py:682
  131.0 1.8 copy-start.1
  132.5 1.0 copy-start.3
  132.7 1.5 collective-permute-start.15
  133.7 10.3 %collective-permute-start.8 = (bf16[800,512]{1,0:T(8,128)(2,1)S(1)}, bf16[800,512]{1,0:T(8,128)(2,1)S(1)}, u32[]{:S(2)}, u32[]{:S(2)}) collective-permute-start(bf16[800,512]{1,0:T(8,128)(2,1)S(1)} %constant_dynamic-update-slice_fusion), channel_id=1, source_target_pairs={{0,2},{2,0},{4,6},{6,4},{8,10},{10,8},{12,14},{14,12},{16,18},{18,... | collective-permute-start | bytes 2457608 | tf_op jit(solution)/shard_map/ppermute | solution.py:613
  134.3 7.0 %collective-permute-start.16 = (bf16[192,512]{1,0:T(8,128)(2,1)S(1)}, bf16[192,512]{1,0:T(8,128)(2,1)S(1)}, u32[]{:S(2)}, u32[]{:S(2)}) collective-permute-start(bf16[192,512]{1,0:T(8,128)(2,1)S(1)} %fusion.4), channel_id=1, source_target_pairs={{0,8},{2,10},{4,12},{6,14},{8,0},{10,2},{12,4},{14,6},{16,24},{18,... | collective-permute-start | bytes 589832 | tf_op jit(solution)/shard_map/ppermute | solution.py:613
  141.3 11.3 %collective-permute-start.17 = (bf16[192,512]{1,0:T(8,128)(2,1)S(1)}, bf16[192,512]{1,0:T(8,128)(2,1)S(1)}, u32[]{:S(2)}, u32[]{:S(2)}) collective-permute-start(bf16[192,512]{1,0:T(8,128)(2,1)S(1)} %add_convert_fusion.1), channel_id=1, source_target_pairs={{0,16},{2,18},{4,20},{6,22},{8,24},{10,26},{12,28},{14,30},{16,0},... | collective-permute-start | bytes 589832 | tf_op jit(solution)/shard_map/ppermute | solution.py:613
  144.4 10.5 %collective-permute-start.9 = (bf16[400,512]{1,0:T(8,128)(2,1)S(1)}, bf16[400,512]{1,0:T(8,128)(2,1)S(1)}, u32[]{:S(2)}, u32[]{:S(2)}) collective-permute-start(bf16[400,512]{1,0:T(8,128)(2,1)S(1)} %pad_maximum_fusion.2), channel_id=1, source_target_pairs={{0,1},{1,0},{2,3},{3,2},{4,5},{5,4},{6,7},{7,6},{8,9},{9,8},{10,11... | collective-permute-start | bytes 1228808 | tf_op jit(solution)/shard_map/ppermute | solution.py:625
  152.7 3.0 %collective-permute-start.18 = (bf16[192,512]{1,0:T(8,128)(2,1)S(1)}, bf16[192,512]{1,0:T(8,128)(2,1)S(1)}, u32[]{:S(2)}, u32[]{:S(2)}) collective-permute-start(bf16[192,512]{1,0:T(8,128)(2,1)S(1)} %add_convert_fusion), channel_id=1, source_target_pairs={{0,2},{2,0},{4,6},{6,4},{8,10},{10,8},{12,14},{14,12},{16,18},{18,... | collective-permute-start | bytes 589832 | tf_op jit(solution)/shard_map/ppermute | solution.py:613
  155.1 8.3 %collective-permute-start.10 = (bf16[208,512]{1,0:T(8,128)(2,1)S(1)}, bf16[208,512]{1,0:T(8,128)(2,1)S(1)}, u32[]{:S(2)}, u32[]{:S(2)}) collective-permute-start(bf16[208,512]{1,0:T(8,128)(2,1)S(1)} %pad_maximum_fusion.6), channel_id=1, source_target_pairs={{0,4},{2,6},{4,0},{6,2},{8,12},{10,14},{12,8},{14,10},{16,20},{18,... | collective-permute-start | bytes 638984 | tf_op jit(solution)/shard_map/ppermute | solution.py:613
  155.7 13.4 %collective-permute-start.19 = (bf16[384,512]{1,0:T(8,128)(2,1)S(1)}, bf16[384,512]{1,0:T(8,128)(2,1)S(1)}, u32[]{:S(2)}, u32[]{:S(2)}) collective-permute-start(bf16[384,512]{1,0:T(8,128)(2,1)S(1)} %pad_maximum_fusion.5), channel_id=1, source_target_pairs={{0,4},{2,6},{4,0},{6,2},{8,12},{10,14},{12,8},{14,10},{16,20},{18,... | collective-permute-start | bytes 1179656 | tf_op jit(solution)/shard_map/ppermute | solution.py:613
  163.4 5.9 %collective-permute-start.11 = (bf16[208,512]{1,0:T(8,128)(2,1)S(1)}, bf16[208,512]{1,0:T(8,128)(2,1)S(1)}, u32[]{:S(2)}, u32[]{:S(2)}) collective-permute-start(bf16[208,512]{1,0:T(8,128)(2,1)S(1)} %pad_maximum_fusion.7), channel_id=1, source_target_pairs={{0,8},{2,10},{4,12},{6,14},{8,0},{10,2},{12,4},{14,6},{16,24},{18,... | collective-permute-start | bytes 638984 | tf_op jit(solution)/shard_map/ppermute | solution.py:613
  169.4 10.9 %collective-permute-start.12 = (bf16[208,512]{1,0:T(8,128)(2,1)S(1)}, bf16[208,512]{1,0:T(8,128)(2,1)S(1)}, u32[]{:S(2)}, u32[]{:S(2)}) collective-permute-start(bf16[208,512]{1,0:T(8,128)(2,1)S(1)} %pad_maximum_fusion.8), channel_id=1, source_target_pairs={{0,16},{2,18},{4,20},{6,22},{8,24},{10,26},{12,28},{14,30},{16,0},... | collective-permute-start | bytes 638984 | tf_op jit(solution)/shard_map/ppermute | solution.py:613
  180.4 5.7 %collective-permute-start.13 = (bf16[192,512]{1,0:T(8,128)(2,1)S(1)}, bf16[192,512]{1,0:T(8,128)(2,1)S(1)}, u32[]{:S(2)}, u32[]{:S(2)}) collective-permute-start(bf16[192,512]{1,0:T(8,128)(2,1)S(1)} %add_convert_fusion.2), channel_id=1, source_target_pairs={{0,4},{2,6},{4,0},{6,2},{8,12},{10,14},{12,8},{14,10},{16,20},{18,... | collective-permute-start | bytes 589832 | tf_op jit(solution)/shard_map/ppermute | solution.py:613
  186.2 1.9 collective-permute-start.14

commit v3 on v2

--- a/solution.py
+++ b/solution.py
@@ -39,14 +39,14 @@
 
 
 def key_value_block(x, w_refs, bias_ref, extra_k, k_ref, v_ref, rows):
-    shard = w_refs[0].shape[1] // 3
+    shard = w_refs[0].shape[2]
     extra_k = extra_k.astype(F32)
     extra_v = values_columns(x.shape[0])
     low = lax.broadcasted_iota(jnp.int32, extra_k.shape, 1) < HD
     for side, w_ref in enumerate(w_refs):
         mine = slice(side * shard, (side + 1) * shard)
-        keys = dot(x, w_ref[:, shard : 2 * shard], 1, 0)
-        values = dot(x, w_ref[:, 2 * shard :], 1, 0) + bias_ref[1:2, mine]
+        keys = dot(x, w_ref[1], 1, 0)
+        values = dot(x, w_ref[2], 1, 0) + bias_ref[1:2, mine]
         for i in range(shard // HD):
             pair = slice((i // 2) * LANES, (i // 2 + 1) * LANES)
             k_pair, v_pair = keys[:, pair], values[:, pair]
@@ -59,11 +59,11 @@
 
 def project_kernel(x_ref, own_ref, oth_ref, bias_ref, extra_k_ref, extra_q_ref, k_ref, v_ref, qt_ref, q_ref):
     x = x_ref[...]
-    shard = own_ref.shape[1] // 3
+    shard = own_ref.shape[2]
     key_value_block(x, (own_ref, oth_ref), bias_ref, extra_k_ref[...], k_ref, v_ref, slice(None))
     for side, w_ref in enumerate((own_ref, oth_ref)):
         mine = slice(side * shard, (side + 1) * shard)
-        q = (dot(x, w_ref[:, :shard], 1, 0) + bias_ref[0:1, mine]).astype(BF)
+        q = (dot(x, w_ref[0], 1, 0) + bias_ref[0:1, mine]).astype(BF)
         q_ref[:, mine] = q
         turned = q.T
         for i in range(shard // HD):
@@ -391,23 +391,23 @@
 
 
 def times_weights(grad, own_ref, oth_ref, third):
-    shard = own_ref.shape[1] // 3
-    mine = slice(third * shard, (third + 1) * shard)
-    return dot(grad[:, :shard], own_ref[:, mine], 1, 1) + dot(grad[:, shard:], oth_ref[:, mine], 1, 1)
+    shard = own_ref.shape[2]
+    return dot(grad[:, :shard], own_ref[third], 1, 1) + dot(grad[:, shard:], oth_ref[third], 1, 1)
 
 
 def backward_kernel(sub, count, part, *refs):
     if part:
         (p_hbm, dot_hbm, dnat_hbm, q_hbm, k_hbm, v_hbm, x_hbm, own_hbm, oth_hbm,
-         dq_ref, dx_ref, gw_ref,
+         dq_hbm, dx_ref, gw_ref, bias_ref,
          dot_ref, dnat_ref, q_ref, k_ref, v_ref, x_ref, own_ref, oth_ref,
-         dk_ref, dv_ref, acc_scr, p_scr, sem, pair_sem, last_sem) = refs
+         dq_ref, dk_ref, dv_ref, acc_scr, p_scr, sem, pair_sem, last_sem, out_sem) = refs
         more = ((own_hbm, own_ref), (oth_hbm, oth_ref))
     else:
-        (p_hbm, dot_hbm, dnat_hbm, q_hbm, k_hbm, v_hbm, x_hbm, dq_hbm, gw_hbm,
-         pack_ref, bias_ref, dq_out, dk_ref, dv_ref,
-         dot_ref, dnat_ref, q_ref, k_ref, v_ref, x_ref, before_ref, gw_ref, dq_ref,
-         acc_scr, p_scr, sem, pair_sem, last_sem) = refs
+        (core_ref, small_ref, value_ref,
+         p_hbm, dot_hbm, dnat_hbm, q_hbm, k_hbm, v_hbm, x_hbm, dq_hbm, gw_hbm,
+         sent_ref, kept_ref, dq_out, dk_hbm, dv_hbm,
+         dot_ref, dnat_ref, q_ref, k_ref, v_ref, x_ref, before_ref, gw_ref,
+         dq_ref, dk_ref, dv_ref, gq_ref, bias_ref, acc_scr, p_scr, sem, pair_sem, last_sem, out_sem) = refs
         more = ((dq_hbm, before_ref), (gw_hbm, gw_ref))
     heads, _, queries = dot_ref.shape
     keys = k_ref.shape[1]
@@ -438,23 +438,34 @@
         ]
 
     last = ((x_hbm, x_ref),) + more
+
+    def rows_out(p):
+        rows = pl.ds(pl.multiple_of(p * 2 * HD, 2 * HD), 2 * HD)
+        return pltpu.make_async_copy(dq_ref.at[rows, :], dq_hbm.at[rows, :], out_sem.at[p])
+
     last_copies = [pltpu.make_async_copy(src, dst, last_sem.at[n]) for n, (src, dst) in enumerate(last)]
 
     for copy in pair_copies(0):
         copy.start()
     for step in range(slots - 1):
         copy_in(step).start()
-    for p in range(1, heads // 2):
-        for copy in pair_copies(p):
-            copy.start()
-    for copy in last_copies:
-        copy.start()
 
     @pl.loop(0, heads // 2)
     def _(p):
         lanes = pl.ds(pl.multiple_of(p * LANES, LANES), LANES)
         for copy in pair_copies(p):
             copy.wait()
+
+        @pl.when(p + 1 < heads // 2)
+        def _():
+            for copy in pair_copies(p + 1):
+                copy.start()
+
+        @pl.when(p == 1)
+        def _():
+            for copy in last_copies:
+                copy.start()
+
         acc_scr[...] = jnp.zeros_like(acc_scr)
 
         @pl.loop(0, blocks)
@@ -486,13 +497,23 @@
 
         for side in range(2):
             dq_ref[pl.ds(pl.multiple_of((2 * p + side) * HD, HD), HD), :] = acc_scr[side, :HD, :]
+        if part:
+            rows_out(p).start()
 
     for copy in last_copies:
         copy.wait()
+    bias_ref[...] = jnp.zeros_like(bias_ref)
     if part:
         gw_ref[...] = jnp.zeros_like(gw_ref)
+        copies_out = [rows_out(p) for p in range(heads // 2)]
     else:
-        bias_ref[...] = jnp.zeros_like(bias_ref)
+        gq_ref[...] = jnp.zeros_like(gq_ref)
+        copies_out = [
+            pltpu.make_async_copy(dk_ref, dk_hbm, out_sem.at[0]),
+            pltpu.make_async_copy(dv_ref, dv_hbm, out_sem.at[1]),
+        ]
+        for copy in copies_out:
+            copy.start()
 
     @pl.loop(0, keys // sub)
     def _(i):
@@ -500,56 +521,64 @@
         x, dk, dv = x_ref[rows, :], dk_ref[rows, :], dv_ref[rows, :]
         gw_ref[0] += dot(x, dk, 0, 0)
         gw_ref[1] += dot(x, dv, 0, 0)
+        bias_ref[1:2, :] += jnp.sum(dv.astype(F32), axis=0, keepdims=True)
         if part:
             dx_ref[rows, :] = (times_weights(dk, own_ref, oth_ref, 1) + times_weights(dv, own_ref, oth_ref, 2)).astype(BF)
-            gw_ref[2, 0:1, :] += jnp.sum(dv.astype(F32), axis=0, keepdims=True)
         else:
             dq = ((before_ref[:, rows] + dq_ref[:, rows]) * HD**-0.5).astype(BF).T
             dq_out[rows, :] = dq
-            gw_ref[2] = jnp.where(i == 0, 0.0, gw_ref[2]) + dot(x, dq, 0, 0)
+            gq_ref[...] += dot(x, dq, 0, 0)
             bias_ref[0:1, :] += jnp.sum(dq.astype(F32), axis=0, keepdims=True)
-            bias_ref[1:2, :] += jnp.sum(dv.astype(F32), axis=0, keepdims=True)
 
     if not part:
-        for cut in range(2):
-            for third in range(3):
-                row = third * shard + cut * (shard // 2)
-                core, at = row // (3 * shard // 2), row % (3 * shard // 2)
-                to = slice(at, at + shard // 2)
-                grad = gw_ref.at[(2, 0, 1)[third]]
-                for side in range(2):
-                    mine = slice(side * shard, (side + 1) * shard)
-                    for place, start in ((slice(0, shard), 0), (slice(shard, width), shard)):
-                        top = slice(start + cut * (shard // 2), start + (cut + 1) * (shard // 2))
-                        pack_ref[core, side, to, place] = grad[top, mine].astype(BF)
-
-
-def attend_backward(part, probs, dot_turned, dnat, q, k, v, x, *more):
+        first = core_ref[0] == 0
+        bias_ref[1:2, :] += value_ref[1:2, :]
+        cut = 3 * width // 2
+        for side in range(2):
+            mine = slice(side * shard, (side + 1) * shard)
+            pieces = [gq_ref[:, mine], gw_ref[0, :, mine], gw_ref[1, :, mine]]
+            blocks = [piece[at : at + shard, :].astype(BF) for piece in pieces for at in (0, shard)]
+            for n in range(3):
+                to = slice(side * cut + n * shard, side * cut + (n + 1) * shard)
+                kept_ref[to, :] = jnp.where(first, blocks[n], blocks[3 + n])
+                sent_ref[to, :] = jnp.where(first, blocks[3 + n], blocks[n])
+            rows16 = [small_ref[:6, :shard], small_ref[6:7, mine], bias_ref[0:1, mine]]
+            rows16 += [small_ref[:6, shard:], jnp.zeros((1, shard), F32), bias_ref[1:2, mine]]
+            value = jnp.concatenate(rows16, axis=0)
+            high = value.astype(BF)
+            for n, half in enumerate((high, (value - high.astype(F32)).astype(BF))):
+                to = slice(2 * cut + (2 * side + n) * 16, 2 * cut + (2 * side + n + 1) * 16)
+                kept_ref[to, :] = half
+                sent_ref[to, :] = half
+
+    for copy in copies_out:
+        copy.wait()
+
+
+def attend_backward(part, first, probs, dot_turned, dnat, q, k, v, x, *more):
     heads, keys, queries = probs.shape
     width = heads * HD
     sub, count, slots = 256, 2, 4
-    sums = jax.ShapeDtypeStruct((3, width, width), F32)
+    sums = jax.ShapeDtypeStruct((2, width, width), F32)
     turned = jax.ShapeDtypeStruct((width, queries), F32)
     grad = jax.ShapeDtypeStruct((queries, width), BF)
     inputs = (dot_turned, dnat, q, k, v, x) + more
     held = [pltpu.VMEM(a.shape, a.dtype) for a in inputs]
+    held += [pltpu.VMEM(turned.shape, F32), pltpu.VMEM(grad.shape, BF), pltpu.VMEM(grad.shape, BF)]
     if part:
-        out_shape = (turned, grad, sums)
-        held += [pltpu.VMEM(grad.shape, BF)] * 2
+        out_shape = (turned, grad, sums, jax.ShapeDtypeStruct((2, width), F32))
+        out_specs = (HBM, VMEM, VMEM, VMEM)
     else:
-        out_shape = (
-            jax.ShapeDtypeStruct((2, 2, 3 * width // 4, width), BF),
-            jax.ShapeDtypeStruct((2, width), F32),
-            grad,
-            grad,
-            grad,
-        )
-        held = held[:6] + [pltpu.VMEM(turned.shape, F32), pltpu.VMEM(sums.shape, F32), pltpu.VMEM(turned.shape, F32)]
+        payload = jax.ShapeDtypeStruct((3 * width + 64, width // 2), BF)
+        out_shape = (payload, payload, grad, grad, grad)
+        out_specs = (VMEM, VMEM, VMEM, HBM, HBM)
+        held += [pltpu.VMEM((width, width), F32), pltpu.VMEM((2, width), F32)]
+    first_specs = [pl.BlockSpec(memory_space=pltpu.SMEM), VMEM, VMEM][: len(first)]
     return pl.pallas_call(
         functools.partial(backward_kernel, sub, count, part),
         out_shape=out_shape,
-        in_specs=[HBM] * (1 + len(inputs)),
-        out_specs=(VMEM,) * len(out_shape),
+        in_specs=first_specs + [HBM] * (1 + len(inputs)),
+        out_specs=out_specs,
         scratch_shapes=held
         + [
             pltpu.VMEM((2, LANES, queries), F32),
@@ -557,11 +586,12 @@
             pltpu.SemaphoreType.DMA((slots,)),
             pltpu.SemaphoreType.DMA((heads // 2, 5)),
             pltpu.SemaphoreType.DMA((1 + len(more),)),
+            pltpu.SemaphoreType.DMA((heads // 2,)),
         ],
         compiler_params=params(),
         cost_estimate=cost(heads * keys * queries * 512, heads * keys * queries),
         name="attend_back_own" if not part else "attend_back_other",
-    )(probs, *inputs)
+    )(*first, probs, *inputs)
 
 
 def input_kernel(res_ref, got_ref, dq_ref, dk_ref, dv_ref, own_ref, oth_ref, dx_ref):
@@ -574,7 +604,7 @@
 def input_gradient(res, got, dq, dk, dv, w_own, w_oth):
     tokens, width = res.shape
     rows = pl.BlockSpec((256, width), lambda i: (i, 0))
-    whole = pl.BlockSpec(w_own.shape, lambda i: (0, 0))
+    whole = pl.BlockSpec(w_own.shape, lambda i: (0, 0, 0))
     return pl.pallas_call(
         input_kernel,
         grid=(tokens // 256,),
@@ -587,13 +617,18 @@
     )(res, got, dq, dk, dv, w_own, w_oth)
 
 
+def after(values, *others):
+    return lax.optimization_barrier((values,) + others)[0]
+
+
 def two_halves(values):
     high = values.astype(BF)
     return jnp.concatenate([high, (values - high.astype(F32)).astype(BF)], axis=0)
 
 
 def one_value(halves):
-    return halves[:8].astype(F32) + halves[8:].astype(F32)
+    rows = halves.shape[0] // 2
+    return halves[:rows].astype(F32) + halves[rows:].astype(F32)
 
 
 def take(values, which):
@@ -604,51 +639,53 @@
     return jnp.concatenate([jnp.where(which == 0, mine, theirs), jnp.where(which == 0, theirs, mine)])
 
 
-def sum_gradients(packed, small_own, small_oth, mid, devices):
+def sum_gradients(sent, kept, mid, input_grad, devices):
     index = lax.axis_index("dp")
     core, near = lax.rem(index, 2), lax.rem(index // 2, 2)
-    rows = packed.shape[2]
+    rows = (sent.shape[0] - 64) // 2
 
     def across(values, bit):
         return lax.ppermute(values, "dp", [(i, i ^ bit) for i in range(devices)])
 
-    own_two, oth_two = two_halves(small_own), two_halves(small_oth)
-    sent = jnp.concatenate([take(packed, 1 - core).reshape(2 * rows, -1), own_two, oth_two])
     got = across(sent, 1)
-    kept = take(packed, core).reshape(2 * rows, -1).astype(F32) + got[: 2 * rows].astype(F32)
-    small_own = one_value(own_two) + one_value(got[2 * rows : 2 * rows + 16])
-    small_oth = one_value(oth_two) + one_value(got[2 * rows + 16 :])
-    halves = mid.reshape(2, rows // 2, -1)
-    mid = take(halves, core) + across(take(halves, 1 - core).astype(BF), 1).astype(F32)
-
-    own_two, oth_two = two_halves(small_own), two_halves(small_oth)
-    got = lax.ppermute(jnp.concatenate([kept[rows:].astype(BF), oth_two]), "tensor", [(0, 1), (1, 0)])
-    kept = kept[:rows] + got[:rows].astype(F32)
+    halves = mid.reshape(2, mid.shape[0] // 2, -1)
+    mid_got = across(take(halves, 1 - core).astype(BF), 1)
+    total = kept[: 2 * rows].astype(F32) + got[: 2 * rows].astype(F32)
+    small_own = one_value(kept[2 * rows : 2 * rows + 32]) + one_value(got[2 * rows : 2 * rows + 32])
+    small_oth = one_value(kept[2 * rows + 32 :]) + one_value(got[2 * rows + 32 :])
+    mid = (take(halves, core) + mid_got.astype(F32)).astype(BF)
+    oth_two = two_halves(small_oth)
+    mid_got = across(after(mid, oth_two), 4)
+    result = input_grad(got)
+
+    own_two = two_halves(small_own)
+    got = lax.ppermute(jnp.concatenate([total[rows:].astype(BF), oth_two]), "tensor", [(0, 1), (1, 0)])
+    total = total[:rows] + got[:rows].astype(F32)
     small = one_value(own_two) + one_value(got[rows:])
 
-    halves = kept.reshape(2, rows // 2, -1)
+    halves = total.reshape(2, rows // 2, -1)
     two = two_halves(small)
     got = across(jnp.concatenate([take(halves, 1 - near).astype(BF), two]), 2)
-    kept = take(halves, near) + got[: rows // 2].astype(F32)
+    total = take(halves, near) + got[: rows // 2].astype(F32)
     small = one_value(two) + one_value(got[rows // 2 :])
 
     bit = 4
     while bit < devices:
-        low = mid.astype(BF)
-        mid = low.astype(F32) + across(low, bit).astype(F32)
-        sent = jnp.concatenate([kept.astype(BF), two_halves(small)])
+        sent = jnp.concatenate([total.astype(BF), two_halves(small)])
+        mid = (mid.astype(F32) + mid_got.astype(F32)).astype(BF)
+        if 2 * bit < devices:
+            mid_got = across(mid, 2 * bit)
         got = across(sent, bit)
-        kept = sent[: rows // 2].astype(F32) + got[: rows // 2].astype(F32)
+        total = sent[: rows // 2].astype(F32) + got[: rows // 2].astype(F32)
         small = one_value(sent[rows // 2 :]) + one_value(got[rows // 2 :])
         bit *= 2
-
-    mid = mid.astype(BF)
     mid = in_order(mid, across(mid, 1), core)
-    mid = in_order(mid, across(mid, 2), near)
-    kept = kept.astype(BF)
-    kept = in_order(kept, across(kept, 2), near)
-    kept = in_order(kept, across(kept, 1), core)
-    return kept.astype(F32), small, mid.astype(F32)
+    mid = in_order(after(mid, got), after(across(mid, 2), got), near)
+
+    total = total.astype(BF)
+    total = in_order(total, across(total, 2), near)
+    total = in_order(total, across(total, 1), core)
+    return total.astype(F32), small, mid.astype(F32), result
 
 
 def mask_columns(known, lengths):
@@ -681,17 +718,15 @@
     def across(values, bit):
         return lax.ppermute(values, "dp", [(i, i ^ bit) for i in range(devices)])
 
-    w_own = w_qkv.reshape(width, 3 * shard)
-    quarter = width // 4
-    bias_row = jnp.pad(bias_qv.reshape(1, 2 * shard), ((0, 15), (0, shard)))
-    sent = jnp.concatenate([lax.dynamic_slice_in_dim(w_own, (2 * core + near) * quarter, quarter, 0), bias_row])
-    got = swapped(sent)
+    w_own = w_qkv.transpose(1, 0, 2)
+    quarter = 3 * width // 4
+    mine = lax.dynamic_slice_in_dim(w_own.reshape(3 * width, shard), (2 * core + near) * quarter, quarter, 0)
+    got = swapped(jnp.concatenate([mine, jnp.pad(bias_qv, ((0, 14), (0, 0)))]))
     x_oth = swapped(layer_input)
     piece = got[:quarter]
     piece = in_order(piece, across(piece, 2), near)
-    w_oth = in_order(piece, across(piece, 1), core)
-    bias_oth = got[quarter, : 2 * shard].reshape(2, shard)
-    bias = jnp.concatenate([bias_qv, bias_oth], axis=1).astype(F32)
+    w_oth = in_order(piece, across(piece, 1), core).reshape(3, width, shard)
+    bias = jnp.concatenate([bias_qv, got[quarter : quarter + 2]], axis=1).astype(F32)
 
     key_cols, query_rows = mask_columns(gene_known, cell_genes[0])
     key_own = lax.dynamic_slice_in_dim(key_cols, side * tokens, tokens, 0)
@@ -709,32 +744,29 @@
         layer_input, cotangent, ot, linv, mid_w, mid_w_oth, vectors
     )
     mid_got = swapped(mid_oth)
-    dq, dx_oth, sums = attend_backward(1, probs, dot_turned, dnat, q, k_oth, v_oth, x_oth, w_own, w_oth)
+    dq, dx_oth, sums, value_grad = attend_backward(
+        1, (), probs, dot_turned, dnat, q, k_oth, v_oth, x_oth, w_own, w_oth
+    )
     mid_got, dq = lax.optimization_barrier((mid_got, dq))
     mid = (mid_own + mid_got.astype(F32)).reshape(2, 3 * shard // 2, width)
     mid_got = across(take(mid, 1 - near).astype(BF), 2)
     dx_got = swapped(dx_oth)
-    packed, bias_grad, dq, dk, dv = attend_backward(
-        0, probs, dot_turned, dnat, q, k_own, v_own, layer_input, dq, sums
+    sent, kept, dq, dk, dv = attend_backward(
+        0, (core[None], small, value_grad), probs, dot_turned, dnat, q, k_own, v_own, layer_input, dq, sums
     )
-    mid_got, dx_got, packed = lax.optimization_barrier((mid_got, dx_got, packed))
+    mid_got, dx_got, sent = lax.optimization_barrier((mid_got, dx_got, sent))
     mid = take(mid, near) + mid_got.astype(F32)
-    input_grad = input_gradient(res, dx_got, dq, dk, dv, w_own, w_oth)
-    values_grad = bias_grad[1:2] + sums[2, 0:1]
-
-    def small_rows(mine):
-        b_up_row = jnp.pad(small[6:7, mine], ((0, 0), (0, shard)))
-        bias_row = jnp.concatenate([bias_grad[0:1, mine], values_grad[:, mine]], axis=1)
-        return jnp.concatenate([small[:6], b_up_row, bias_row])
-
-    qkv, small, mid = sum_gradients(
-        packed, small_rows(slice(0, shard)), small_rows(slice(shard, width)), mid, devices
-    )
-    qkv_g = qkv.reshape(3, shard, 2, shard).transpose(2, 1, 0, 3).reshape(width, 3, shard)
+
+    def input_grad(token):
+        return input_gradient(res, dx_got, after(dq, token), dk, dv, w_own, w_oth)
+
+    qkv, small, mid, input_grad = sum_gradients(sent, kept, mid, input_grad, devices)
+    qkv_g = qkv.reshape(3, width, shard).transpose(1, 0, 2)
+    wide = jnp.concatenate([small[:6], small[8:14]], axis=1)
     up_g = jnp.concatenate([mid[width:, :shard], mid[width:, shard:]])
     return (
-        activations, input_grad, qkv_g, small[7].reshape(2, shard), mid[:shard], small[0], small[1], small[2],
-        up_g, small[6, :shard], mid[shard:width], small[3], small[4], small[5],
+        activations, input_grad, qkv_g, jnp.stack([small[7], small[15]]), mid[:shard], wide[0], wide[1], wide[2],
+        up_g, small[6], mid[shard:width], wide[3], wide[4], wide[5],
     )
 
 

time: 191 us -> 182 us (0.953)
  waiting for transfers between devices: 45.7 us -> 34.1 us
  other arithmetic: 7.21 us -> 15.5 us
  local copies, waits for them, and re-layouts: 12 us -> 6.2 us
    ppermute x14, waiting for transfers between devices: 33.5 us -> 21.6 us  [across(): return lax.ppermute(values, 'dp', [(i, i ^ bit) for i in range(devices)])]
    ppermute x1, waiting for transfers between devices: 2.1 us -> 5.33 us  [sum_gradients(): lax.ppermute(jnp.concatenate([total[rows:].astype(BF), oth_two]), 'tensor...]
    ppermute x5, waiting for transfers between devices: 10.1 us -> 7.2 us  [swapped(): return lax.ppermute(values, 'tensor', [(0, 1), (1, 0)])]
    reshape x3 -> x0, local copies, waits for them, and re-layouts: 2.58 us -> none  [the longest x2 2.31 us: local(): qkv.reshape(3, shard, 2, shard).transpose(2, 1, 0, 3)]
    unnamed x43 -> x32, local copies, waits for them, and re-layouts: 3.06 us -> 1 us
  transfers between devices with their start and end apart: 20 -> 20, of which waited for: 12 -> 10; matrix products, arithmetic and copies ran while one was open for 7% -> 10% of each run, Pallas kernels for 47% -> 49%
where the time goes in v3:
time: 182 us
  Pallas kernels  102 us (56%)
  waiting for transfers between devices  34.1 us (19%)
  starting transfers between devices  22.6 us (12%)
  other arithmetic  15.5 us (9%)
  local copies, waits for them, and re-layouts  6.2 us (3%)
    pallas_call x2, Pallas kernels, attend_backward(): pl.pallas_call(functools.partial(backward_kernel, sub, count, part), out_...  50.6 us
    pallas_call x1, Pallas kernels, attend(): pl.pallas_call(functools.partial(attend_kernel, sub, chunk), out_shape=(j...  25 us
    ppermute x14, waiting for transfers between devices, across(): return lax.ppermute(values, 'dp', [(i, i ^ bit) for i in range(devices)])  21.6 us
    ppermute x14, starting transfers between devices, across(): return lax.ppermute(values, 'dp', [(i, i ^ bit) for i in range(devices)])  15 us
    pallas_call x1, Pallas kernels, middle(): pl.pallas_call(functools.partial(middle_kernel, sub), grid=(tokens // blo...  13.6 us
    ppermute x5, waiting for transfers between devices, swapped(): return lax.ppermute(values, 'tensor', [(0, 1), (1, 0)])  7.2 us
    ppermute x5, starting transfers between devices, swapped(): return lax.ppermute(values, 'tensor', [(0, 1), (1, 0)])  7.01 us
    pallas_call x1, Pallas kernels, project(): pl.pallas_call(project_kernel, grid=(tokens // block,), out_shape=(jax.Sh...  6.43 us
  transfers between devices with their start and end apart: 20, of which 10 were waited for; matrix products, arithmetic and copies ran while one was open for 10% of the time, Pallas kernels for 49%

profile of v3, /device:TPU:0, one launch (start us, length us, event | category | flops | bytes accessed | tf_op | source)
XLA Modules:
  0.0 181.7 jit_solution(7100729852075855024)
XLA Ops:
  0.7 1.0 constant_dynamic-slice_fusion.2
  1.7 0.7 fusion.6
  2.4 3.0 %collective-permute-start = (bf16[400,256]{1,0:T(8,128)(2,1)S(1)}, bf16[400,256]{1,0:T(8,128)(2,1)S(1)}, u32[]{:S(2)}, u32[]{:S(2)}) collective-permute-start(bf16[400,256]{1,0:T(8,128)(2,1)S(1)} %fusion.6), channel_id=1, source_target_pairs={{0,1},{1,0},{2,3},{3,2},{4,5},{5,4},{6,7},{7,6},{8,9},{9,8},{10,11... | collective-permute-start | bytes 614408 | tf_op jit(solution)/shard_map/ppermute | solution.py:716
  5.5 0.7 compare_bitcast_fusion
  6.1 0.8 reduce-window.4
  7.0 0.7 fusion.25
  7.7 0.7 or_not_fusion
  9.5 1.8 %collective-permute-done = bf16[400,256]{1,0:T(8,128)(2,1)S(1)} collective-permute-done((bf16[400,256]{1,0:T(8,128)(2,1)S(1)}, bf16[400,256]{1,0:T(8,128)(2,1)S(1)}, u32[]{:S(2)}, u32[]{:S(2)}) %collective-permute-start) | collective-permute-done | bytes 204832 | tf_op jit(solution)/shard_map/ppermute | solution.py:716
  11.3 2.1 %collective-permute-start.1 = (bf16[384,256]{1,0:T(8,128)(2,1)S(1)}, bf16[384,256]{1,0:T(8,128)(2,1)S(1)}, u32[]{:S(2)}, u32[]{:S(2)}) collective-permute-start(bf16[384,256]{1,0:T(8,128)(2,1)S(1)} %slice.197), channel_id=1, source_target_pairs={{0,4},{2,6},{4,0},{6,2},{8,12},{10,14},{12,8},{14,10},{16,20},{18,... | collective-permute-start | bytes 589832 | tf_op jit(solution)/shard_map/ppermute | solution.py:719
  13.4 3.6 %collective-permute-done.1 = bf16[384,256]{1,0:T(8,128)(2,1)S(1)} collective-permute-done((bf16[384,256]{1,0:T(8,128)(2,1)S(1)}, bf16[384,256]{1,0:T(8,128)(2,1)S(1)}, u32[]{:S(2)}, u32[]{:S(2)}) %collective-permute-start.1) | collective-permute-done | bytes 196640 | tf_op jit(solution)/shard_map/ppermute | solution.py:719
  17.2 0.7 fusion.9.extra_q_ref
  18.0 0.6 stack.32.vec_ref
  18.6 0.8 constant_dynamic-slice_fusion
  19.5 0.7 maximum_convert_fusion.4.bias_ref
  20.4 0.9 pad_maximum_fusion
  21.3 6.4 %project.1 = (bf16[8,1024,128]{2,1,0:T(8,128)(2,1)}, bf16[8,1024,128]{2,1,0:T(8,128)(2,1)}, bf16[8,128,1024]{2,1,0:T(8,128)(2,1)}, bf16[1024,512]{1,0:T(8,128)(2,1)}) custom-call(bf16[1024,512]{1,0:T(8,128)(2,1)} %refs_9_.1, bf16[3,512,256]{2,1,0:T(8,128)(2,1)} %bitcast.65, bf16[3,512,256]{2,1,0:T(8,128)(2,1)} %bitcast.55, ...), custom_call_target="tpu_custom_call" | custom-call | flops 1610612736 | bytes 6291456 | tf_op jit(solution)/shard_map/project/pallas_call | solution.py:81
  27.7 5.4 %collective-permute-done.3.x_ref.refs_6_ = bf16[1024,512]{1,0:T(8,128)(2,1)} collective-permute-done((bf16[1024,512]{1,0:T(8,128)(2,1)}, bf16[1024,512]{1,0:T(8,128)(2,1)}, u32[]{:S(2)}, u32[]{:S(2)}) %collective-permute-start.3) | collective-permute-done | bytes 1048608 | tf_op jit(solution)/shard_map/ppermute | solution.py:716
  33.1 1.7 collective-permute-start.4
  34.8 25.0 %attend.1 = (bf16[8,2048,1024]{2,1,0:T(8,128)(2,1)}, f32[8,64,1024]{2,1,0:T(8,128)}, f32[8,1,1024]{2,1,0:T(1,128)}, bf16[8,1024,128]{2,1,0:T(8,128)(2,1)}, bf16[8,1024,128]{2,1,0:T(8,128)(2,1)}) custom-call(bf16[8,128,1024]{2,1,0:T(8,128)(2,1)} %get-tuple-element.50.qt_hbm, bf16[8,1024,128]{2,1,0:T(8,128)(2,1)} %get-tuple-element.52.k_hbm.refs_7_, ...), custom_call_target="tpu_custom_call" | custom-call | flops 17179869184 | bytes 33554432 | tf_op jit(solution)/shard_map/attend/pallas_call | solution.py:215
  59.9 0.9 copy-done.14
  60.8 13.6 %middle.1 = (bf16[1024,512]{1,0:T(8,128)(2,1)}, f32[1024,512]{1,0:T(8,128)}, bf16[8,128,1024]{2,1,0:T(8,128)(2,1)}, bf16[1024,512]{1,0:T(8,128)(2,1)}, f32[768,5...) custom-call(bf16[1024,512]{1,0:T(8,128)(2,1)} %refs_9_.1, bf16[1024,512]{1,0:T(8,128)(2,1)} %cot_ref.1, ...), custom_call_target="tpu_custom_call" | custom-call | flops 4831838208 | bytes 10485760 | tf_op jit(solution)/shard_map/middle/pallas_call | solution.py:366
  74.8 25.2 %attend_back_other.1 = (f32[512,1024]{1,0:T(8,128)}, bf16[1024,512]{1,0:T(8,128)(2,1)}, f32[2,512,512]{2,1,0:T(8,128)}, f32[2,512]{1,0:T(2,128)}) custom-call(bf16[8,2048,1024]{2,1,0:T(8,128)(2,1)} %get-tuple-element.62.refs_0_.refs_3_, bf16[8,128,1024]{2,1,0:T(8,128)(2,1)} %get-tuple-element.63.refs_1_.refs_4_, ...), custom_call_target="tpu_custom_call" | custom-call | flops 17179869184 | bytes 16777216 | tf_op jit(solution)/shard_map/attend_back_other/pallas_call | solution.py:577
  100.0 1.8 collective-permute-start.7
  102.1 1.6 collective-permute-start.6
  103.6 25.5 %attend_back_own.1 = (bf16[1600,256]{1,0:T(8,128)(2,1)}, bf16[1600,256]{1,0:T(8,128)(2,1)}, bf16[1024,512]{1,0:T(8,128)(2,1)}, bf16[1024,512]{1,0:T(8,128)(2,1)}, bf16[1024,512]{1,0:T(8,128)(2,1)}) custom-call(s32[1]{0:T(128)} %bitcast.17.refs_0_, f32[8,512]{1,0:T(8,128)} %get-tuple-element.71.refs_1_, f32[2,512]{1,0:T(2,128)} %get-tuple-element.72.refs_2_, ...), custom_call_target="tpu_custom_call" | custom-call | flops 17179869184 | bytes 16777216 | tf_op jit(solution)/shard_map/attend_back_own/pallas_call | solution.py:577
  129.2 1.4 bitcast_add_fusion
  130.9 1.2 collective-permute-done.15
  132.2 1.6 collective-permute-start.16
  133.9 1.3 convert_add_fusion
  135.2 0.7 subtract_convert_fusion
  136.5 2.7 %collective-permute-done.16 = bf16[192,512]{1,0:T(8,128)(2,1)S(1)} collective-permute-done((bf16[192,512]{1,0:T(8,128)(2,1)S(1)}, bf16[192,512]{1,0:T(8,128)(2,1)S(1)}, u32[]{:S(2)}, u32[]{:S(2)}) %collective-permute-start.16) | collective-permute-done | bytes 196640 | tf_op jit(solution)/shard_map/ppermute | solution.py:648
  139.4 2.7 %collective-permute-start.17 = (bf16[192,512]{1,0:T(8,128)(2,1)S(1)}, bf16[192,512]{1,0:T(8,128)(2,1)S(1)}, u32[]{:S(2)}, u32[]{:S(2)}) collective-permute-start(bf16[192,512]{1,0:T(8,128)(2,1)S(1)} %add_convert_fusion.1), channel_id=1, source_target_pairs={{0,16},{2,18},{4,20},{6,22},{8,24},{10,26},{12,28},{14,30},{16,0},... | collective-permute-start | bytes 589832 | tf_op jit(solution)/shard_map/ppermute | solution.py:648
  142.0 5.3 %collective-permute-done.9 = bf16[800,256]{1,0:T(8,128)(2,1)S(1)} collective-permute-done((bf16[800,256]{1,0:T(8,128)(2,1)S(1)}, bf16[800,256]{1,0:T(8,128)(2,1)S(1)}, u32[]{:S(2)}, u32[]{:S(2)}) %collective-permute-start.9) | collective-permute-done | bytes 409632 | tf_op jit(solution)/shard_map/ppermute | solution.py:662
  147.4 0.7 fusion.16
  148.2 0.6 collective-permute-start.10
  148.8 1.9 %collective-permute-done.17 = bf16[192,512]{1,0:T(8,128)(2,1)S(1)} collective-permute-done((bf16[192,512]{1,0:T(8,128)(2,1)S(1)}, bf16[192,512]{1,0:T(8,128)(2,1)S(1)}, u32[]{:S(2)}, u32[]{:S(2)}) %collective-permute-start.17) | collective-permute-done | bytes 196640 | tf_op jit(solution)/shard_map/ppermute | solution.py:648
  150.8 3.6 %collective-permute-done.10 = bf16[416,256]{1,0:T(8,128)(2,1)S(1)} collective-permute-done((bf16[416,256]{1,0:T(8,128)(2,1)S(1)}, bf16[416,256]{1,0:T(8,128)(2,1)S(1)}, u32[]{:S(2)}, u32[]{:S(2)}) %collective-permute-start.10) | collective-permute-done | bytes 213024 | tf_op jit(solution)/shard_map/ppermute | solution.py:648
  155.2 0.6 collective-permute-start.19
  155.8 4.7 %collective-permute-done.11 = bf16[416,256]{1,0:T(8,128)(2,1)S(1)} collective-permute-done((bf16[416,256]{1,0:T(8,128)(2,1)S(1)}, bf16[416,256]{1,0:T(8,128)(2,1)S(1)}, u32[]{:S(2)}, u32[]{:S(2)}) %collective-permute-start.11) | collective-permute-done | bytes 213024 | tf_op jit(solution)/shard_map/ppermute | solution.py:648
  160.6 4.2 %collective-permute-start.12 = (bf16[416,256]{1,0:T(8,128)(2,1)S(1)}, bf16[416,256]{1,0:T(8,128)(2,1)S(1)}, u32[]{:S(2)}, u32[]{:S(2)}) collective-permute-start(bf16[416,256]{1,0:T(8,128)(2,1)S(1)} %pad_maximum_fusion.9), channel_id=1, source_target_pairs={{0,16},{2,18},{4,20},{6,22},{8,24},{10,26},{12,28},{14,30},{16,0},... | collective-permute-start | bytes 638984 | tf_op jit(solution)/shard_map/ppermute | solution.py:648
  164.8 6.3 %input_gradient.1 = f32[1024,512]{1,0:T(8,128)} custom-call(f32[1024,512]{1,0:T(8,128)} %get-tuple-element.59.res_ref, bf16[1024,512]{1,0:T(8,128)(2,1)} %copy-done.1, bf16[1024,512]{1,0:T(8,128)(2,1)} %get-tuple-element.79.dq_ref, bf16[1024,512]{1,0:T(8,128)(2,1)} %get-tuple-element.80.dk_ref, bf16[1024,512]{1,0:T(8,128)(2,1)} %get-tuple-element.81.dv_ref, ...), custom_call_target="tpu_custom_call" | custom-call | flops 1610612736 | bytes 8388608 | tf_op jit(solution)/shard_map/input_gradient/pallas_call | solution.py:608
  171.2 0.6 collective-permute-start.13
  171.9 0.6 pad_maximum_fusion.10
  173.3 3.7 %collective-permute-done.13 = bf16[384,256]{1,0:T(8,128)(2,1)S(1)} collective-permute-done((bf16[384,256]{1,0:T(8,128)(2,1)S(1)}, bf16[384,256]{1,0:T(8,128)(2,1)S(1)}, u32[]{:S(2)}, u32[]{:S(2)}) %collective-permute-start.13) | collective-permute-done | bytes 196640 | tf_op jit(solution)/shard_map/ppermute | solution.py:648
  177.7 0.8 slice.220
  178.5 0.9 maximum_convert_fusion.1
  179.4 0.8 pad_maximum_fusion.2
  180.5 1.3 convert_bitcast_fusion
  (95 shorter events, 6.2 us)
Async XLA Ops:
  0.6 8.8 %copy-start.4 = (bf16[512,256]{1,0:T(8,128)(2,1)S(1)}, bf16[512,256]{1,0:T(8,128)(2,1)}, u32[]{:S(2)}) copy-start(bf16[512,256]{1,0:T(8,128)(2,1)} %param.25) | copy-start | bytes 786436
  2.4 8.9 %collective-permute-start = (bf16[400,256]{1,0:T(8,128)(2,1)S(1)}, bf16[400,256]{1,0:T(8,128)(2,1)S(1)}, u32[]{:S(2)}, u32[]{:S(2)}) collective-permute-start(bf16[400,256]{1,0:T(8,128)(2,1)S(1)} %fusion.6), channel_id=1, source_target_pairs={{0,1},{1,0},{2,3},{3,2},{4,5},{5,4},{6,7},{7,6},{8,9},{9,8},{10,11... | collective-permute-start | bytes 614408 | tf_op jit(solution)/shard_map/ppermute | solution.py:716
  5.4 27.7 %collective-permute-start.3 = (bf16[1024,512]{1,0:T(8,128)(2,1)}, bf16[1024,512]{1,0:T(8,128)(2,1)}, u32[]{:S(2)}, u32[]{:S(2)}) collective-permute-start(bf16[1024,512]{1,0:T(8,128)(2,1)} %refs_9_.1), channel_id=1, source_target_pairs={{0,1},{1,0},{2,3},{3,2},{4,5},{5,4},{6,7},{7,6},{8,9},{9,8},{10,11... | collective-permute-start | bytes 3145736 | tf_op jit(solution)/shard_map/ppermute | solution.py:716
  9.0 8.9 %copy-start.15 = (bf16[256]{0:T(256)(128)(2,1)S(1)}, bf16[256]{0:T(256)(128)(2,1)}, u32[]{:S(2)}) copy-start(bf16[256]{0:T(256)(128)(2,1)} %param.26) | copy-start | bytes 1540
  9.0 8.9 %copy-start.7 = (f32[512]{0:T(512)S(1)}, f32[512]{0:T(512)}, u32[]{:S(2)}) copy-start(f32[512]{0:T(512)} %param.22) | copy-start | bytes 6148
  9.0 8.9 %copy-start.9 = (f32[512]{0:T(512)S(1)}, f32[512]{0:T(512)}, u32[]{:S(2)}) copy-start(f32[512]{0:T(512)} %param.23) | copy-start | bytes 6148
  9.0 8.9 %copy-start.10 = (f32[512]{0:T(512)S(1)}, f32[512]{0:T(512)}, u32[]{:S(2)}) copy-start(f32[512]{0:T(512)} %param.24) | copy-start | bytes 6148
  9.0 8.9 %copy-start.11 = (f32[512]{0:T(512)S(1)}, f32[512]{0:T(512)}, u32[]{:S(2)}) copy-start(f32[512]{0:T(512)} %param.28) | copy-start | bytes 6148
  9.0 8.9 %copy-start.12 = (f32[512]{0:T(512)S(1)}, f32[512]{0:T(512)}, u32[]{:S(2)}) copy-start(f32[512]{0:T(512)} %param.29) | copy-start | bytes 6148
  9.0 8.9 %copy-start.13 = (f32[512]{0:T(512)S(1)}, f32[512]{0:T(512)}, u32[]{:S(2)}) copy-start(f32[512]{0:T(512)} %param.30) | copy-start | bytes 6148
  9.4 10.0 %copy-start.5 = (bf16[256,512]{1,0:T(8,128)(2,1)S(1)}, bf16[256,512]{1,0:T(8,128)(2,1)}, u32[]{:S(2)}) copy-start(bf16[256,512]{1,0:T(8,128)(2,1)} %param.27) | copy-start | bytes 786436
  9.5 10.0 %copy-start.6 = (bf16[256,512]{1,0:T(8,128)(2,1)S(1)}, bf16[256,512]{1,0:T(8,128)(2,1)}, u32[]{:S(2)}) copy-start(bf16[256,512]{1,0:T(8,128)(2,1)} %param.21) | copy-start | bytes 786436
  11.3 5.7 %collective-permute-start.1 = (bf16[384,256]{1,0:T(8,128)(2,1)S(1)}, bf16[384,256]{1,0:T(8,128)(2,1)S(1)}, u32[]{:S(2)}, u32[]{:S(2)}) collective-permute-start(bf16[384,256]{1,0:T(8,128)(2,1)S(1)} %slice.197), channel_id=1, source_target_pairs={{0,4},{2,6},{4,0},{6,2},{8,12},{10,14},{12,8},{14,10},{16,20},{18,... | collective-permute-start | bytes 589832 | tf_op jit(solution)/shard_map/ppermute | solution.py:719
  17.1 2.4 %copy-start.8 = (bf16[2,256]{1,0:T(2,128)(2,1)S(1)}, bf16[2,256]{1,0:T(2,128)(2,1)}, u32[]{:S(2)}) copy-start(bf16[2,256]{1,0:T(2,128)(2,1)} %param.20) | copy-start | bytes 3076
  17.2 3.0 %collective-permute-start.2 = (bf16[768,256]{1,0:T(8,128)(2,1)S(1)}, bf16[768,256]{1,0:T(8,128)(2,1)S(1)}, u32[]{:S(2)}, u32[]{:S(2)}) collective-permute-start(bf16[768,256]{1,0:T(8,128)(2,1)S(1)} %pad_maximum_fusion.4), channel_id=1, source_target_pairs={{0,2},{2,0},{4,6},{6,4},{8,10},{10,8},{12,14},{14,12},{16,18},{18,... | collective-permute-start | bytes 1179656 | tf_op jit(solution)/shard_map/ppermute | solution.py:719
  19.5 13.6 %copy-start.3 = (bf16[784,512]{1,0:T(8,128)(2,1)}, bf16[784,512]{1,0:T(8,128)(2,1)S(1)}, u32[]{:S(2)}) copy-start(bf16[784,512]{1,0:T(8,128)(2,1)S(1)} %fusion.1.w_own_ref) | copy-start | bytes 2408452
  33.1 26.8 %collective-permute-start.4 = (bf16[784,512]{1,0:T(8,128)(2,1)S(1)}, bf16[784,512]{1,0:T(8,128)(2,1)S(1)}, u32[]{:S(2)}, u32[]{:S(2)}) collective-permute-start(bf16[784,512]{1,0:T(8,128)(2,1)S(1)} %fusion.1.w_own_ref), channel_id=1, source_target_pairs={{0,1},{1,0},{2,3},{3,2},{4,5},{5,4},{6,7},{7,6},{8,9},{9,8},{10,11... | collective-permute-start | bytes 2408456 | tf_op jit(solution)/shard_map/ppermute | solution.py:716
  59.9 0.9 copy-start.14
  74.4 27.3 %collective-permute-start.5 = (bf16[768,512]{1,0:T(8,128)(2,1)}, bf16[768,512]{1,0:T(8,128)(2,1)S(1)}, u32[]{:S(2)}, u32[]{:S(2)}) collective-permute-start(bf16[768,512]{1,0:T(8,128)(2,1)} %get-tuple-element.61), channel_id=1, source_target_pairs={{0,1},{1,0},{2,3},{3,2},{4,5},{5,4},{6,7},{7,6},{8,9},{9,8},{10,11... | collective-permute-start | bytes 2359304 | tf_op jit(solution)/shard_map/ppermute | solution.py:716
  74.8 27.0 %copy-start = (f32[768,512]{1,0:T(8,128)S(1)}, f32[768,512]{1,0:T(8,128)}, u32[]{:S(2)}) copy-start(f32[768,512]{1,0:T(8,128)} %get-tuple-element.60) | copy-start | bytes 4718596
  100.0 29.1 %collective-permute-start.7 = (bf16[1024,512]{1,0:T(8,128)(2,1)}, bf16[1024,512]{1,0:T(8,128)(2,1)S(1)}, u32[]{:S(2)}, u32[]{:S(2)}) collective-permute-start(bf16[1024,512]{1,0:T(8,128)(2,1)} %get-tuple-element.70), channel_id=1, source_target_pairs={{0,1},{1,0},{2,3},{3,2},{4,5},{5,4},{6,7},{7,6},{8,9},{9,8},{10,11... | collective-permute-start | bytes 3145736 | tf_op jit(solution)/shard_map/ppermute | solution.py:716
  102.1 27.0 %collective-permute-start.6 = (bf16[384,512]{1,0:T(8,128)(2,1)S(1)}, bf16[384,512]{1,0:T(8,128)(2,1)}, u32[]{:S(2)}, u32[]{:S(2)}) collective-permute-start(bf16[384,512]{1,0:T(8,128)(2,1)S(1)} %fusion.3), channel_id=1, source_target_pairs={{0,4},{2,6},{4,0},{6,2},{8,12},{10,14},{12,8},{14,10},{16,20},{18,... | collective-permute-start | bytes 1179656 | tf_op jit(solution)/shard_map/ppermute | solution.py:719
  129.1 3.1 %copy-start.1 = (bf16[1024,512]{1,0:T(8,128)(2,1)}, bf16[1024,512]{1,0:T(8,128)(2,1)S(1)}, u32[]{:S(2)}) copy-start(bf16[1024,512]{1,0:T(8,128)(2,1)S(1)} %collective-permute-done.7.got_ref) | copy-start | bytes 3145732
  129.1 4.7 %collective-permute-start.8 = (bf16[1600,256]{1,0:T(8,128)(2,1)}, bf16[1600,256]{1,0:T(8,128)(2,1)}, u32[]{:S(2)}, u32[]{:S(2)}) collective-permute-start(bf16[1600,256]{1,0:T(8,128)(2,1)} %get-tuple-element.78), channel_id=1, source_target_pairs={{0,2},{2,0},{4,6},{6,4},{8,10},{10,8},{12,14},{14,12},{16,18},{18,... | collective-permute-start | bytes 2457608 | tf_op jit(solution)/shard_map/ppermute | solution.py:648
  130.6 3.3 %copy-start.2 = (bf16[1600,256]{1,0:T(8,128)(2,1)S(1)}, bf16[1600,256]{1,0:T(8,128)(2,1)}, u32[]{:S(2)}) copy-start(bf16[1600,256]{1,0:T(8,128)(2,1)} %get-tuple-element.82) | copy-start | bytes 2457604
  130.7 1.5 collective-permute-start.15
  132.2 7.1 %collective-permute-start.16 = (bf16[192,512]{1,0:T(8,128)(2,1)S(1)}, bf16[192,512]{1,0:T(8,128)(2,1)S(1)}, u32[]{:S(2)}, u32[]{:S(2)}) collective-permute-start(bf16[192,512]{1,0:T(8,128)(2,1)S(1)} %fusion.4), channel_id=1, source_target_pairs={{0,8},{2,10},{4,12},{6,14},{8,0},{10,2},{12,4},{14,6},{16,24},{18,... | collective-permute-start | bytes 589832 | tf_op jit(solution)/shard_map/ppermute | solution.py:648
  136.0 11.4 %collective-permute-start.9 = (bf16[800,256]{1,0:T(8,128)(2,1)S(1)}, bf16[800,256]{1,0:T(8,128)(2,1)S(1)}, u32[]{:S(2)}, u32[]{:S(2)}) collective-permute-start(bf16[800,256]{1,0:T(8,128)(2,1)S(1)} %pad_maximum_fusion.3), channel_id=1, source_target_pairs={{0,1},{1,0},{2,3},{3,2},{4,5},{5,4},{6,7},{7,6},{8,9},{9,8},{10,11... | collective-permute-start | bytes 1228808 | tf_op jit(solution)/shard_map/ppermute | solution.py:662
  139.4 11.4 %collective-permute-start.17 = (bf16[192,512]{1,0:T(8,128)(2,1)S(1)}, bf16[192,512]{1,0:T(8,128)(2,1)S(1)}, u32[]{:S(2)}, u32[]{:S(2)}) collective-permute-start(bf16[192,512]{1,0:T(8,128)(2,1)S(1)} %add_convert_fusion.1), channel_id=1, source_target_pairs={{0,16},{2,18},{4,20},{6,22},{8,24},{10,26},{12,28},{14,30},{16,0},... | collective-permute-start | bytes 589832 | tf_op jit(solution)/shard_map/ppermute | solution.py:648
  148.2 6.3 %collective-permute-start.10 = (bf16[416,256]{1,0:T(8,128)(2,1)S(1)}, bf16[416,256]{1,0:T(8,128)(2,1)S(1)}, u32[]{:S(2)}, u32[]{:S(2)}) collective-permute-start(bf16[416,256]{1,0:T(8,128)(2,1)S(1)} %pad_maximum_fusion.7), channel_id=1, source_target_pairs={{0,4},{2,6},{4,0},{6,2},{8,12},{10,14},{12,8},{14,10},{16,20},{18,... | collective-permute-start | bytes 638984 | tf_op jit(solution)/shard_map/ppermute | solution.py:648
  150.8 4.3 %collective-permute-start.18 = (bf16[192,512]{1,0:T(8,128)(2,1)S(1)}, bf16[192,512]{1,0:T(8,128)(2,1)S(1)}, u32[]{:S(2)}, u32[]{:S(2)}) collective-permute-start(bf16[192,512]{1,0:T(8,128)(2,1)S(1)} %add_convert_fusion), channel_id=1, source_target_pairs={{0,2},{2,0},{4,6},{6,4},{8,10},{10,8},{12,14},{14,12},{16,18},{18,... | collective-permute-start | bytes 589832 | tf_op jit(solution)/shard_map/ppermute | solution.py:648
  154.6 5.9 %collective-permute-start.11 = (bf16[416,256]{1,0:T(8,128)(2,1)S(1)}, bf16[416,256]{1,0:T(8,128)(2,1)S(1)}, u32[]{:S(2)}, u32[]{:S(2)}) collective-permute-start(bf16[416,256]{1,0:T(8,128)(2,1)S(1)} %pad_maximum_fusion.8), channel_id=1, source_target_pairs={{0,8},{2,10},{4,12},{6,14},{8,0},{10,2},{12,4},{14,6},{16,24},{18,... | collective-permute-start | bytes 638984 | tf_op jit(solution)/shard_map/ppermute | solution.py:648
  155.2 15.9 %collective-permute-start.19 = (bf16[384,512]{1,0:T(8,128)(2,1)S(1)}, bf16[384,512]{1,0:T(8,128)(2,1)S(1)}, u32[]{:S(2)}, u32[]{:S(2)}) collective-permute-start(bf16[384,512]{1,0:T(8,128)(2,1)S(1)} %pad_maximum_fusion.6), channel_id=1, source_target_pairs={{0,4},{2,6},{4,0},{6,2},{8,12},{10,14},{12,8},{14,10},{16,20},{18,... | collective-permute-start | bytes 1179656 | tf_op jit(solution)/shard_map/ppermute | solution.py:648
  160.6 10.5 %collective-permute-start.12 = (bf16[416,256]{1,0:T(8,128)(2,1)S(1)}, bf16[416,256]{1,0:T(8,128)(2,1)S(1)}, u32[]{:S(2)}, u32[]{:S(2)}) collective-permute-start(bf16[416,256]{1,0:T(8,128)(2,1)S(1)} %pad_maximum_fusion.9), channel_id=1, source_target_pairs={{0,16},{2,18},{4,20},{6,22},{8,24},{10,26},{12,28},{14,30},{16,0},... | collective-permute-start | bytes 638984 | tf_op jit(solution)/shard_map/ppermute | solution.py:648
  171.2 5.7 %collective-permute-start.13 = (bf16[384,256]{1,0:T(8,128)(2,1)S(1)}, bf16[384,256]{1,0:T(8,128)(2,1)S(1)}, u32[]{:S(2)}, u32[]{:S(2)}) collective-permute-start(bf16[384,256]{1,0:T(8,128)(2,1)S(1)} %add_convert_fusion.2), channel_id=1, source_target_pairs={{0,4},{2,6},{4,0},{6,2},{8,12},{10,14},{12,8},{14,10},{16,20},{18,... | collective-permute-start | bytes 589832 | tf_op jit(solution)/shard_map/ppermute | solution.py:648
  177.0 3.2 %collective-permute-start.14 = (bf16[768,256]{1,0:T(8,128)(2,1)S(1)}, bf16[768,256]{1,0:T(8,128)(2,1)S(1)}, u32[]{:S(2)}, u32[]{:S(2)}) collective-permute-start(bf16[768,256]{1,0:T(8,128)(2,1)S(1)} %pad_maximum_fusion.5), channel_id=1, source_target_pairs={{0,2},{2,0},{4,6},{6,4},{8,10},{10,8},{12,14},{14,12},{16,18},{18,... | collective-permute-start | bytes 1179656 | tf_op jit(solution)/shard_map/ppermute | solution.py:648
